TPU v7x, 32 devices: a whole 2x2x4 slice. The times are simulated.
32 devices in a mesh: seq: 16 (over z, x, core), fsdp: 2 (over y).
Axes of the slice: x: 2, y: 2, z: 4, core: 2. Of those that a mesh axis runs over, the one named last changes fastest.
Arguments:
- tokens: bfloat16 [16, 2048, 768], P('fsdp', 'seq'), may hold values from -6 to 6
- positions: int32 [16, 2048], P('fsdp'), may hold values from 0 to 2047, as said below
- qkv_weight: bfloat16 [768, 2304], P('fsdp'), may hold values from -0.3125 to 0.3125
- out_weight: bfloat16 [768, 768], P('fsdp'), may hold values from -1.75 to 1.75
- in_weight: bfloat16 [768, 2304], P('fsdp'), may hold values from -0.21875 to 0.21875
- down_weight: bfloat16 [1152, 768], P('fsdp'), may hold values from -0.3125 to 0.3125
- norm_gains: bfloat16 [2, 768], P(None, 'fsdp'), may hold values from 0.5 to 1.5
- cotangent: bfloat16 [16, 2048, 768], P('fsdp', 'seq'), may hold values from -6 to 6
Outputs:
- layer_out: bfloat16 [16, 2048, 768], P('fsdp', 'seq')
- grad_tokens: bfloat16 [16, 2048, 768], P('fsdp', 'seq')
- grad_qkv: float32 [768, 2304], P('fsdp')
- grad_out: float32 [768, 768], P('fsdp')
- grad_in: float32 [768, 2304], P('fsdp')
- grad_down: float32 [1152, 768], P('fsdp')
- grad_gains: float32 [2, 768], P(None, 'fsdp')
Inputs may be any that keep to these rules, and one draw needn't show every extreme that they name: In each row, positions count up by one from token to token and fall back to 0 where a document begins; every row starts at 0. Of each aligned block of 8 rows, one row is a single document.
All inputs are finite; a program needn't handle non-finite values.
Results may differ from a plain program's by a relative error of at most 0.015.
The roundings to bfloat16 on the way count: a program that leaves them out, or rounds other values in their place, can miss the bound.
Values may be sent and summed in bfloat16 or wider, within the bound.
No kernel may reach another device: no remote copies, remote signals or barrier semaphores. Data moves between devices by JAX's collectives and lax.ppermute only.
A program may use at most 192 MiB of HBM per device.

v0:
```python
import jax
import jax.numpy as jnp
from jax import lax
from jax.sharding import PartitionSpec as P

HEAD_DIM = 64
HALF_WINDOW = 64


masked_score = -1000000000.0
norm_epsilon = 1e-05


def with_halo(value, sides, width):
    for axis, dim in sides:
        size, length = (lax.axis_size(axis), value.shape[dim])
        up = [(i, (i + 1) % size) for i in range(size - 1)]
        down = [(j, i) for i, j in up]
        last = lax.slice_in_dim(value, length - width, length, axis=dim)
        leading = lax.slice_in_dim(value, 0, width, axis=dim)
        before = lax.ppermute(last, axis, up)
        after = lax.ppermute(leading, axis, down)
        value = jnp.concatenate([before, value, after], axis=dim)
    return value


def passed_along(block, axis, distance):
    devices = range(lax.axis_size(axis))
    route = [(i - distance, i) for i in devices if i - distance in devices]
    return lax.ppermute(block, axis, route)


def norm_parts(values):
    center = values - jnp.mean(values, -1, keepdims=True)
    factor = lax.rsqrt(jnp.mean(center * center, -1, keepdims=True) + norm_epsilon)
    return (center * factor, factor)


def norm_back(grad_normed, normed, factor):
    first = jnp.mean(grad_normed, -1, keepdims=True)
    second = jnp.mean(grad_normed * normed, -1, keepdims=True)
    return factor * (grad_normed - first - normed * second)


def rotary_tables(pos, head_width):
    half = head_width // 2
    freqs = 10000.0 ** (-(jnp.arange(half, dtype=jnp.float32) * 2.0 / head_width))
    angle = pos.astype(jnp.float32)[..., None] * freqs
    return (jnp.cos(angle)[..., None, :], jnp.sin(angle)[..., None, :])


def rotate_heads(values, cosine, sine):
    half = values.shape[-1] // 2
    first = values[..., :half]
    second = values[..., half:]
    return jnp.concatenate([first * cosine - second * sine, second * cosine + first * sine], -1)


def rotate_back(grads, cosine, sine):
    half = grads.shape[-1] // 2
    first = grads[..., :half]
    second = grads[..., half:]
    return jnp.concatenate([first * cosine + second * sine, second * cosine - first * sine], -1)


def window_mask(query_pos, key_pos, rows, half_span):
    offsets = (
        jnp.arange(rows + 2 * half_span, dtype=jnp.int32)[None, :]
        - half_span
        - jnp.arange(rows, dtype=jnp.int32)[:, None]
    )
    query_col = query_pos[..., :, None]
    key_row = key_pos[..., None, :]
    return (
        (jnp.abs(offsets) <= half_span)
        & (key_row >= 0)
        & ((offsets > 0) | (query_col >= -offsets))
        & ((offsets <= 0) | (key_row >= offsets))
    )


def weight_grad(left, right):
    left_rows = left.reshape(-1, left.shape[-1])
    right_rows = right.reshape(-1, right.shape[-1])
    return lax.dot_general(
        left_rows, right_rows, (((0,), (0,)), ((), ())), preferred_element_type=jnp.float32
    )


def through_weight(grads, weight):
    return lax.dot_general(
        grads, weight, (((grads.ndim - 1,), (1,)), ((), ())), preferred_element_type=jnp.float32
    )


def local(tokens, positions, qkv_weight, out_weight, in_weight, down_weight, norm_gains, cotangent):
    num_seqs, tok_block, model_width = tokens.shape
    head_width = HEAD_DIM
    head_count = model_width // head_width
    half_span = HALF_WINDOW
    span = tok_block + 2 * half_span
    scale = head_width ** (-0.5)
    w_qkv, w_out, w_in, w_down, gains = (
        lax.all_gather(qkv_weight, "fsdp", axis=0, tiled=True),
        lax.all_gather(out_weight, "fsdp", axis=0, tiled=True),
        lax.all_gather(in_weight, "fsdp", axis=0, tiled=True),
        lax.all_gather(down_weight, "fsdp", axis=0, tiled=True),
        lax.all_gather(norm_gains, "fsdp", axis=1, tiled=True),
    )
    ffn_width = w_in.shape[1] // 2
    gain_one = gains[0].astype(jnp.float32)
    gain_two = gains[1].astype(jnp.float32)
    stream = tokens.astype(jnp.float32)
    normed_one, factor_one = norm_parts(stream)
    hidden_one = (normed_one * gain_one).astype(jnp.bfloat16)
    qkv = jnp.dot(hidden_one, w_qkv, preferred_element_type=jnp.float32)
    block_index = lax.axis_index("seq")
    padded_pos = jnp.pad(positions, ((0, 0), (half_span, half_span)), constant_values=-1)
    key_pos = lax.dynamic_slice_in_dim(padded_pos, block_index * tok_block, span, 1)
    own_pos = key_pos[:, half_span : half_span + tok_block]
    cosine, sine = rotary_tables(own_pos, head_width)
    head_shape = (num_seqs, tok_block, head_count, head_width)
    query = rotate_heads(qkv[..., :model_width].reshape(head_shape), cosine, sine).astype(
        jnp.bfloat16
    )
    keys = rotate_heads(qkv[..., model_width : 2 * model_width].reshape(head_shape), cosine, sine)
    keys = keys.astype(jnp.bfloat16).reshape(num_seqs, tok_block, model_width)
    values = qkv[..., 2 * model_width :].astype(jnp.bfloat16)
    edges = with_halo(jnp.concatenate([keys, values], -1), (("seq", 1),), half_span)
    ext_shape = (num_seqs, span, head_count, head_width)
    key_ext = edges[..., :model_width].reshape(ext_shape)
    value_ext = edges[..., model_width:].reshape(ext_shape)
    allowed = window_mask(own_pos, key_pos, tok_block, half_span)

    def banded_scores(query_heads):
        raw = (
            jnp.einsum("gihd,gjhd->ghij", query_heads, key_ext, preferred_element_type=jnp.float32)
            * scale
        )
        return jnp.where(allowed[:, None], raw, masked_score)

    scores = banded_scores(query)
    row_top = jnp.max(scores, -1, keepdims=True)
    expo = jnp.exp(scores - row_top)
    row_total = jnp.sum(expo, -1, keepdims=True)
    log_total = row_top + jnp.log(row_total)
    probs = (expo / row_total).astype(jnp.bfloat16)
    mixed = jnp.einsum("ghij,gjhd->gihd", probs, value_ext, preferred_element_type=jnp.float32)
    mixed = mixed.reshape(num_seqs, tok_block, model_width).astype(jnp.bfloat16)
    after_attn = stream + jnp.dot(mixed, w_out, preferred_element_type=jnp.float32)
    normed_two, factor_two = norm_parts(after_attn)
    hidden_two = (normed_two * gain_two).astype(jnp.bfloat16)
    up_proj = jnp.dot(hidden_two, w_in, preferred_element_type=jnp.float32)
    act_input = up_proj[..., :ffn_width]
    gate_part = up_proj[..., ffn_width:]
    act_value, gelu_pull = jax.vjp(lambda value: jax.nn.gelu(value, approximate=False), act_input)
    middle = (act_value * gate_part).astype(jnp.bfloat16)
    layer_out = after_attn + jnp.dot(middle, w_down, preferred_element_type=jnp.float32)
    grad_down = weight_grad(middle, cotangent)
    grad_middle = through_weight(cotangent, w_down)
    grad_act = gelu_pull(grad_middle * gate_part)[0]
    grad_up = jnp.concatenate([grad_act, grad_middle * act_value], -1).astype(jnp.bfloat16)
    grad_in = weight_grad(hidden_two, grad_up)
    grad_hidden_two = through_weight(grad_up, w_in)
    gain_grad_two = jnp.sum((grad_hidden_two * normed_two).reshape(-1, model_width), 0)
    grad_stream = cotangent.astype(jnp.float32) + norm_back(
        grad_hidden_two * gain_two, normed_two, factor_two
    )
    grad_attn = grad_stream.astype(jnp.bfloat16)
    grad_out = weight_grad(mixed, grad_attn)
    grad_mixed = through_weight(grad_attn, w_out).astype(jnp.bfloat16).reshape(head_shape)
    again = jnp.exp(banded_scores(query) - log_total)
    grad_values = jnp.einsum(
        "ghij,gihd->gjhd",
        again.astype(jnp.bfloat16),
        grad_mixed,
        preferred_element_type=jnp.float32,
    )
    grad_probs = jnp.einsum(
        "gihd,gjhd->ghij", grad_mixed, value_ext, preferred_element_type=jnp.float32
    )
    inner_sum = jnp.sum(grad_probs * again, -1, keepdims=True)
    grad_scores = (again * (grad_probs - inner_sum)).astype(jnp.bfloat16)
    grad_query = (
        jnp.einsum("ghij,gjhd->gihd", grad_scores, key_ext, preferred_element_type=jnp.float32)
        * scale
    )
    grad_keys = (
        jnp.einsum("ghij,gihd->gjhd", grad_scores, query, preferred_element_type=jnp.float32)
        * scale
    )
    grad_edges = jnp.concatenate(
        [
            grad_keys.reshape(num_seqs, span, model_width),
            grad_values.reshape(num_seqs, span, model_width),
        ],
        -1,
    )
    from_next = passed_along(grad_edges[:, :half_span].astype(jnp.bfloat16), "seq", -1).astype(
        jnp.float32
    )
    from_prev = passed_along(grad_edges[:, tok_block + half_span :], "seq", 1)
    grad_own = grad_edges[:, half_span : half_span + tok_block]
    grad_own = (
        grad_own
        + jnp.pad(from_prev, ((0, 0), (0, tok_block - half_span), (0, 0)))
        + jnp.pad(from_next, ((0, 0), (tok_block - half_span, 0), (0, 0)))
    )
    grad_key_own = rotate_back(grad_own[..., :model_width].reshape(head_shape), cosine, sine)
    grad_query_raw = rotate_back(grad_query, cosine, sine)
    grad_qkv_all = jnp.concatenate(
        [
            grad_query_raw.reshape(num_seqs, tok_block, model_width),
            grad_key_own.reshape(num_seqs, tok_block, model_width),
            grad_own[..., model_width:],
        ],
        -1,
    ).astype(jnp.bfloat16)
    grad_qkv = weight_grad(hidden_one, grad_qkv_all)
    grad_hidden_one = through_weight(grad_qkv_all, w_qkv)
    gain_grad_one = jnp.sum((grad_hidden_one * normed_one).reshape(-1, model_width), 0)
    grad_tokens = grad_stream + norm_back(grad_hidden_one * gain_one, normed_one, factor_one)
    grad_gains = jnp.stack([gain_grad_one, gain_grad_two])
    local_grads = (grad_qkv, grad_out, grad_in, grad_down, grad_gains)
    summed = lax.psum(
        (local_grads[0], local_grads[1], local_grads[2], local_grads[3], local_grads[4]),
        ("seq", "fsdp"),
    )
    owner_index = lax.axis_index("fsdp")
    shard_like = (qkv_weight, out_weight, in_weight, down_weight, norm_gains)
    shard_dims = (0, 0, 0, 0, 1)
    pieces = tuple(
        (
            lax.dynamic_slice_in_dim(
                whole_grad,
                owner_index * like_arg.shape[axis_dim],
                like_arg.shape[axis_dim],
                axis_dim,
            )
            for whole_grad, like_arg, axis_dim in zip(summed, shard_like, shard_dims)
        )
    )
    return (
        layer_out.astype(jnp.bfloat16),
        grad_tokens.astype(jnp.bfloat16),
        pieces[0],
        pieces[1],
        pieces[2],
        pieces[3],
        pieces[4],
    )


def solution(mesh):
    in_specs = (
        P("fsdp", "seq", None),
        P("fsdp", None),
        P("fsdp", None),
        P("fsdp", None),
        P("fsdp", None),
        P("fsdp", None),
        P(None, "fsdp"),
        P("fsdp", "seq", None),
    )
    out_specs = (
        P("fsdp", "seq", None),
        P("fsdp", "seq", None),
        P("fsdp", None),
        P("fsdp", None),
        P("fsdp", None),
        P("fsdp", None),
        P(None, "fsdp"),
    )
    return jax.shard_map(local, mesh=mesh, in_specs=in_specs, out_specs=out_specs, check_vma=False)
```

profile of v0, /device:TPU:0, one launch (start us, length us, event | category | flops | bytes accessed | tf_op | source)
XLA Modules:
  0.0 674.9 jit_solution(9298906354205010199)
XLA Ops:
  9.5 5.2 all_gather.15
  16.4 45.3 %all-gather.5.cloned.1.call-done = bf16[768,2304]{1,0:T(8,128)(2,1)} async-done(((bf16[384,2304]{1,0:T(8,128)(2,1)}), bf16[768,2304]{1,0:T(8,128)(2,1)}) %all-gather.5.cloned.1.call-update) | async-done | bytes 3538960 | tf_op jit(solution)/shard_map/all_gather | solution.py:104
  61.7 6.1 fusion.29
  78.5 4.9 subtract_convert_fusion.2
  89.7 4.2 collective-permute-start
  96.1 4.1 pad_maximum_fusion
  108.4 5.6 fusion.15
  114.0 5.0 fusion
  119.3 6.2 fusion.45
  130.3 6.7 all-gather.9.cloned.1.call-done
  137.0 8.4 %fusion.25 = f32[8,128,2304]{2,1,0:T(8,128)} fusion(bf16[768,2304]{1,0:T(8,128)(2,1)} %all-gather.9.cloned.1.call-done, f32[8,128,768]{2,1,0:T(8,128)S(1)} %get-tuple-element.55, f32[768]{0:T(1024)S(1)} %get-tuple-element.13, f32[8,128]{1,0:T(8,128)S(1)} %add_rsqrt_fusion, f32[8,128]{1,0:T(8,128)S(1)} %broadcast_multiply_fusion.5), kind=kOutput, calls=%fused_computation.56 | convolution fusion | flops 3627024384 | bytes 16133120 | tf_op jit(solution)/shard_map/dot_general | solution.py:153
  145.3 22.5 %all-gather.11.cloned.1.call-done = bf16[1152,768]{1,0:T(8,128)(2,1)} async-done(((bf16[576,768]{1,0:T(8,128)(2,1)}), bf16[1152,768]{1,0:T(8,128)(2,1)}) %all-gather.11.cloned.1.call-update) | async-done | bytes 1769488 | tf_op jit(solution)/shard_map/all_gather | solution.py:107
  167.8 15.7 %add_convert_fusion = (bf16[8,128,1152]{2,1,0:T(8,128)(2,1)}, f32[8,128,1152]{2,1,0:T(8,128)S(1)}, f32[8,128,1152]{2,1,0:T(8,128)S(1)}) fusion(f32[8,128,2304]{2,1,0:T(8,128)} %fusion.25, bf16[8,128,768]{2,1,0:T(8,128)(2,1)} %param.15, bf16[1152,768]{1,0:T(8,128)(2,1)} %all-gather.11.cloned.1.call-done), kind=kOutput, calls=%fused_computation.29 | convolution fusion | flops 1898053632 | bytes 24576000 | tf_op jit(solution)/shard_map/dot_general | solution.py:91
  186.2 6.9 %multiply_reduce_fusion.1 = (f32[768]{0:T(1024)S(1)}, f32[8,128]{1,0:T(8,128)S(1)}, f32[8,128]{1,0:T(8,128)S(1)}, f32[8,128,768]{2,1,0:T(8,128)S(1)}) fusion(f32[8,128,768]{2,1,0:T(8,128)S(1)} %get-tuple-element.55, f32[8,128]{1,0:T(8,128)S(1)} %add_rsqrt_fusion, f32[8,128]{1,0:T(8,128)S(1)} %broadcast_multiply_fusion.5, f32[768]{0:T(1024)S(1)} %get-tuple-element.13, ...), kind=kOutput, calls=%fused_computation.77 | convolution fusion | flops 3639604480 | bytes 14571520 | tf_op jit(solution)/shard_map/dot_general | solution.py:91
  198.3 11.3 %multiply_reduce_fusion = (f32[8,12,128]{2,1,0:T(8,128)S(1)}, f32[8,12,128,256]{3,2,1,0:T(8,128)}) fusion(f32[8,12,128]{2,1,0:T(8,128)S(1)} %log_add_fusion, f32[8,12,128,256]{3,2,1,0:T(8,128)} %copy-done, pred[8,128,256]{2,1,0:T(8,128)(4,1)S(1)} %or_and_fusion, bf16[8,128,12,64]{1,3,2,0:T(8,128)(2,1)S(1)} %bitcast.82, bf16[8,256,12,64]{1,3,2,0:T(8,128)(2,1)} %bitcast.87), kind=kOutput, calls=%fused_computation.5 | convolution fusion | flops 418369536 | bytes 30244864 | tf_op jit(solution)/shard_map/gihd,gjhd->ghij/dot_general | solution.py:179
  209.6 9.0 %fusion.2 = f32[8,12,64,256]{3,2,1,0:T(8,128)} fusion(bf16[8,128,12,64]{1,3,2,0:T(8,128)(2,1)S(1)} %bitcast.83, f32[8,12,128]{2,1,0:T(8,128)S(1)} %log_add_fusion, f32[8,12,128,256]{3,2,1,0:T(8,128)} %copy-done, pred[8,128,256]{2,1,0:T(8,128)(4,1)S(1)} %or_and_fusion), kind=kOutput, calls=%fused_computation.13 | convolution fusion | flops 415236096 | bytes 20758528 | tf_op jit(solution)/shard_map/ghij,gihd->gjhd/dot_general | solution.py:173
  218.7 8.7 %multiply_convert_fusion = bf16[8,12,128,256]{3,2,1,0:T(8,128)(2,1)S(1)} fusion(f32[8,12,128,256]{3,2,1,0:T(8,128)} %get-tuple-element.59, f32[8,12,128]{2,1,0:T(8,128)S(1)} %get-tuple-element.58, f32[8,12,128]{2,1,0:T(8,128)S(1)} %log_add_fusion, f32[8,12,128,256]{3,2,1,0:T(8,128)S(1)} %bitcast.73, pred[8,128,256]{2,1,0:T(8,128)(4,1)S(1)} %or_and_fusion), kind=kLoop, calls=%fused_computation.4 | loop fusion | flops 18874368 | bytes 31817728 | tf_op jit(solution)/shard_map/convert_element_type | solution.py:183
  227.4 4.0 broadcast_multiply_fusion
  231.9 6.6 copy.42
  238.5 6.7 copy.43
  245.2 4.0 fusion.39
  249.3 6.2 collective-permute-start.2
  265.3 4.0 multiply_bitcast_fusion
  269.3 9.3 %convolution_bitcast_fusion = f32[768,2304]{1,0:T(8,128)} fusion(bf16[8,128,1152]{2,1,0:T(8,128)(2,1)} %copy-done.19, bf16[8,128,1152]{2,1,0:T(8,128)(2,1)} %get-tuple-element.19, f32[8,128,768]{2,1,0:T(8,128)S(1)} %copy-done.4, f32[768]{0:T(1024)S(1)} %get-tuple-element.13, f32[8,128]{1,0:T(8,128)S(1)} %add_rsqrt_fusion, ...), kind=kOutput, calls=%fused_computation.20 | convolution fusion | flops 3636461568 | bytes 14953472 | tf_op jit(solution)/shard_map/dot_general | solution.py:85
  285.6 4.9 add_convert_fusion.3
  295.6 9.3 %convolution_bitcast_fusion.1 = f32[768,2304]{1,0:T(8,128)} fusion(bf16[8,128,768]{2,1,0:T(8,128)(2,1)} %slice.190, bf16[8,128,768]{2,1,0:T(8,128)(2,1)} %copy.46, bf16[8,128,768]{2,1,0:T(8,128)(2,1)} %copy.45, bf16[8,128,768]{2,1,0:T(8,128)(2,1)S(1)} %copy-done.9, f32[768]{0:T(1024)S(1)} %copy-done.39, f32[8,128]{1,0:T(8,128)S(1)} %copy-done.41, ...), kind=kOutput, calls=%fused_computation.21 | convolution fusion | flops 3641966592 | bytes 13380608 | tf_op jit(solution)/shard_map/dot_general | solution.py:85
  306.8 5.7 add_convert_fusion.1
  312.6 5.7 fusion.37
  318.3 71.8 %psum.39 = f32[2,768]{1,0:T(2,128)S(1)} all-reduce(f32[2,768]{1,0:T(2,128)S(1)} %pad_maximum_fusion.15), channel_id=1, replica_groups=mesh['seq'=16,'fsdp'=2] {'seq','fsdp'}, use_global_device_ids=true, to_apply=%region_17.18 | all-reduce | flops 1536 | bytes 12288 | tf_op jit(solution)/shard_map/psum | solution.py:225
  390.7 4.8 fusion.36
  395.5 261.1 %all-reduce.6.cloned.1.call-done = (f32[768,2304]{1,0:T(8,128)}, f32[768,768]{1,0:T(8,128)}, f32[768,2304]{1,0:T(8,128)}, f32[1152,768]{1,0:T(8,128)}) async-done(((f32[768,2304]{1,0:T(8,128)}, f32[768,768]{1,0:T(8,128)}, f32[768,2304]{1,0:T(8,128)}, f32[1152,768]{1,0:T(8,128)}), (f32[768,2304]{1,0:T(8,128)}, f32[768,768]{1,0:T(8,128)}, f32[768,2304]{1,0:T(8,128)}, ...) | async-done | bytes 20054032 | tf_op jit(solution)/shard_map/psum | solution.py:225
  656.6 4.2 constant_dynamic-slice_fusion.4
  (177 shorter events, 75.8 us)
Async XLA Ops:
  7.2 7.6 %copy-start.8 = (bf16[8,128,768]{2,1,0:T(8,128)(2,1)S(1)}, bf16[8,128,768]{2,1,0:T(8,128)(2,1)}, u32[]{:S(2)}) copy-start(bf16[8,128,768]{2,1,0:T(8,128)(2,1)} %param.8) | copy-start | bytes 4718596
  7.2 7.9 %copy-start.35 = (s32[8,2048]{1,0:T(8,128)S(1)}, s32[8,2048]{1,0:T(8,128)}, u32[]{:S(2)}) copy-start(s32[8,2048]{1,0:T(8,128)} %param.9) | copy-start | bytes 196612
  7.2 54.5 %all-gather.5.cloned.1.call-start = ((), (), s32[]{:S(2)}) async-start(), calls=%async_computation | async-start | bytes 5308416 | tf_op jit(solution)/shard_map/all_gather | solution.py:104
  7.9 117.6 %all-gather.7.cloned.1.call-start = ((), (), s32[]{:S(2)}) async-start(), calls=%async_computation.1 | async-start | bytes 1769472 | tf_op jit(solution)/shard_map/all_gather | solution.py:105
  8.7 128.3 %all-gather.9.cloned.1.call-start = ((), (), s32[]{:S(2)}) async-start(), calls=%async_computation.2 | async-start | bytes 5308416 | tf_op jit(solution)/shard_map/all_gather | solution.py:106
  9.4 158.4 %all-gather.11.cloned.1.call-start = ((), (), s32[]{:S(2)}) async-start(), calls=%async_computation.3 | async-start | bytes 2654208 | tf_op jit(solution)/shard_map/all_gather | solution.py:107
  14.8 53.0 %copy-start.38 = (f32[768]{0:T(1024)}, f32[768]{0:T(1024)S(1)}, u32[]{:S(2)}) copy-start(f32[768]{0:T(1024)S(1)} %get-tuple-element.14) | copy-start | bytes 9220
  15.1 52.7 %copy-start.36 = (f32[8,128]{1,0:T(8,128)}, f32[8,128]{1,0:T(8,128)S(1)}, u32[]{:S(2)}) copy-start(f32[8,128]{1,0:T(8,128)S(1)} %broadcast_multiply_fusion.6) | copy-start | bytes 12292
  15.8 52.0 %copy-start.40 = (f32[8,128]{1,0:T(8,128)}, f32[8,128]{1,0:T(8,128)S(1)}, u32[]{:S(2)}) copy-start(f32[8,128]{1,0:T(8,128)S(1)} %add_rsqrt_fusion.1) | copy-start | bytes 12292
  16.3 62.1 %copy-start.27 = (f32[8,128,32]{1,2,0:T(8,128)}, f32[8,128,32]{1,2,0:T(8,128)S(1)}, u32[]{:S(2)}) copy-start(f32[8,128,32]{1,2,0:T(8,128)S(1)} %get-tuple-element.45) | copy-start | bytes 393220
  16.3 62.1 %copy-start.29 = (f32[8,128,32]{1,2,0:T(8,128)}, f32[8,128,32]{1,2,0:T(8,128)S(1)}, u32[]{:S(2)}) copy-start(f32[8,128,32]{1,2,0:T(8,128)S(1)} %get-tuple-element.46) | copy-start | bytes 393220
  88.4 6.2 collective-permute-start.1
  89.7 6.4 collective-permute-start
  93.9 562.7 %all-reduce.6.cloned.1.call-start = ((), (), s32[]{:S(2)}) async-start(), calls=%async_computation.4 | async-start | bytes 40108032 | tf_op jit(solution)/shard_map/psum | solution.py:225
  129.4 63.7 %copy-start.3 = (f32[8,128,768]{2,1,0:T(8,128)}, f32[8,128,768]{2,1,0:T(8,128)S(1)}, u32[]{:S(2)}) copy-start(f32[8,128,768]{2,1,0:T(8,128)S(1)} %get-tuple-element.55) | copy-start | bytes 9437188
  167.8 15.7 %copy-start.15 = (f32[8,128,2304]{2,1,0:T(8,128)S(1)}, f32[8,128,2304]{2,1,0:T(8,128)}, u32[]{:S(2)}) copy-start(f32[8,128,2304]{2,1,0:T(8,128)} %fusion.25) | copy-start | bytes 28311556
  186.2 6.9 %copy-start.19 = (bf16[8,128,1152]{2,1,0:T(8,128)(2,1)}, bf16[8,128,1152]{2,1,0:T(8,128)(2,1)S(1)}, u32[]{:S(2)}) copy-start(bf16[8,128,1152]{2,1,0:T(8,128)(2,1)S(1)} %get-tuple-element.25) | copy-start | bytes 7077892
  186.2 6.9 %copy-start.21 = (bf16[8,128,768]{2,1,0:T(8,128)(2,1)S(1)}, bf16[8,128,768]{2,1,0:T(8,128)(2,1)}, u32[]{:S(2)}) copy-start(bf16[8,128,768]{2,1,0:T(8,128)(2,1)} %param.15) | copy-start | bytes 4718596
  198.3 20.4 %slice-start = ((s8[12582912]{0:T(1024)(128)(4,1)}), s8[4194304]{0:T(1024)(128)(4,1)S(1)}, s32[]{:S(2)}) async-start(s8[12582912]{0:T(1024)(128)(4,1)} %bitcast.72), calls=%async_computation.5 | async-start | bytes 8388608
  198.3 20.4 %slice-start.1 = ((s8[12582912]{0:T(1024)(128)(4,1)}), s8[4194304]{0:T(1024)(128)(4,1)S(1)}, s32[]{:S(2)}) async-start(s8[12582912]{0:T(1024)(128)(4,1)} %bitcast.72), calls=%async_computation.6 | async-start | bytes 8388608
  209.6 9.0 %slice-start.2 = ((s8[12582912]{0:T(1024)(128)(4,1)}), s8[4194304]{0:T(1024)(128)(4,1)S(1)}, s32[]{:S(2)}) async-start(s8[12582912]{0:T(1024)(128)(4,1)} %bitcast.72), calls=%async_computation.7 | async-start | bytes 8388608
  218.7 8.7 %copy-start.16 = (bf16[8,128,12,32]{1,3,2,0:T(8,128)(2,1)S(1)}, bf16[8,128,12,32]{1,3,2,0:T(8,128)(2,1)}, u32[]{:S(2)}) copy-start(bf16[8,128,12,32]{1,3,2,0:T(8,128)(2,1)} %get-tuple-element.35) | copy-start | bytes 2359300
  218.7 8.7 %copy-start.17 = (bf16[8,128,12,32]{1,3,2,0:T(8,128)(2,1)S(1)}, bf16[8,128,12,32]{1,3,2,0:T(8,128)(2,1)}, u32[]{:S(2)}) copy-start(bf16[8,128,12,32]{1,3,2,0:T(8,128)(2,1)} %get-tuple-element.36) | copy-start | bytes 2359300
  238.5 16.9 %slice-start.3 = ((s8[6291456]{0:T(1024)(128)(4,1)}), s8[2097152]{0:T(1024)(128)(4,1)S(1)}, s32[]{:S(2)}) async-start(s8[6291456]{0:T(1024)(128)(4,1)} %bitcast.74), calls=%async_computation.8 | async-start | bytes 4194304
  245.2 10.2 %slice-start.4 = ((s8[6291456]{0:T(1024)(128)(4,1)}), s8[4194304]{0:T(1024)(128)(4,1)S(1)}, s32[]{:S(2)}) async-start(s8[6291456]{0:T(1024)(128)(4,1)} %bitcast.74), calls=%async_computation.9 | async-start | bytes 8388608
  245.2 10.2 %copy-start.1 = (f32[8,256,768]{2,1,0:T(8,128)S(1)}, f32[8,256,768]{2,1,0:T(8,128)}, u32[]{:S(2)}) copy-start(f32[8,256,768]{2,1,0:T(8,128)} %copy.43) | copy-start | bytes 18874372
  249.3 9.2 %copy-start.18 = (bf16[8,128,1152]{2,1,0:T(8,128)(2,1)S(1)}, bf16[8,128,1152]{2,1,0:T(8,128)(2,1)}, u32[]{:S(2)}) copy-start(bf16[8,128,1152]{2,1,0:T(8,128)(2,1)} %get-tuple-element.26) | copy-start | bytes 7077892
  249.3 9.2 %copy-start.22 = (bf16[8,128,768]{2,1,0:T(8,128)(2,1)S(1)}, bf16[8,128,768]{2,1,0:T(8,128)(2,1)}, u32[]{:S(2)}) copy-start(bf16[8,128,768]{2,1,0:T(8,128)(2,1)} %param.15) | copy-start | bytes 4718596
  249.3 29.3 %collective-permute-start.2 = (f32[8,64,1536]{2,1,0:T(8,128)}, f32[8,64,1536]{2,1,0:T(8,128)}, u32[]{:S(2)}, u32[]{:S(2)}) collective-permute-start(f32[8,64,1536]{2,1,0:T(8,128)} %fusion.39), channel_id=1, source_target_pairs={{0,2},{2,4},{4,6},{6,8},{8,10},{10,12},{12,14},{14,16},{16,18},{18... | collective-permute-start | bytes 9437192 | tf_op jit(solution)/shard_map/ppermute | solution.py:30
  255.5 9.8 %slice-start.5 = ((s8[6291456]{0:T(1024)(128)(4,1)}), s8[4194304]{0:T(1024)(128)(4,1)S(1)}, s32[]{:S(2)}) async-start(s8[6291456]{0:T(1024)(128)(4,1)} %bitcast.76), calls=%async_computation.10 | async-start | bytes 8388608
  256.8 21.7 %collective-permute-start.3 = (bf16[8,64,1536]{2,1,0:T(8,128)(2,1)}, bf16[8,64,1536]{2,1,0:T(8,128)(2,1)}, u32[]{:S(2)}, u32[]{:S(2)}) collective-permute-start(bf16[8,64,1536]{2,1,0:T(8,128)(2,1)} %fusion.40), channel_id=1, source_target_pairs={{2,0},{4,2},{6,4},{8,6},{10,8},{12,10},{14,12},{16,14},{18,16},{20... | collective-permute-start | bytes 4718600 | tf_op jit(solution)/shard_map/ppermute | solution.py:30
  312.6 78.1 %copy-start.11 = (bf16[8,128,768]{2,1,0:T(8,128)(2,1)S(1)}, bf16[8,128,768]{2,1,0:T(8,128)(2,1)}, u32[]{:S(2)}) copy-start(bf16[8,128,768]{2,1,0:T(8,128)(2,1)} %param.8) | copy-start | bytes 4718596
  (29 other events, 117.3 us)
Sparse Core Ops, SparseCore 0:
  9.6 52.0 all-gather.4
  63.2 22.7 all-gather.6
  87.6 49.3 all-gather.8
  138.4 29.4 all-gather.10
  305.1 351.4 all-reduce.5
where the time goes:
time: 682 us; the launch traced here: 675 us
  waiting for transfers between devices  339 us (50%)
  matrix products  119 us (17%)
  blocking collectives  77 us (11%)
  local copies, waits for them, and re-layouts  58.6 us (9%)
  other arithmetic  52.5 us (8%)
  between operations  14.9 us (2%)
  starting transfers between devices  13.5 us (2%)
    psum x1, waiting for transfers between devices, local(): lax.psum((local_grads[0], local_grads[1], local_grads[2], local_grads[3],...  261 us
    psum x1, blocking collectives, local(): lax.psum((local_grads[0], local_grads[1], local_grads[2], local_grads[3],...  71.8 us
    all_gather x1, waiting for transfers between devices, local(): lax.all_gather(qkv_weight, 'fsdp', axis=0, tiled=True)  45.3 us
    dot_general x4, matrix products, through_weight(): lax.dot_general(grads, weight, (((grads.ndim - 1,), (1,)), ((), ())), pre...  29.7 us
    dot_general x4, matrix products, weight_grad(): lax.dot_general(left_rows, right_rows, (((0,), (0,)), ((), ())), preferre...  25.3 us
    all_gather x1, waiting for transfers between devices, local(): lax.all_gather(down_weight, 'fsdp', axis=0, tiled=True)  22.5 us
    another operation x4, other arithmetic  13.8 us
  transfers between devices with their start and end apart: 9, of which 5 were waited for; matrix products, arithmetic and copies ran while one was open for 16% of the time, Pallas kernels for 0%

commit v1 on v0

--- a/solution.py
+++ b/solution.py
@@ -93,6 +93,99 @@
     )
 
 
+def flip_route(size, bit):
+    return [(i, i ^ bit) for i in range(size)]
+
+
+def gather_shards(shards):
+    own_y = lax.axis_index("fsdp")
+    core = lax.axis_index("seq") % 2
+    seq = lax.axis_size("seq")
+    wholes = []
+    for shard in shards:
+        rows = shard.shape[0]
+        half = rows // 2
+        mine = lax.dynamic_slice_in_dim(shard, core * half, half, 0)
+        far = lax.ppermute(mine, "fsdp", flip_route(2, 1))
+        near = lax.ppermute(far, "seq", flip_route(seq, 1))
+        other = jnp.where(
+            core == 0, jnp.concatenate([far, near], 0), jnp.concatenate([near, far], 0)
+        )
+        wholes.append(
+            jnp.where(
+                own_y == 0,
+                jnp.concatenate([shard, other], 0),
+                jnp.concatenate([other, shard], 0),
+            )
+        )
+    return wholes
+
+
+def keep_and_send(block, bit, dim):
+    half = block.shape[dim] // 2
+    keep = lax.dynamic_slice_in_dim(block, bit * half, half, dim)
+    send = lax.dynamic_slice_in_dim(block, (1 - bit) * half, half, dim)
+    return keep, send
+
+
+def exchange(block, stage):
+    if stage < 0:
+        return lax.ppermute(block, "fsdp", flip_route(2, 1))
+    return lax.ppermute(block, "seq", flip_route(lax.axis_size("seq"), 1 << stage))
+
+
+def stage_bit(stage):
+    if stage < 0:
+        return lax.axis_index("fsdp")
+    return (lax.axis_index("seq") >> stage) & 1
+
+
+def reduce_stage(block, stage):
+    keep, send = keep_and_send(block, stage_bit(stage), 0 if stage < 0 else 1)
+    got = exchange(send.astype(jnp.bfloat16), stage)
+    return (keep.astype(jnp.float32) + got.astype(jnp.float32)).astype(jnp.bfloat16)
+
+
+def summed_half(bundle):
+    stages = (lax.axis_size("seq") - 1).bit_length()
+    width = bundle.shape[2] // 2
+    bundle = jnp.pad(bundle, ((0, 0), (0, -bundle.shape[1] % lax.axis_size("seq")), (0, 0)))
+    bundle = reduce_stage(bundle, 0)
+    parts = [bundle[:, :, :width], bundle[:, :, width:]]
+    orders = [[-1] + list(range(1, stages)), [1, -1] + list(range(2, stages))]
+    for step in range(stages):
+        parts = [reduce_stage(part, order[step]) for part, order in zip(parts, orders)]
+    parts = [part[0] for part in parts]
+    for stage in reversed(range(stages)):
+        if stage == 0:
+            parts = [jnp.concatenate(parts, 1)]
+        bit = stage_bit(stage)
+        got = [exchange(part, stage) for part in parts]
+        parts = [
+            jnp.where(bit == 0, jnp.concatenate([p, g], 0), jnp.concatenate([g, p], 0))
+            for p, g in zip(parts, got)
+        ]
+    return parts[0]
+
+
+def summed_small(value):
+    stages = (lax.axis_size("seq") - 1).bit_length()
+    for stage in range(-1, stages):
+        value = value + exchange(value, stage)
+    return value
+
+
+def fold_rows(block, width):
+    count = width // block.shape[2]
+    rows = block.shape[1] // count
+    return jnp.concatenate([block[:, i * rows : (i + 1) * rows] for i in range(count)], 2)
+
+
+def unfold_rows(block, width):
+    count = block.shape[1] // width
+    return jnp.concatenate([block[:, i * width : (i + 1) * width] for i in range(count)], 0)
+
+
 def local(tokens, positions, qkv_weight, out_weight, in_weight, down_weight, norm_gains, cotangent):
     num_seqs, tok_block, model_width = tokens.shape
     head_width = HEAD_DIM
@@ -100,13 +193,13 @@
     half_span = HALF_WINDOW
     span = tok_block + 2 * half_span
     scale = head_width ** (-0.5)
-    w_qkv, w_out, w_in, w_down, gains = (
-        lax.all_gather(qkv_weight, "fsdp", axis=0, tiled=True),
-        lax.all_gather(out_weight, "fsdp", axis=0, tiled=True),
-        lax.all_gather(in_weight, "fsdp", axis=0, tiled=True),
-        lax.all_gather(down_weight, "fsdp", axis=0, tiled=True),
-        lax.all_gather(norm_gains, "fsdp", axis=1, tiled=True),
-    )
+    gains_other = lax.ppermute(norm_gains, "fsdp", flip_route(2, 1))
+    gains = jnp.where(
+        lax.axis_index("fsdp") == 0,
+        jnp.concatenate([norm_gains, gains_other], 1),
+        jnp.concatenate([gains_other, norm_gains], 1),
+    )
+    w_qkv, w_out, w_in, w_down = gather_shards([qkv_weight, out_weight, in_weight, down_weight])
     ffn_width = w_in.shape[1] // 2
     gain_one = gains[0].astype(jnp.float32)
     gain_two = gains[1].astype(jnp.float32)
@@ -221,24 +314,30 @@
     gain_grad_one = jnp.sum((grad_hidden_one * normed_one).reshape(-1, model_width), 0)
     grad_tokens = grad_stream + norm_back(grad_hidden_one * gain_one, normed_one, factor_one)
     grad_gains = jnp.stack([gain_grad_one, gain_grad_two])
-    local_grads = (grad_qkv, grad_out, grad_in, grad_down, grad_gains)
-    summed = lax.psum(
-        (local_grads[0], local_grads[1], local_grads[2], local_grads[3], local_grads[4]),
-        ("seq", "fsdp"),
-    )
-    owner_index = lax.axis_index("fsdp")
-    shard_like = (qkv_weight, out_weight, in_weight, down_weight, norm_gains)
-    shard_dims = (0, 0, 0, 0, 1)
+    qkv_sum = summed_half(grad_qkv.reshape(2, -1, grad_qkv.shape[1]))
+    wide = grad_in.shape[1]
+    bundle = jnp.concatenate(
+        [
+            grad_in.reshape(2, -1, wide),
+            fold_rows(grad_down.reshape(2, -1, model_width), wide),
+            fold_rows(grad_out.reshape(2, -1, model_width), wide),
+        ],
+        1,
+    )
+    bundle_sum = summed_half(bundle)
+    in_rows = in_weight.shape[0]
+    down_rows = down_weight.shape[0] * model_width // wide
+    in_sum = bundle_sum[:in_rows]
+    down_sum = unfold_rows(bundle_sum[in_rows : in_rows + down_rows], model_width)
+    out_sum = unfold_rows(
+        bundle_sum[in_rows + down_rows : in_rows + down_rows + out_weight.shape[0] * model_width // wide],
+        model_width,
+    )
+    gains_sum = lax.dynamic_slice_in_dim(
+        summed_small(grad_gains), lax.axis_index("fsdp") * norm_gains.shape[1], norm_gains.shape[1], 1
+    )
     pieces = tuple(
-        (
-            lax.dynamic_slice_in_dim(
-                whole_grad,
-                owner_index * like_arg.shape[axis_dim],
-                like_arg.shape[axis_dim],
-                axis_dim,
-            )
-            for whole_grad, like_arg, axis_dim in zip(summed, shard_like, shard_dims)
-        )
+        total.astype(jnp.float32) for total in (qkv_sum, out_sum, in_sum, down_sum, gains_sum)
     )
     return (
         layer_out.astype(jnp.bfloat16),

time: 682 us -> 553 us (0.81)
  waiting for transfers between devices: 339 us -> 132 us
  blocking collectives: 77 us -> 0 us
  starting transfers between devices: 13.5 us -> 88.7 us
  local copies, waits for them, and re-layouts: 58.6 us -> 111 us
  other arithmetic: 52.5 us -> 102 us
  between operations: 14.9 us -> 2.27 us
  matrix products: 119 us -> 108 us
    psum x1 -> x0, waiting for transfers between devices: 261 us -> none  [local(): lax.psum((local_grads[0], local_grads[1], local_grads[2], local_grads[3],...]
    ppermute x0 -> x46, waiting for transfers between devices: none -> 132 us  [the longest x32 81.4 us: exchange(): lax.ppermute(block, 'seq', flip_route(lax.axis_size('seq'), 1 << stage))]
    all_gather x4 -> x0, waiting for transfers between devices: 74.5 us -> none  [the longest x1 45.3 us: local(): lax.all_gather(qkv_weight, 'fsdp', axis=0, tiled=True)]
    psum x1 -> x0, blocking collectives: 71.8 us -> none  [local(): lax.psum((local_grads[0], local_grads[1], local_grads[2], local_grads[3],...]
    ppermute x0 -> x46, starting transfers between devices: none -> 61.9 us  [the longest x32 46.6 us: exchange(): lax.ppermute(block, 'seq', flip_route(lax.axis_size('seq'), 1 << stage))]
    select_n x0 -> x18, other arithmetic: none -> 24 us  [the longest x13 13.4 us: summed_half(): jnp.where(bit == 0, jnp.concatenate([p, g], 0), jnp.concatenate([g, p], 0))]
    unnamed x104 -> x153, local copies, waits for them, and re-layouts: 6.04 us -> 25.3 us
    ppermute x2, starting transfers between devices: 7.8 us -> 22.3 us  [passed_along(): return lax.ppermute(block, axis, route)]
  transfers between devices with their start and end apart: 9 -> 50, of which waited for: 5 -> 27; matrix products, arithmetic and copies ran while one was open for 16% -> 28% of each run, Pallas kernels for 0% -> 0%
where the time goes in v1:
time: 553 us; the launch traced here: 545 us
  waiting for transfers between devices  132 us (24%)
  local copies, waits for them, and re-layouts  111 us (20%)
  matrix products  108 us (20%)
  other arithmetic  102 us (18%)
  starting transfers between devices  88.7 us (16%)
    ppermute x32, waiting for transfers between devices, exchange(): lax.ppermute(block, 'seq', flip_route(lax.axis_size('seq'), 1 << stage))  81.4 us
    ppermute x32, starting transfers between devices, exchange(): lax.ppermute(block, 'seq', flip_route(lax.axis_size('seq'), 1 << stage))  46.6 us
    dot_general x4, matrix products, through_weight(): lax.dot_general(grads, weight, (((grads.ndim - 1,), (1,)), ((), ())), pre...  36.6 us
    ppermute x4, waiting for transfers between devices, gather_shards(): far = lax.ppermute(mine, 'fsdp', flip_route(2, 1))  28.4 us
    unnamed x153, local copies, waits for them, and re-layouts  25.3 us
    ppermute x2, starting transfers between devices, passed_along(): return lax.ppermute(block, axis, route)  22.3 us
    ppermute x5, waiting for transfers between devices, exchange(): return lax.ppermute(block, 'fsdp', flip_route(2, 1))  20.3 us
    dot_general x4, matrix products, weight_grad(): lax.dot_general(left_rows, right_rows, (((0,), (0,)), ((), ())), preferre...  18.5 us
  transfers between devices with their start and end apart: 50, of which 27 were waited for; matrix products, arithmetic and copies ran while one was open for 28% of the time, Pallas kernels for 0%

profile of v1, /device:TPU:0, one launch (start us, length us, event | category | flops | bytes accessed | tf_op | source)
XLA Modules:
  0.0 544.7 jit_solution(16180355921963783004)
XLA Ops:
  15.6 28.4 %collective-permute-done.1 = bf16[192,2304]{1,0:T(8,128)(2,1)} collective-permute-done((bf16[192,2304]{1,0:T(8,128)(2,1)S(1)}, bf16[192,2304]{1,0:T(8,128)(2,1)}, u32[]{:S(2)}, u32[]{:S(2)}) %collective-permute-start.1) | collective-permute-done | bytes 884768 | tf_op jit(solution)/shard_map/ppermute | solution.py:109
  63.3 5.0 subtract_convert_fusion
  104.6 5.4 copy.37
  110.0 5.0 fusion.34
  115.0 5.0 fusion
  120.3 5.6 %fusion.62 = bf16[8,12,64,128]{3,2,1,0:T(8,128)(2,1)S(1)} fusion(bf16[8,256,12,64]{1,3,2,0:T(8,128)(2,1)S(1)} %bitcast.151, f32[8,12,128]{2,1,0:T(8,128)S(1)} %fusion, f32[8,12,128]{2,1,0:T(8,128)S(1)} %get-tuple-element.64, f32[8,12,128,256]{3,2,1,0:T(8,128)S(1)} %get-tuple-element.65, pred[8,128,256]{2,1,0:T(8,128)(4,1)S(1)} %or_and_fusion), kind=kOutput, calls=%fused_computation.118 | convolution fusion | flops 419168256 | bytes 17661952 | tf_op jit(solution)/shard_map/ghij,gjhd->gihd/dot_general | solution.py:241
  134.6 15.5 %add_convert_fusion.1 = (bf16[8,128,1152]{2,1,0:T(8,128)(2,1)}, f32[8,128,1152]{2,1,0:T(8,128)S(1)}, f32[1152,8,128]{0,2,1:T(8,128)S(1)}) fusion(f32[8,128,2304]{2,1,0:T(8,128)S(1)} %fusion.55, bf16[8,128,768]{2,1,0:T(8,128)(2,1)S(1)} %copy-done.24, bf16[576,768]{1,0:T(8,128)(2,1)S(1)} %copy-done.42, bf16[576,768]{1,0:T(8,128)(2,1)S(1)} %copy-done.49, ...), kind=kOutput, calls=%fused_computation.50 | convolution fusion | flops 1906016256 | bytes 24576000 | tf_op jit(solution)/shard_map/dot_general | solution.py:91
  153.0 9.0 %multiply_reduce_fusion.1 = (f32[768]{0:T(1024)S(1)}, f32[8,128]{1,0:T(8,128)S(1)}, f32[8,128]{1,0:T(8,128)S(1)}, f32[8,128,768]{2,1,0:T(8,128)S(1)}) fusion(f32[8,128,768]{2,1,0:T(8,128)S(1)} %get-tuple-element.67, f32[8,128]{1,0:T(8,128)S(1)} %add_rsqrt_fusion, f32[8,128]{1,0:T(8,128)S(1)} %broadcast_multiply_fusion.5, f32[768]{0:T(1024)S(1)} %get-tuple-element.13, ...), kind=kOutput, calls=%fused_computation.98 | convolution fusion | flops 3655529728 | bytes 14571521 | tf_op jit(solution)/shard_map/dot_general | solution.py:91
  167.2 8.0 %fusion.2 = f32[8,12,64,256]{3,2,1,0:T(8,128)} fusion(bf16[8,128,12,64]{1,3,2,0:T(8,128)(2,1)S(1)} %bitcast.146, f32[8,12,128]{2,1,0:T(8,128)S(1)} %log_add_fusion, f32[8,12,128,256]{3,2,1,0:T(8,128)} %copy-done, pred[8,128,256]{2,1,0:T(8,128)(4,1)S(1)} %or_and_fusion), kind=kOutput, calls=%fused_computation.16 | convolution fusion | flops 415236096 | bytes 20758528 | tf_op jit(solution)/shard_map/ghij,gihd->gjhd/dot_general | solution.py:266
  175.2 11.5 %multiply_reduce_fusion = (f32[8,12,128]{2,1,0:T(8,128)S(1)}, f32[8,12,128,256]{3,2,1,0:T(8,128)}) fusion(f32[8,12,128]{2,1,0:T(8,128)S(1)} %log_add_fusion, f32[8,12,128,256]{3,2,1,0:T(8,128)} %copy-done, pred[8,128,256]{2,1,0:T(8,128)(4,1)S(1)} %or_and_fusion, bf16[8,128,12,64]{1,3,2,0:T(8,128)(2,1)S(1)} %bitcast.147, ...), kind=kOutput, calls=%fused_computation.6 | convolution fusion | flops 418369536 | bytes 30244864 | tf_op jit(solution)/shard_map/gihd,gjhd->ghij/dot_general | solution.py:272
  186.7 6.6 %copy.43 = f32[8,256,768]{2,1,0:T(8,128)} copy(f32[8,256,768]{1,2,0:T(8,128)} %bitcast.143) | data formatting | bytes 12582912 | tf_op jit(solution)/shard_map/reshape | solution.py:288
  193.4 10.6 %multiply_convert_fusion = bf16[8,12,128,256]{3,2,1,0:T(8,128)(2,1)S(1)} fusion(f32[8,12,128,256]{3,2,1,0:T(8,128)} %get-tuple-element.71, f32[8,12,128]{2,1,0:T(8,128)S(1)} %get-tuple-element.70, f32[8,12,128]{2,1,0:T(8,128)S(1)} %log_add_fusion, f32[8,12,128,256]{3,2,1,0:T(8,128)} %copy-done, pred[8,128,256]{2,1,0:T(8,128)(4,1)S(1)} %or_and_fusion), kind=kLoop, calls=%fused_computation.5 | loop fusion | flops 18874368 | bytes 31817728 | tf_op jit(solution)/shard_map/convert_element_type | solution.py:276
  208.5 6.7 %copy.42 = f32[8,256,768]{2,1,0:T(8,128)} copy(f32[8,256,768]{1,2,0:T(8,128)} %bitcast.140) | data formatting | bytes 12582912 | tf_op jit(solution)/shard_map/reshape | solution.py:287
  237.6 20.9 %collective-permute-start.11 = (f32[8,64,1536]{2,1,0:T(8,128)}, f32[8,64,1536]{2,1,0:T(8,128)}, u32[]{:S(2)}, u32[]{:S(2)}) collective-permute-start(f32[8,64,1536]{2,1,0:T(8,128)} %fusion.52), channel_id=1, source_target_pairs={{0,2},{2,4},{4,6},{6,8},{8,10},{10,12},{12,14},{14,16},{16,18},{18... | collective-permute-start | bytes 9437192 | tf_op jit(solution)/shard_map/ppermute | solution.py:30
  261.4 6.2 %fusion.25 = f32[2,384,2304]{2,1,0:T(8,128)} fusion(bf16[2,384,1024]{2,1,0:T(8,128)(2,1)S(1)} %bitcast.171, bf16[1024,1152]{1,0:T(8,128)(2,1)S(1)} %bitcast.165, bf16[1024,1152]{1,0:T(8,128)(2,1)S(1)} %bitcast.174), kind=kOutput, calls=%fused_computation.44 | convolution fusion | flops 3633315840 | bytes 13369344 | tf_op jit(solution)/shard_map/dot_general | solution.py:85
  269.1 10.2 %maximum_maximum_fusion = f32[2,704,2304]{2,1,0:T(8,128)S(1)} fusion(f32[2,128,768]{2,1,0:T(8,128)} %get-tuple-element.49, f32[2,128,768]{2,1,0:T(8,128)} %get-tuple-element.50, f32[2,128,768]{2,1,0:T(8,128)} %get-tuple-element.48, f32[2,192,768]{2,1,0:T(8,128)S(1)} %get-tuple-element.28, f32[2,192,768]{2,1,0:T(8,128)} %get-tuple-element.29, ...), kind=kLoop, calls=%fused_computation.4 | loop fusion | flops 19464192 | bytes 25952256 | tf_op jit(solution)/shard_map/concatenate | solution.py:319
  279.3 4.6 copy-done.5
  286.9 6.4 %multiply_bitcast_fusion = f32[8,128,12,64]{1,3,2,0:T(8,128)} fusion(bf16[8,256,12,64]{1,3,2,0:T(8,128)(2,1)} %bitcast.142, bf16[8,12,128,256]{3,2,1,0:T(8,128)(2,1)S(1)} %bitcast.137), kind=kOutput, calls=%fused_computation.100 | convolution fusion | flops 403439616 | bytes 12582912 | tf_op jit(solution)/shard_map/ghij,gjhd->gihd/dot_general | solution.py:278
  307.9 5.0 multiply_add_fusion.2
  336.0 10.7 %fusion.50 = (f32[768]{0:T(1024)S(1)}, f32[8,128]{1,0:T(8,128)S(1)}, f32[8,128]{1,0:T(8,128)S(1)}, f32[8,128,768]{2,1,0:T(8,128)}) fusion(bf16[8,128,768]{2,1,0:T(8,128)(2,1)} %param.8, f32[8,128]{1,0:T(8,128)S(1)} %copy-done.58, f32[8,128]{1,0:T(8,128)S(1)} %copy-done.54, f32[768]{0:T(1024)S(1)} %copy-done.56, bf16[384,2304]{1,0:T(8,128)(2,1)} %copy-done.29, ...), kind=kOutput, calls=%fused_computation.87 | convolution fusion | flops 3661034752 | bytes 12998657 | tf_op jit(solution)/shard_map/dot_general | solution.py:91
  351.5 6.8 %fusion.20 = f32[2,384,2304]{2,1,0:T(8,128)S(1)} fusion(bf16[2,384,1024]{2,1,0:T(8,128)(2,1)} %bitcast.167, bf16[1024,768]{1,0:T(8,128)(2,1)} %bitcast.170, bf16[1024,768]{1,0:T(8,128)(2,1)} %copy.51, bf16[1024,768]{1,0:T(8,128)(2,1)} %copy.50), kind=kOutput, calls=%fused_computation.38 | convolution fusion | flops 3638034432 | bytes 13369344 | tf_op jit(solution)/shard_map/dot_general | solution.py:85
  368.3 17.3 %collective-permute-done.47 = f32[2,768]{1,0:T(2,128)S(1)} collective-permute-done((f32[2,768]{1,0:T(2,128)S(1)}, f32[2,768]{1,0:T(2,128)S(1)}, u32[]{:S(2)}, u32[]{:S(2)}) %collective-permute-start.47) | collective-permute-done | bytes 6176 | tf_op jit(solution)/shard_map/ppermute | solution.py:134
  385.6 12.9 %collective-permute-start.48 = (f32[2,768]{1,0:T(2,128)S(1)}, f32[2,768]{1,0:T(2,128)S(1)}, u32[]{:S(2)}, u32[]{:S(2)}) collective-permute-start(f32[2,768]{1,0:T(2,128)S(1)} %add.281), channel_id=1, source_target_pairs={{0,8},{2,10},{4,12},{6,14},{8,0},{10,2},{12,4},{14,6},{16,24},{18,... | collective-permute-start | bytes 18440 | tf_op jit(solution)/shard_map/ppermute | solution.py:134
  405.1 14.5 %collective-permute-done.30 = bf16[1,352,1152]{2,1,0:T(8,128)(2,1)S(1)} collective-permute-done((bf16[1,352,1152]{2,1,0:T(8,128)(2,1)S(1)}, bf16[1,352,1152]{2,1,0:T(8,128)(2,1)S(1)}, u32[]{:S(2)}, u32[]{:S(2)}) %collective-permute-start.30) | collective-permute-done | bytes 811040 | tf_op jit(solution)/shard_map/ppermute | solution.py:133
  421.7 5.8 %collective-permute-done.38 = bf16[1,176,1152]{2,1,0:T(8,128)(2,1)S(1)} collective-permute-done((bf16[1,176,1152]{2,1,0:T(8,128)(2,1)S(1)}, bf16[1,176,1152]{2,1,0:T(8,128)(2,1)S(1)}, u32[]{:S(2)}, u32[]{:S(2)}) %collective-permute-start.38) | collective-permute-done | bytes 405536 | tf_op jit(solution)/shard_map/ppermute | solution.py:133
  430.8 5.0 collective-permute-done.39
  442.5 4.5 collective-permute-done.40
  450.1 5.4 collective-permute-done.41
  465.9 5.7 %collective-permute-done.21 = bf16[2,96,1152]{2,1,0:T(8,128)(2,1)S(1)} collective-permute-done((bf16[2,96,1152]{2,1,0:T(8,128)(2,1)S(1)}, bf16[2,96,1152]{2,1,0:T(8,128)(2,1)S(1)}, u32[]{:S(2)}, u32[]{:S(2)}) %collective-permute-start.21) | collective-permute-done | bytes 442400 | tf_op jit(solution)/shard_map/ppermute | solution.py:134
  473.7 6.5 %collective-permute-done.43 = bf16[176,1152]{1,0:T(8,128)(2,1)S(1)} collective-permute-done((bf16[176,1152]{1,0:T(8,128)(2,1)S(1)}, bf16[176,1152]{1,0:T(8,128)(2,1)S(1)}, u32[]{:S(2)}, u32[]{:S(2)}) %collective-permute-start.43) | collective-permute-done | bytes 405536 | tf_op jit(solution)/shard_map/ppermute | solution.py:134
  480.4 8.5 %collective-permute-done.36 = bf16[176,1152]{1,0:T(8,128)(2,1)S(1)} collective-permute-done((bf16[176,1152]{1,0:T(8,128)(2,1)S(1)}, bf16[176,1152]{1,0:T(8,128)(2,1)S(1)}, u32[]{:S(2)}, u32[]{:S(2)}) %collective-permute-start.36) | collective-permute-done | bytes 405536 | tf_op jit(solution)/shard_map/ppermute | solution.py:134
  527.4 12.4 %maximum_select_fusion.2 = bf16[704,2304]{1,0:T(8,128)(2,1)S(1)} fusion(bf16[352,2304]{1,0:T(8,128)(2,1)S(1)} %collective-permute-done.44, bf16[352,1152]{1,0:T(8,128)(2,1)S(1)} %maximum_select_fusion.10, bf16[352,1152]{1,0:T(8,128)(2,1)S(1)} %maximum_select_fusion.9, pred[]{:T(512)S(6)} %eq.16), kind=kLoop, calls=%fused_computation.80 | loop fusion | flops 21086208 | bytes 6488065 | tf_op jit(solution)/shard_map/jit(_where)/select_n | solution.py:165
  (385 shorter events, 250.7 us)
Async XLA Ops:
  0.7 44.0 %collective-permute-start = (bf16[2,384]{1,0:T(2,128)(2,1)}, bf16[2,384]{1,0:T(2,128)(2,1)S(1)}, u32[]{:S(2)}, u32[]{:S(2)}) collective-permute-start(bf16[2,384]{1,0:T(2,128)(2,1)} %param.14), channel_id=1, source_target_pairs={{0,1},{1,0},{2,3},{3,2},{4,5},{5,4},{6,7},{7,6},{8,9},{9,8},{10,11... | collective-permute-start | bytes 4616 | tf_op jit(solution)/shard_map/ppermute | solution.py:196
  5.4 74.9 %collective-permute-start.5 = (bf16[192,768]{1,0:T(8,128)(2,1)}, bf16[192,768]{1,0:T(8,128)(2,1)}, u32[]{:S(2)}, u32[]{:S(2)}) collective-permute-start(bf16[192,768]{1,0:T(8,128)(2,1)} %constant_dynamic-slice_fusion.20), channel_id=1, source_target_pairs={{0,1},{1,0},{2,3},{3,2},{4,5},{5,4},{6,7},{7,6},{8,9},{9,8},{10,11... | collective-permute-start | bytes 884744 | tf_op jit(solution)/shard_map/ppermute | solution.py:109
  7.3 73.0 %collective-permute-start.9 = (bf16[288,768]{1,0:T(8,128)(2,1)}, bf16[288,768]{1,0:T(8,128)(2,1)}, u32[]{:S(2)}, u32[]{:S(2)}) collective-permute-start(bf16[288,768]{1,0:T(8,128)(2,1)} %constant_dynamic-slice_fusion.18), channel_id=1, source_target_pairs={{0,1},{1,0},{2,3},{3,2},{4,5},{5,4},{6,7},{7,6},{8,9},{9,8},{10,11... | collective-permute-start | bytes 1327112 | tf_op jit(solution)/shard_map/ppermute | solution.py:109
  10.4 33.6 %collective-permute-start.1 = (bf16[192,2304]{1,0:T(8,128)(2,1)S(1)}, bf16[192,2304]{1,0:T(8,128)(2,1)}, u32[]{:S(2)}, u32[]{:S(2)}) collective-permute-start(bf16[192,2304]{1,0:T(8,128)(2,1)S(1)} %constant_dynamic-slice_fusion.21), channel_id=1, source_target_pairs={{0,1},{1,0},{2,3},{3,2},{4,5},{5,4},{6,7},{7,6},{8,9},{9,8},{10,11... | collective-permute-start | bytes 2654216 | tf_op jit(solution)/shard_map/ppermute | solution.py:109
  12.8 64.9 %collective-permute-start.7 = (bf16[192,2304]{1,0:T(8,128)(2,1)}, bf16[192,2304]{1,0:T(8,128)(2,1)}, u32[]{:S(2)}, u32[]{:S(2)}) collective-permute-start(bf16[192,2304]{1,0:T(8,128)(2,1)} %constant_dynamic-slice_fusion.19), channel_id=1, source_target_pairs={{0,1},{1,0},{2,3},{3,2},{4,5},{5,4},{6,7},{7,6},{8,9},{9,8},{10,11... | collective-permute-start | bytes 2654216 | tf_op jit(solution)/shard_map/ppermute | solution.py:109
  73.2 21.3 %collective-permute-start.3 = (bf16[8,64,1536]{2,1,0:T(8,128)(2,1)}, bf16[8,64,1536]{2,1,0:T(8,128)(2,1)}, u32[]{:S(2)}, u32[]{:S(2)}) collective-permute-start(bf16[8,64,1536]{2,1,0:T(8,128)(2,1)} %get-tuple-element.46), channel_id=1, source_target_pairs={{0,2},{2,4},{4,6},{6,8},{8,10},{10,12},{12,14},{14,16},{16,18},{18... | collective-permute-start | bytes 4718600 | tf_op jit(solution)/shard_map/ppermute | solution.py:21
  76.4 18.1 %collective-permute-start.4 = (bf16[8,64,1536]{2,1,0:T(8,128)(2,1)}, bf16[8,64,1536]{2,1,0:T(8,128)(2,1)}, u32[]{:S(2)}, u32[]{:S(2)}) collective-permute-start(bf16[8,64,1536]{2,1,0:T(8,128)(2,1)} %get-tuple-element.47), channel_id=1, source_target_pairs={{2,0},{4,2},{6,4},{8,6},{10,8},{12,10},{14,12},{16,14},{18,16},{20... | collective-permute-start | bytes 4718600 | tf_op jit(solution)/shard_map/ppermute | solution.py:22
  77.7 13.2 %collective-permute-start.8 = (bf16[192,2304]{1,0:T(8,128)(2,1)}, bf16[192,2304]{1,0:T(8,128)(2,1)}, u32[]{:S(2)}, u32[]{:S(2)}) collective-permute-start(bf16[192,2304]{1,0:T(8,128)(2,1)} %collective-permute-done.7), channel_id=1, source_target_pairs={{0,2},{2,0},{4,6},{6,4},{8,10},{10,8},{12,14},{14,12},{16,18},{18,... | collective-permute-start | bytes 2654216 | tf_op jit(solution)/shard_map/ppermute | solution.py:110
  236.2 60.5 %collective-permute-start.12 = (bf16[8,64,1536]{2,1,0:T(8,128)(2,1)}, bf16[8,64,1536]{2,1,0:T(8,128)(2,1)}, u32[]{:S(2)}, u32[]{:S(2)}) collective-permute-start(bf16[8,64,1536]{2,1,0:T(8,128)(2,1)} %fusion.53), channel_id=1, source_target_pairs={{2,0},{4,2},{6,4},{8,6},{10,8},{12,10},{14,12},{16,14},{18,16},{20... | collective-permute-start | bytes 4718600 | tf_op jit(solution)/shard_map/ppermute | solution.py:30
  237.6 59.1 %collective-permute-start.11 = (f32[8,64,1536]{2,1,0:T(8,128)}, f32[8,64,1536]{2,1,0:T(8,128)}, u32[]{:S(2)}, u32[]{:S(2)}) collective-permute-start(f32[8,64,1536]{2,1,0:T(8,128)} %fusion.52), channel_id=1, source_target_pairs={{0,2},{2,4},{4,6},{6,8},{8,10},{10,12},{12,14},{14,16},{16,18},{18... | collective-permute-start | bytes 9437192 | tf_op jit(solution)/shard_map/ppermute | solution.py:30
  286.0 75.7 %collective-permute-start.29 = (bf16[2,352,2304]{2,1,0:T(8,128)(2,1)}, bf16[2,352,2304]{2,1,0:T(8,128)(2,1)}, u32[]{:S(2)}, u32[]{:S(2)}) collective-permute-start(bf16[2,352,2304]{2,1,0:T(8,128)(2,1)} %dynamic-slice_convert_fusion), channel_id=1, source_target_pairs={{0,2},{2,0},{4,6},{6,4},{8,10},{10,8},{12,14},{14,12},{16,18},{18,... | collective-permute-start | bytes 9732104 | tf_op jit(solution)/shard_map/ppermute | solution.py:134
  346.7 13.2 %collective-permute-start.45 = (f32[2,768]{1,0:T(2,128)S(1)}, f32[2,768]{1,0:T(2,128)S(1)}, u32[]{:S(2)}, u32[]{:S(2)}) collective-permute-start(f32[2,768]{1,0:T(2,128)S(1)} %pad_maximum_fusion.9), channel_id=1, source_target_pairs={{0,1},{1,0},{2,3},{3,2},{4,5},{5,4},{6,7},{7,6},{8,9},{9,8},{10,11... | collective-permute-start | bytes 18440 | tf_op jit(solution)/shard_map/ppermute | solution.py:133
  359.9 8.2 %collective-permute-start.46 = (f32[2,768]{1,0:T(2,128)S(1)}, f32[2,768]{1,0:T(2,128)S(1)}, u32[]{:S(2)}, u32[]{:S(2)}) collective-permute-start(f32[2,768]{1,0:T(2,128)S(1)} %fusion.97), channel_id=1, source_target_pairs={{0,2},{2,0},{4,6},{6,4},{8,10},{10,8},{12,14},{14,12},{16,18},{18,... | collective-permute-start | bytes 18440 | tf_op jit(solution)/shard_map/ppermute | solution.py:134
  364.8 38.3 %collective-permute-start.37 = (bf16[2,176,1152]{2,1,0:T(8,128)(2,1)S(1)}, bf16[2,176,1152]{2,1,0:T(8,128)(2,1)S(1)}, u32[]{:S(2)}, u32[]{:S(2)}) collective-permute-start(bf16[2,176,1152]{2,1,0:T(8,128)(2,1)S(1)} %constant_dynamic-slice_fusion.5), channel_id=1, source_target_pairs={{0,4},{2,6},{4,0},{6,2},{8,12},{10,14},{12,8},{14,10},{16,20},{18,... | collective-permute-start | bytes 2433032 | tf_op jit(solution)/shard_map/ppermute | solution.py:134
  368.2 17.4 %collective-permute-start.47 = (f32[2,768]{1,0:T(2,128)S(1)}, f32[2,768]{1,0:T(2,128)S(1)}, u32[]{:S(2)}, u32[]{:S(2)}) collective-permute-start(f32[2,768]{1,0:T(2,128)S(1)} %fusion.132), channel_id=1, source_target_pairs={{0,4},{2,6},{4,0},{6,2},{8,12},{10,14},{12,8},{14,10},{16,20},{18,... | collective-permute-start | bytes 18440 | tf_op jit(solution)/shard_map/ppermute | solution.py:134
  385.6 14.6 %collective-permute-start.48 = (f32[2,768]{1,0:T(2,128)S(1)}, f32[2,768]{1,0:T(2,128)S(1)}, u32[]{:S(2)}, u32[]{:S(2)}) collective-permute-start(f32[2,768]{1,0:T(2,128)S(1)} %add.281), channel_id=1, source_target_pairs={{0,8},{2,10},{4,12},{6,14},{8,0},{10,2},{12,4},{14,6},{16,24},{18,... | collective-permute-start | bytes 18440 | tf_op jit(solution)/shard_map/ppermute | solution.py:134
  398.6 21.0 %collective-permute-start.30 = (bf16[1,352,1152]{2,1,0:T(8,128)(2,1)S(1)}, bf16[1,352,1152]{2,1,0:T(8,128)(2,1)S(1)}, u32[]{:S(2)}, u32[]{:S(2)}) collective-permute-start(bf16[1,352,1152]{2,1,0:T(8,128)(2,1)S(1)} %constant_dynamic-slice_fusion.9), channel_id=1, source_target_pairs={{0,1},{1,0},{2,3},{3,2},{4,5},{5,4},{6,7},{7,6},{8,9},{9,8},{10,11... | collective-permute-start | bytes 2433032 | tf_op jit(solution)/shard_map/ppermute | solution.py:133
  400.2 57.6 %collective-permute-start.13 = (bf16[2,192,2304]{2,1,0:T(8,128)(2,1)S(1)}, bf16[2,192,2304]{2,1,0:T(8,128)(2,1)S(1)}, u32[]{:S(2)}, u32[]{:S(2)}) collective-permute-start(bf16[2,192,2304]{2,1,0:T(8,128)(2,1)S(1)} %copy-done.30), channel_id=1, source_target_pairs={{0,2},{2,0},{4,6},{6,4},{8,10},{10,8},{12,14},{14,12},{16,18},{18,... | collective-permute-start | bytes 5308424 | tf_op jit(solution)/shard_map/ppermute | solution.py:134
  400.2 124.5 %collective-permute-start.49 = (f32[2,768]{1,0:T(2,128)S(1)}, f32[2,768]{1,0:T(2,128)S(1)}, u32[]{:S(2)}, u32[]{:S(2)}) collective-permute-start(f32[2,768]{1,0:T(2,128)S(1)} %add.282), channel_id=1, source_target_pairs={{0,16},{2,18},{4,20},{6,22},{8,24},{10,26},{12,28},{14,30},{16,0},... | collective-permute-start | bytes 18440 | tf_op jit(solution)/shard_map/ppermute | solution.py:134
  403.5 24.1 %collective-permute-start.38 = (bf16[1,176,1152]{2,1,0:T(8,128)(2,1)S(1)}, bf16[1,176,1152]{2,1,0:T(8,128)(2,1)S(1)}, u32[]{:S(2)}, u32[]{:S(2)}) collective-permute-start(bf16[1,176,1152]{2,1,0:T(8,128)(2,1)S(1)} %constant_dynamic-slice_fusion.4), channel_id=1, source_target_pairs={{0,1},{1,0},{2,3},{3,2},{4,5},{5,4},{6,7},{7,6},{8,9},{9,8},{10,11... | collective-permute-start | bytes 1216520 | tf_op jit(solution)/shard_map/ppermute | solution.py:133
  419.8 10.1 %collective-permute-start.31 = (bf16[1,176,1152]{2,1,0:T(8,128)(2,1)S(1)}, bf16[1,176,1152]{2,1,0:T(8,128)(2,1)S(1)}, u32[]{:S(2)}, u32[]{:S(2)}) collective-permute-start(bf16[1,176,1152]{2,1,0:T(8,128)(2,1)S(1)} %constant_dynamic-slice_fusion.8), channel_id=1, source_target_pairs={{0,4},{2,6},{4,0},{6,2},{8,12},{10,14},{12,8},{14,10},{16,20},{18,... | collective-permute-start | bytes 1216520 | tf_op jit(solution)/shard_map/ppermute | solution.py:134
  430.1 9.6 %collective-permute-start.32 = (bf16[1,88,1152]{2,1,0:T(8,128)(2,1)S(1)}, bf16[1,88,1152]{2,1,0:T(8,128)(2,1)S(1)}, u32[]{:S(2)}, u32[]{:S(2)}) collective-permute-start(bf16[1,88,1152]{2,1,0:T(8,128)(2,1)S(1)} %constant_dynamic-slice_fusion.7), channel_id=1, source_target_pairs={{0,8},{2,10},{4,12},{6,14},{8,0},{10,2},{12,4},{14,6},{16,24},{18,... | collective-permute-start | bytes 608264 | tf_op jit(solution)/shard_map/ppermute | solution.py:134
  435.9 11.1 %collective-permute-start.40 = (bf16[1,44,1152]{2,1,0:T(8,128)(2,1)S(1)}, bf16[1,44,1152]{2,1,0:T(8,128)(2,1)S(1)}, u32[]{:S(2)}, u32[]{:S(2)}) collective-permute-start(bf16[1,44,1152]{2,1,0:T(8,128)(2,1)S(1)} %constant_dynamic-slice_fusion.2), channel_id=1, source_target_pairs={{0,16},{2,18},{4,20},{6,22},{8,24},{10,26},{12,28},{14,30},{16,0},... | collective-permute-start | bytes 304136 | tf_op jit(solution)/shard_map/ppermute | solution.py:134
  439.8 9.5 %collective-permute-start.33 = (bf16[1,44,1152]{2,1,0:T(8,128)(2,1)S(1)}, bf16[1,44,1152]{2,1,0:T(8,128)(2,1)S(1)}, u32[]{:S(2)}, u32[]{:S(2)}) collective-permute-start(bf16[1,44,1152]{2,1,0:T(8,128)(2,1)S(1)} %constant_dynamic-slice_fusion.6), channel_id=1, source_target_pairs={{0,16},{2,18},{4,20},{6,22},{8,24},{10,26},{12,28},{14,30},{16,0},... | collective-permute-start | bytes 304136 | tf_op jit(solution)/shard_map/ppermute | solution.py:134
  447.0 8.5 %collective-permute-start.41 = (bf16[44,1152]{1,0:T(8,128)(2,1)S(1)}, bf16[44,1152]{1,0:T(8,128)(2,1)S(1)}, u32[]{:S(2)}, u32[]{:S(2)}) collective-permute-start(bf16[44,1152]{1,0:T(8,128)(2,1)S(1)} %fusion.75), channel_id=1, source_target_pairs={{0,16},{2,18},{4,20},{6,22},{8,24},{10,26},{12,28},{14,30},{16,0},... | collective-permute-start | bytes 304136 | tf_op jit(solution)/shard_map/ppermute | solution.py:134
  458.4 13.1 %collective-permute-start.21 = (bf16[2,96,1152]{2,1,0:T(8,128)(2,1)S(1)}, bf16[2,96,1152]{2,1,0:T(8,128)(2,1)S(1)}, u32[]{:S(2)}, u32[]{:S(2)}) collective-permute-start(bf16[2,96,1152]{2,1,0:T(8,128)(2,1)S(1)} %constant_dynamic-slice_fusion.13), channel_id=1, source_target_pairs={{0,4},{2,6},{4,0},{6,2},{8,12},{10,14},{12,8},{14,10},{16,20},{18,... | collective-permute-start | bytes 1327112 | tf_op jit(solution)/shard_map/ppermute | solution.py:134
  459.2 14.1 %collective-permute-start.14 = (bf16[1,192,1152]{2,1,0:T(8,128)(2,1)S(1)}, bf16[1,192,1152]{2,1,0:T(8,128)(2,1)S(1)}, u32[]{:S(2)}, u32[]{:S(2)}) collective-permute-start(bf16[1,192,1152]{2,1,0:T(8,128)(2,1)S(1)} %constant_dynamic-slice_fusion.17), channel_id=1, source_target_pairs={{0,1},{1,0},{2,3},{3,2},{4,5},{5,4},{6,7},{7,6},{8,9},{9,8},{10,11... | collective-permute-start | bytes 1327112 | tf_op jit(solution)/shard_map/ppermute | solution.py:133
  462.9 17.4 %collective-permute-start.43 = (bf16[176,1152]{1,0:T(8,128)(2,1)S(1)}, bf16[176,1152]{1,0:T(8,128)(2,1)S(1)}, u32[]{:S(2)}, u32[]{:S(2)}) collective-permute-start(bf16[176,1152]{1,0:T(8,128)(2,1)S(1)} %maximum_select_fusion.15), channel_id=1, source_target_pairs={{0,4},{2,6},{4,0},{6,2},{8,12},{10,14},{12,8},{14,10},{16,20},{18,... | collective-permute-start | bytes 1216520 | tf_op jit(solution)/shard_map/ppermute | solution.py:134
  465.8 23.1 %collective-permute-start.36 = (bf16[176,1152]{1,0:T(8,128)(2,1)S(1)}, bf16[176,1152]{1,0:T(8,128)(2,1)S(1)}, u32[]{:S(2)}, u32[]{:S(2)}) collective-permute-start(bf16[176,1152]{1,0:T(8,128)(2,1)S(1)} %maximum_select_fusion.14), channel_id=1, source_target_pairs={{0,4},{2,6},{4,0},{6,2},{8,12},{10,14},{12,8},{14,10},{16,20},{18,... | collective-permute-start | bytes 1216520 | tf_op jit(solution)/shard_map/ppermute | solution.py:134
  471.7 17.7 %collective-permute-start.22 = (bf16[1,96,1152]{2,1,0:T(8,128)(2,1)S(1)}, bf16[1,96,1152]{2,1,0:T(8,128)(2,1)S(1)}, u32[]{:S(2)}, u32[]{:S(2)}) collective-permute-start(bf16[1,96,1152]{2,1,0:T(8,128)(2,1)S(1)} %constant_dynamic-slice_fusion.12), channel_id=1, source_target_pairs={{0,1},{1,0},{2,3},{3,2},{4,5},{5,4},{6,7},{7,6},{8,9},{9,8},{10,11... | collective-permute-start | bytes 663560 | tf_op jit(solution)/shard_map/ppermute | solution.py:133
  473.5 18.8 %collective-permute-start.15 = (bf16[1,96,1152]{2,1,0:T(8,128)(2,1)S(1)}, bf16[1,96,1152]{2,1,0:T(8,128)(2,1)S(1)}, u32[]{:S(2)}, u32[]{:S(2)}) collective-permute-start(bf16[1,96,1152]{2,1,0:T(8,128)(2,1)S(1)} %constant_dynamic-slice_fusion.16), channel_id=1, source_target_pairs={{0,4},{2,6},{4,0},{6,2},{8,12},{10,14},{12,8},{14,10},{16,20},{18,... | collective-permute-start | bytes 663560 | tf_op jit(solution)/shard_map/ppermute | solution.py:134
  489.3 38.2 %collective-permute-start.44 = (bf16[352,2304]{1,0:T(8,128)(2,1)S(1)}, bf16[352,2304]{1,0:T(8,128)(2,1)S(1)}, u32[]{:S(2)}, u32[]{:S(2)}) collective-permute-start(bf16[352,2304]{1,0:T(8,128)(2,1)S(1)} %pad_maximum_fusion.2), channel_id=1, source_target_pairs={{0,2},{2,0},{4,6},{6,4},{8,10},{10,8},{12,14},{14,12},{16,18},{18,... | collective-permute-start | bytes 4866056 | tf_op jit(solution)/shard_map/ppermute | solution.py:134
  (93 other events, 985.3 us)

commit v2 on v1

v2 whole, which is shorter than its diff:
```python
import jax
import jax.numpy as jnp
from jax import lax
from jax.experimental import pallas as pl
from jax.experimental.pallas import tpu as pltpu
from jax.sharding import PartitionSpec as P

HEAD_DIM = 64
HALF_WINDOW = 64
PAIR = 128
HEAD_ROWS = 16
MIB = 1 << 20


masked_score = -1000000000.0
norm_epsilon = 1e-05
root_half = 0.7071067811865476
normal_peak = 0.3989422804014327
f32 = jnp.float32
bf16 = jnp.bfloat16


def passed_along(block, axis, distance):
    devices = range(lax.axis_size(axis))
    route = [(i - distance, i) for i in devices if i - distance in devices]
    return lax.ppermute(block, axis, route)


def norm_parts(values):
    center = values - jnp.mean(values, -1, keepdims=True)
    factor = lax.rsqrt(jnp.mean(center * center, -1, keepdims=True) + norm_epsilon)
    return (center * factor, factor)


def norm_back(grad_normed, normed, factor):
    first = jnp.mean(grad_normed, -1, keepdims=True)
    second = jnp.mean(grad_normed * normed, -1, keepdims=True)
    return factor * (grad_normed - first - normed * second)


def dot(left, right):
    return jnp.dot(left, right, preferred_element_type=f32)


def dot_right(left, right):
    return lax.dot_general(left, right, (((1,), (1,)), ((), ())), preferred_element_type=f32)


def dot_left(left, right):
    return lax.dot_general(left, right, (((0,), (0,)), ((), ())), preferred_element_type=f32)


def half_swap(value, first_half):
    return jnp.where(first_half, pltpu.roll(value, PAIR - 32, 1), pltpu.roll(value, 32, 1))


def place_weight(place_ref, whole, own, far, near):
    rows = own.shape[0]
    half = rows // 2
    index, core = place_ref[0], place_ref[1]
    other = (1 - index) * rows
    whole[pl.ds(pl.multiple_of(index * rows, half), rows), :] = own[...]
    whole[pl.ds(pl.multiple_of(other + core * half, half), half), :] = far[...]
    whole[pl.ds(pl.multiple_of(other + (1 - core) * half, half), half), :] = near[...]


def attend_kernel(
    place_ref, before, own, after, cos_ref, sin_ref, bias_ref, gain_ref, w_own, w_far, w_near,
    h1_ref, q_ref, k_ref, v_ref, mix_ref, lse_ref, weight,
):
    @pl.when(pl.program_id(0) == 0)
    def _():
        place_weight(place_ref, weight, w_own, w_far, w_near)

    width = own.shape[2]
    rows = own.shape[1]
    span = rows + 2 * HALF_WINDOW
    stream = jnp.concatenate([before[0], own[0], after[0]], 0).astype(f32)
    normed, _ = norm_parts(stream)
    hidden = (normed * gain_ref[0:1, :].astype(f32)).astype(bf16)
    h1_ref[0] = hidden[HALF_WINDOW : HALF_WINDOW + rows]
    lane = lax.broadcasted_iota(jnp.int32, (1, PAIR), 1)
    first_half = (lane % HEAD_DIM) < HEAD_DIM // 2
    first_head = lane < HEAD_DIM
    cosine, sine = cos_ref[0], sin_ref[0]
    for start in range(0, 3 * width, 2 * PAIR):
        part = dot(hidden, weight[:, start : start + 2 * PAIR])
        for sub in range(0, 2 * PAIR, PAIR):
            value = part[:, sub : sub + PAIR]
            column = (start + sub) % width
            if start + sub < 2 * width:
                value = value * cosine + half_swap(value, first_half) * sine
            if start + sub < width:
                q_ref[0, :, column : column + PAIR] = (value * HEAD_DIM**-0.5).astype(bf16)
            elif start + sub < 2 * width:
                k_ref[0, :, column : column + PAIR] = value.astype(bf16)
            else:
                v_ref[0, :, column : column + PAIR] = value.astype(bf16)
    bias = bias_ref[0]
    bias = jnp.concatenate([bias, bias], 0)
    log_totals = jnp.zeros((rows, PAIR), f32)
    for pair in range(width // PAIR):
        columns = slice(pair * PAIR, (pair + 1) * PAIR)
        query = q_ref[0, HALF_WINDOW : HALF_WINDOW + rows, columns]
        zero = jnp.zeros_like(query)
        both = jnp.concatenate(
            [jnp.where(first_head, query, zero), jnp.where(first_head, zero, query)], 0
        )
        scores = dot_right(both, k_ref[0, :, columns]) + bias
        top = jnp.max(scores, -1, keepdims=True)
        expo = jnp.exp(scores - top)
        total = jnp.sum(expo, -1, keepdims=True)
        log_total = top + jnp.log(total)
        probs = (expo * (1.0 / total)).astype(bf16)
        mixed = dot(probs, v_ref[0, :, columns])
        mix_ref[0, :, columns] = jnp.where(first_head, mixed[:rows], mixed[rows:]).astype(bf16)
        log_totals = jnp.where(lane == 2 * pair, log_total[:rows], log_totals)
        log_totals = jnp.where(lane == 2 * pair + 1, log_total[rows:], log_totals)
    lse_ref[0] = jnp.transpose(log_totals)[:HEAD_ROWS]


def feed_kernel(
    place_ref, tok_ref, mix_ref, dy_ref, gain_ref,
    out_own, out_far, out_near, in_own, in_far, in_near, down_own, down_far, down_near,
    layer_ref, dx1_ref, do_ref, lo_ref, hi_ref, delta_ref, h2_ref, dup_ref, mid_ref, dmix_ref, gsum_ref,
    w_out, w_in, w_down,
):
    @pl.when(pl.program_id(0) == 0)
    def _():
        place_weight(place_ref, w_out, out_own, out_far, out_near)
        place_weight(place_ref, w_in, in_own, in_far, in_near)
        place_weight(place_ref, w_down, down_own, down_far, down_near)
        gsum_ref[...] = jnp.zeros_like(gsum_ref)

    rows, width = tok_ref.shape
    ffn = w_down.shape[0]
    block = 2 * HALF_WINDOW
    after_attn = tok_ref[...].astype(f32) + dot(mix_ref[...], w_out[...])
    normed, factor = norm_parts(after_attn)
    gain = gain_ref[1:2, :].astype(f32)
    h2_ref[...] = (normed * gain).astype(bf16)
    step = 3 * PAIR
    for start in range(0, ffn, step):
        columns = slice(start, start + step)
        gates = slice(ffn + start, ffn + start + step)
        act_input = dot(h2_ref[...], w_in[:, columns])
        gate_part = dot(h2_ref[...], w_in[:, gates])
        grad_middle = dot_right(dy_ref[...], w_down[columns, :])
        share = 0.5 + 0.5 * lax.erf(act_input * root_half)
        act_value = act_input * share
        slope = share + act_input * (normal_peak * jnp.exp(-0.5 * act_input * act_input))
        mid_ref[:, columns] = (act_value * gate_part).astype(bf16)
        dup_ref[:, columns] = (grad_middle * gate_part * slope).astype(bf16)
        dup_ref[:, gates] = (grad_middle * act_value).astype(bf16)
    layer_ref[...] = (after_attn + dot(mid_ref[...], w_down[...])).astype(bf16)
    grad_hidden = dot_right(dup_ref[...], w_in[...])
    gain_terms = grad_hidden * normed
    gsum_ref[...] += jnp.sum(gain_terms.reshape(rows // 8, 8, width), 0)
    grad_stream = dy_ref[...].astype(f32) + norm_back(grad_hidden * gain, normed, factor)
    dx1_ref[...] = grad_stream
    dmix_ref[...] = grad_stream.astype(bf16)
    grad_mixed = dot_right(dmix_ref[...], w_out[...]).astype(bf16)
    do_ref[...] = grad_mixed
    products = grad_mixed.astype(f32) * mix_ref[...].astype(f32)
    high = products.astype(bf16)
    low = (products - high.astype(f32)).astype(bf16)
    head_of = lax.broadcasted_iota(jnp.int32, (width, PAIR), 0) // HEAD_DIM
    slot = lax.broadcasted_iota(jnp.int32, (width, PAIR), 1)
    pick = jnp.where(head_of == slot, 1.0, 0.0).astype(bf16)
    delta = dot(high, pick) + dot(low, pick)
    for i in range(rows // block):
        piece = grad_mixed[i * block : (i + 1) * block]
        lo_ref[i] = piece[:HALF_WINDOW]
        hi_ref[i] = piece[HALF_WINDOW:]
        delta_ref[i] = jnp.transpose(delta[i * block : (i + 1) * block])[:HEAD_ROWS]


def grads_kernel(h2_ref, dup_ref, mid_ref, dy_ref, mix_ref, dmix_ref, out_ref):
    step = pl.program_id(0)
    width = dy_ref.shape[1]
    half = out_ref.shape[0] // 2
    part = width // 2
    ffn_rows = mid_ref.shape[1]
    ffn_part = 3 * ffn_rows // 2
    grad = dot_left(h2_ref[...], dup_ref[...]).astype(bf16)
    at = pl.multiple_of(step * part, part)
    out_ref[pl.ds(at, part), :] = grad[:part]
    out_ref[pl.ds(half + at, part), :] = grad[part:]
    grad = dot_left(mid_ref[...], dy_ref[...]).astype(bf16)
    third = ffn_rows // 2
    for i in range(2):
        index = 2 * step + i
        owner = index // 3
        at = pl.multiple_of(owner * half + 3 * part + (index - 3 * owner) * third, 64)
        out_ref[pl.ds(at, third), :] = grad[i * third : (i + 1) * third]
    grad = dot_left(mix_ref[...], dmix_ref[...]).astype(bf16)
    columns = pl.ds(pl.multiple_of(step * (width // 3), PAIR), width // 3)
    at = 3 * part + ffn_part
    out_ref[at : at + part, columns] = grad[:part]
    out_ref[half + at : half + at + part, columns] = grad[part:]


def attend_back_kernel(
    q_ref, k_ref, v_ref, do_ref, do_before, do_after, lse_ref, lse_edge, delta_ref, delta_edge,
    bias_ref, bias_edge, cos_ref, sin_ref, out_ref,
):
    rows, width = do_ref.shape[1], do_ref.shape[2]
    inner = slice(HALF_WINDOW, HALF_WINDOW + rows)
    lane = lax.broadcasted_iota(jnp.int32, (1, PAIR), 1)
    first_half = (lane % HEAD_DIM) < HEAD_DIM // 2
    first_head = lane < HEAD_DIM
    top_rows = lax.broadcasted_iota(jnp.int32, (PAIR, 1), 0) < HEAD_DIM
    cosine, sine = cos_ref[0, inner], sin_ref[0, inner]
    bias = jnp.concatenate([bias_ref[0], bias_ref[0]], 1)
    edge = jnp.concatenate([bias_edge[0], bias_edge[0]], 1)

    def split(value):
        zero = jnp.zeros_like(value)
        return jnp.concatenate(
            [jnp.where(first_head, value, zero), jnp.where(first_head, zero, value)], 0
        )

    def row_of(ref, pair):
        return jnp.concatenate(
            [ref[0, 2 * pair : 2 * pair + 1, :], ref[0, 2 * pair + 1 : 2 * pair + 2, :]], 1
        )

    def back(keys, values, query, grad_mixed, offsets, log_total, inner_sum):
        probs = jnp.exp(dot_right(keys, query) + offsets - log_total)
        grad_probs = dot_right(values, grad_mixed)
        return probs.astype(bf16), (probs * (grad_probs - inner_sum)).astype(bf16)

    def rotated_back(value):
        return value * cosine - half_swap(value, first_half) * sine

    for pair in range(width // PAIR):
        columns = slice(pair * PAIR, (pair + 1) * PAIR)
        keys, values = k_ref[0, :, columns], v_ref[0, :, columns]
        query = split(q_ref[0, inner, columns])
        grad_mixed = split(do_ref[0, :, columns])
        probs, grad_scores = back(
            keys, values, query, grad_mixed, bias, row_of(lse_ref, pair), row_of(delta_ref, pair)
        )
        query_edge = split(
            jnp.concatenate(
                [
                    q_ref[0, HALF_WINDOW + rows :, columns],
                    q_ref[0, :HALF_WINDOW, columns],
                ],
                0,
            )
        )
        grad_edge = split(jnp.concatenate([do_after[0, :, columns], do_before[0, :, columns]], 0))
        probs_edge, scores_edge = back(
            keys[inner], values[inner], query_edge, grad_edge, edge,
            row_of(lse_edge, pair), row_of(delta_edge, pair),
        )
        grad_values = dot(
            jnp.concatenate([probs[inner], probs_edge], 1),
            jnp.concatenate([grad_mixed, grad_edge], 0),
        )
        grad_keys = dot(
            jnp.concatenate([grad_scores[inner], scores_edge], 1),
            jnp.concatenate([query, query_edge], 0),
        )
        grad_query = dot_left(grad_scores, keys)
        grad_query = jnp.where(first_head, grad_query[:rows], grad_query[rows:]) * HEAD_DIM**-0.5
        out_ref[0, :, columns] = rotated_back(grad_query).astype(bf16)
        out_ref[0, :, width + pair * PAIR : width + (pair + 1) * PAIR] = rotated_back(
            grad_keys
        ).astype(bf16)
        out_ref[0, :, 2 * width + pair * PAIR : 2 * width + (pair + 1) * PAIR] = (
            grad_values.astype(bf16)
        )


def grad_qkv_kernel(h1_ref, dqkv_ref, out_ref):
    out_ref[...] = dot_left(h1_ref[...], dqkv_ref[...]).astype(bf16)


def stream_back_kernel(
    place_ref, dqkv_ref, tok_ref, dx1_ref, gain_ref, w_own, w_far, w_near, out_ref, gsum_ref, weight
):
    @pl.when(pl.program_id(0) == 0)
    def _():
        place_weight(place_ref, weight, w_own, w_far, w_near)
        gsum_ref[...] = jnp.zeros_like(gsum_ref)

    rows, width = tok_ref.shape
    grad_hidden = dot_right(dqkv_ref[...], weight[...])
    normed, factor = norm_parts(tok_ref[...].astype(f32))
    gsum_ref[...] += jnp.sum((grad_hidden * normed).reshape(rows // 8, 8, width), 0)
    grad_normed = grad_hidden * gain_ref[0:1, :].astype(f32)
    out_ref[...] = (dx1_ref[...] + norm_back(grad_normed, normed, factor)).astype(bf16)


def shape_of(*dims, dtype=bf16):
    return jax.ShapeDtypeStruct(dims, dtype)


def whole_spec(array):
    return pl.BlockSpec(array.shape, lambda i: (0,) * array.ndim)


def run(kernel, grid, inputs, outputs, scratch=(), flops=0, whole=()):
    def spec(block, place):
        return pl.BlockSpec(block, place)

    specs = []
    for item in inputs:
        if item[1] is None and item[0].dtype == jnp.int32:
            specs.append(pl.BlockSpec(memory_space=pltpu.SMEM))
        elif item[1] is None:
            specs.append(whole_spec(item[0]))
        else:
            specs.append(spec(item[1], item[2]))
    out_specs = [whole_spec(o[0]) if o[1] is None else spec(o[1], o[2]) for o in outputs]
    moved = sum(x[0].size * x[0].dtype.itemsize for x in list(inputs) + list(outputs))
    return pl.pallas_call(
        kernel,
        grid=(grid,),
        in_specs=specs,
        out_specs=out_specs,
        out_shape=[o[0] for o in outputs],
        scratch_shapes=list(scratch),
        cost_estimate=pl.CostEstimate(flops=flops, bytes_accessed=moved, transcendentals=0),
        compiler_params=pltpu.CompilerParams(
            dimension_semantics=("arbitrary",), vmem_limit_bytes=56 * MIB
        ),
    )(*[x[0] for x in inputs])


def flip_route(size, bit):
    return [(i, i ^ bit) for i in range(size)]


def fetch_shards(shards):
    core = lax.axis_index("seq") % 2
    seq = lax.axis_size("seq")
    pieces = []
    for shard in shards:
        half = shard.shape[0] // 2
        mine = lax.dynamic_slice_in_dim(shard, core * half, half, 0)
        far = lax.ppermute(mine, "fsdp", flip_route(2, 1))
        near = lax.ppermute(far, "seq", flip_route(seq, 1))
        pieces.append((shard, far, near))
    return pieces


def keep_and_send(block, bit, dim):
    half = block.shape[dim] // 2
    keep = lax.dynamic_slice_in_dim(block, bit * half, half, dim)
    send = lax.dynamic_slice_in_dim(block, (1 - bit) * half, half, dim)
    return keep, send


def exchange(block, stage):
    if stage < 0:
        return lax.ppermute(block, "fsdp", flip_route(2, 1))
    return lax.ppermute(block, "seq", flip_route(lax.axis_size("seq"), 1 << stage))


def stage_bit(stage):
    if stage < 0:
        return lax.axis_index("fsdp")
    return (lax.axis_index("seq") >> stage) & 1


def reduce_stage(block, stage):
    keep, send = keep_and_send(block, stage_bit(stage), 0 if stage < 0 else 1)
    got = exchange(send.astype(jnp.bfloat16), stage)
    return (keep.astype(jnp.float32) + got.astype(jnp.float32)).astype(jnp.bfloat16)


def summed_half(bundle):
    stages = (lax.axis_size("seq") - 1).bit_length()
    width = bundle.shape[2] // 2
    bundle = jnp.pad(bundle, ((0, 0), (0, -bundle.shape[1] % lax.axis_size("seq")), (0, 0)))
    bundle = reduce_stage(bundle, 0)
    parts = [bundle[:, :, :width], bundle[:, :, width:]]
    orders = [[-1] + list(range(1, stages)), [1, -1] + list(range(2, stages))]
    for step in range(stages):
        parts = [reduce_stage(part, order[step]) for part, order in zip(parts, orders)]
    parts = [part[0] for part in parts]
    for stage in reversed(range(stages)):
        if stage == 0:
            parts = [jnp.concatenate(parts, 1)]
        bit = stage_bit(stage)
        got = [exchange(part, stage) for part in parts]
        parts = [
            jnp.where(bit == 0, jnp.concatenate([p, g], 0), jnp.concatenate([g, p], 0))
            for p, g in zip(parts, got)
        ]
    return parts[0]


def summed_small(value):
    stages = (lax.axis_size("seq") - 1).bit_length()
    for stage in range(-1, stages):
        value = value + exchange(value, stage)
    return value


def window_tables(pos, rows, head_width):
    half = head_width // 2
    freqs = 10000.0 ** (-(jnp.arange(half, dtype=f32) * 2.0 / head_width))
    angle = pos.astype(f32)[..., None] * freqs
    cosine, sine = jnp.cos(angle), jnp.sin(angle)
    cosine = jnp.concatenate([cosine] * 4, -1)
    sine = jnp.concatenate([-sine, sine, -sine, sine], -1)
    span = pos.shape[1]
    index = jnp.arange(span, dtype=jnp.int32)

    def offsets(query_pos, query_index, key_pos, key_index):
        gap = key_index - query_index
        allowed = (
            (jnp.abs(gap) <= HALF_WINDOW)
            & (key_pos >= 0)
            & (query_pos >= 0)
            & ((gap > 0) | (query_pos >= -gap))
            & ((gap <= 0) | (key_pos >= gap))
        )
        return jnp.where(allowed, 0.0, masked_score).astype(f32)

    inner = slice(HALF_WINDOW, HALF_WINDOW + rows)
    outer_pos = jnp.concatenate([pos[:, HALF_WINDOW + rows :], pos[:, :HALF_WINDOW]], 1)
    outer_index = jnp.concatenate([index[HALF_WINDOW + rows :], index[:HALF_WINDOW]])
    bias = offsets(
        pos[:, inner, None], index[None, inner, None], pos[:, None, :], index[None, None, :]
    )
    bias_t = offsets(
        pos[:, None, inner], index[None, None, inner], pos[:, :, None], index[None, :, None]
    )
    bias_edge = offsets(
        outer_pos[:, None, :],
        outer_index[None, None, :],
        pos[:, inner, None],
        index[None, inner, None],
    )
    return cosine, sine, bias, bias_t, bias_edge


def local(tokens, positions, qkv_weight, out_weight, in_weight, down_weight, norm_gains, cotangent):
    num_seqs, rows, width = tokens.shape
    span = rows + 2 * HALF_WINDOW
    count = num_seqs * rows
    ffn = 2 * down_weight.shape[0]
    seq_index, own_y = lax.axis_index("seq"), lax.axis_index("fsdp")
    place = jnp.stack([own_y, seq_index % 2]).astype(jnp.int32)
    tok_before = passed_along(tokens[:, rows - HALF_WINDOW :], "seq", 1)
    tok_after = passed_along(tokens[:, :HALF_WINDOW], "seq", -1)
    gains_other = lax.ppermute(norm_gains, "fsdp", flip_route(2, 1))
    gains = jnp.where(
        own_y == 0,
        jnp.concatenate([norm_gains, gains_other], 1),
        jnp.concatenate([gains_other, norm_gains], 1),
    )
    w_qkv, w_out, w_in, w_down = fetch_shards([qkv_weight, out_weight, in_weight, down_weight])
    padded_pos = jnp.pad(positions, ((0, 0), (HALF_WINDOW, HALF_WINDOW)), constant_values=-1)
    key_pos = lax.dynamic_slice_in_dim(padded_pos, seq_index * rows, span, 1)
    cosine, sine, bias, bias_t, bias_edge = window_tables(key_pos, rows, HEAD_DIM)

    def per_seq(i):
        return (i, 0, 0)

    def row_block(i):
        return (i, 0)

    def column_block(i):
        return (0, i)

    qkv_pieces = [(piece, None) for piece in w_qkv]
    wide = (1, span, width)
    hidden_one, query, keys, values, mixed, log_total = run(
        attend_kernel,
        num_seqs,
        [
            (place, None),
            (tok_before, (1, HALF_WINDOW, width), per_seq),
            (tokens, (1, rows, width), per_seq),
            (tok_after, (1, HALF_WINDOW, width), per_seq),
            (cosine, (1, span, PAIR), per_seq),
            (sine, (1, span, PAIR), per_seq),
            (bias, (1, rows, span), per_seq),
            (gains, None),
            *qkv_pieces,
        ],
        [
            (shape_of(num_seqs, rows, width), (1, rows, width), per_seq),
            (shape_of(num_seqs, span, width), wide, per_seq),
            (shape_of(num_seqs, span, width), wide, per_seq),
            (shape_of(num_seqs, span, width), wide, per_seq),
            (shape_of(num_seqs, rows, width), (1, rows, width), per_seq),
            (shape_of(num_seqs, HEAD_ROWS, PAIR, dtype=f32), (1, HEAD_ROWS, PAIR), per_seq),
        ],
        [pltpu.VMEM((width, 3 * width), bf16)],
        flops=2 * num_seqs * span * width * 3 * width,
    )
    lse_before = passed_along(log_total, "seq", 1)
    lse_after = passed_along(log_total, "seq", -1)

    flat_tokens = tokens.reshape(count, width)
    flat_dy = cotangent.reshape(count, width)
    flat_mixed = mixed.reshape(count, width)
    step = 2 * rows
    tok_block = (step, width)
    half_block = (2, HALF_WINDOW, width)
    (
        layer_out, grad_stream, grad_mixed, grad_lo, grad_hi, inner_sum,
        hidden_two, grad_up, middle, grad_attn, gain_sum_two,
    ) = run(
        feed_kernel,
        count // step,
        [
            (place, None),
            (flat_tokens, tok_block, row_block),
            (flat_mixed, tok_block, row_block),
            (flat_dy, tok_block, row_block),
            (gains, None),
            *[(piece, None) for piece in (*w_out, *w_in, *w_down)],
        ],
        [
            (shape_of(count, width), tok_block, row_block),
            (shape_of(count, width, dtype=f32), tok_block, row_block),
            (shape_of(count, width), tok_block, row_block),
            (shape_of(num_seqs, HALF_WINDOW, width), half_block, per_seq),
            (shape_of(num_seqs, HALF_WINDOW, width), half_block, per_seq),
            (shape_of(num_seqs, HEAD_ROWS, PAIR, dtype=f32), (2, HEAD_ROWS, PAIR), per_seq),
            (shape_of(count, width), tok_block, row_block),
            (shape_of(count, 2 * ffn), (step, 2 * ffn), row_block),
            (shape_of(count, ffn), (step, ffn), row_block),
            (shape_of(count, width), tok_block, row_block),
            (shape_of(8, width, dtype=f32), None),
        ],
        [
            pltpu.VMEM((width, width), bf16),
            pltpu.VMEM((width, 2 * ffn), bf16),
            pltpu.VMEM((ffn, width), bf16),
        ],
        flops=2 * count * width * (2 * width + 4 * ffn + 2 * ffn),
    )
    do_before = passed_along(grad_hi, "seq", 1)
    do_after = passed_along(grad_lo, "seq", -1)
    sum_before = passed_along(inner_sum, "seq", 1)
    sum_after = passed_along(inner_sum, "seq", -1)

    bundle_rows = 2 * (3 * width // 2 + ffn // 2 + width // 2)
    (bundle,) = run(
        grads_kernel,
        3,
        [
            (hidden_two, None),
            (grad_up, (count, 2 * ffn // 3), column_block),
            (middle, (count, ffn // 3), column_block),
            (flat_dy, None),
            (flat_mixed, None),
            (grad_attn, (count, width // 3), column_block),
        ],
        [(shape_of(bundle_rows, width), None)],
        flops=2 * count * width * (3 * ffn + width),
    )
    bundle_sum = summed_half(bundle.reshape(2, bundle_rows // 2, width))

    after_lane = (jnp.arange(PAIR) < HALF_WINDOW)[None, None]
    lse_edge = jnp.where(after_lane, lse_after, lse_before)
    sum_edge = jnp.where(after_lane, sum_after, sum_before)
    half = (1, HALF_WINDOW, width)
    heads = (1, HEAD_ROWS, PAIR)
    (grad_qkv_all,) = run(
        attend_back_kernel,
        num_seqs,
        [
            (query, wide, per_seq),
            (keys, wide, per_seq),
            (values, wide, per_seq),
            (grad_mixed.reshape(num_seqs, rows, width), (1, rows, width), per_seq),
            (do_before, half, per_seq),
            (do_after, half, per_seq),
            (log_total, heads, per_seq),
            (lse_edge, heads, per_seq),
            (inner_sum, heads, per_seq),
            (sum_edge, heads, per_seq),
            (bias_t, (1, span, rows), per_seq),
            (bias_edge, (1, rows, PAIR), per_seq),
            (cosine, (1, span, PAIR), per_seq),
            (sine, (1, span, PAIR), per_seq),
        ],
        [(shape_of(num_seqs, rows, 3 * width), (1, rows, 3 * width), per_seq)],
        flops=2 * num_seqs * (width // PAIR) * 7 * 256 * 256 * 128,
    )
    flat_grad = grad_qkv_all.reshape(count, 3 * width)
    (grad_qkv,) = run(
        grad_qkv_kernel,
        3,
        [
            (hidden_one.reshape(count, width), None),
            (flat_grad, (count, width), column_block),
        ],
        [(shape_of(width, 3 * width), (width, width), column_block)],
        flops=2 * count * width * 3 * width,
    )
    qkv_sum = summed_half(grad_qkv.reshape(2, width // 2, 3 * width))
    grad_tokens, gain_sum_one = run(
        stream_back_kernel,
        count // step,
        [
            (place, None),
            (flat_grad, (step, 3 * width), row_block),
            (flat_tokens, tok_block, row_block),
            (grad_stream, tok_block, row_block),
            (gains, None),
            *qkv_pieces,
        ],
        [
            (shape_of(count, width), tok_block, row_block),
            (shape_of(8, width, dtype=f32), None),
        ],
        [pltpu.VMEM((width, 3 * width), bf16)],
        flops=2 * count * width * 3 * width,
    )
    gain_sums = summed_small(jnp.stack([jnp.sum(gain_sum_one, 0), jnp.sum(gain_sum_two, 0)]))
    gain_width = norm_gains.shape[1]
    part = in_weight.shape[0]
    in_sum = jnp.concatenate([bundle_sum[i * part : (i + 1) * part] for i in range(3)], 1)
    down_rows = down_weight.shape[0]
    down_sum = bundle_sum[3 * part : 3 * part + down_rows]
    out_sum = bundle_sum[3 * part + down_rows : 4 * part + down_rows]
    return (
        layer_out.reshape(tokens.shape),
        grad_tokens.reshape(tokens.shape),
        qkv_sum.astype(f32),
        out_sum.astype(f32),
        in_sum.astype(f32),
        down_sum.astype(f32),
        lax.dynamic_slice_in_dim(gain_sums, own_y * gain_width, gain_width, 1),
    )


def solution(mesh):
    in_specs = (
        P("fsdp", "seq", None),
        P("fsdp", None),
        P("fsdp", None),
        P("fsdp", None),
        P("fsdp", None),
        P("fsdp", None),
        P(None, "fsdp"),
        P("fsdp", "seq", None),
    )
    out_specs = (
        P("fsdp", "seq", None),
        P("fsdp", "seq", None),
        P("fsdp", None),
        P("fsdp", None),
        P("fsdp", None),
        P("fsdp", None),
        P(None, "fsdp"),
    )
    return jax.shard_map(local, mesh=mesh, in_specs=in_specs, out_specs=out_specs, check_vma=False)
```

time: 553 us -> 350 us (0.63)
  matrix products: 108 us -> 0 us
  Pallas kernels: 0 us -> 105 us
  local copies, waits for them, and re-layouts: 111 us -> 13.1 us
  other arithmetic: 102 us -> 43.6 us
  waiting for transfers between devices: 132 us -> 110 us
  starting transfers between devices: 88.7 us -> 70.7 us
    dot_general x18 -> x0, matrix products: 108 us -> none  [the longest x4 36.6 us: through_weight(): lax.dot_general(grads, weight, (((grads.ndim - 1,), (1,)), ((), ())), pre...]
    pallas_call x0 -> x6, Pallas kernels: none -> 105 us  [run(): pl.pallas_call(kernel, grid=(grid,), in_specs=specs, out_specs=out_specs,...]
    slice x14 -> x5, local copies, waits for them, and re-layouts: 34.1 us -> 1.47 us  [the longest x1 1.24 us: local(): tok_after = passed_along(tokens[:, :HALF_WINDOW], 'seq', -1)]
    ppermute x32, waiting for transfers between devices: 81.4 us -> 51.8 us  [exchange(): lax.ppermute(block, 'seq', flip_route(lax.axis_size('seq'), 1 << stage))]
    unnamed x153 -> x34, local copies, waits for them, and re-layouts: 25.3 us -> 4.54 us
    reshape x4 -> x0, local copies, waits for them, and re-layouts: 18.5 us -> none  [the longest x1 6.71 us: local(): grad_keys.reshape(num_seqs, span, model_width)]
    concatenate x5 -> x2, other arithmetic: 19.1 us -> 3.1 us  [the longest x1 3.02 us: window_tables(): cosine = jnp.concatenate([cosine] * 4, -1)]
    convert_element_type x11 -> x4, other arithmetic: 22.8 us -> 6.97 us  [the longest x1 3.61 us: local(): qkv_sum.astype(f32)]
  transfers between devices with their start and end apart: 50 -> 54, of which waited for: 27 -> 27; matrix products, arithmetic and copies ran while one was open for 28% -> 9% of each run, Pallas kernels for 0% -> 15%
where the time goes in v2:
time: 350 us; the launch traced here: 344 us
  waiting for transfers between devices  110 us (31%)
  Pallas kernels  105 us (30%)
  starting transfers between devices  70.7 us (20%)
  other arithmetic  43.6 us (12%)
  local copies, waits for them, and re-layouts  13.1 us (4%)
    pallas_call x6, Pallas kernels, run(): pl.pallas_call(kernel, grid=(grid,), in_specs=specs, out_specs=out_specs,...  105 us
    ppermute x32, waiting for transfers between devices, exchange(): lax.ppermute(block, 'seq', flip_route(lax.axis_size('seq'), 1 << stage))  51.8 us
    ppermute x32, starting transfers between devices, exchange(): lax.ppermute(block, 'seq', flip_route(lax.axis_size('seq'), 1 << stage))  41 us
    ppermute x4, waiting for transfers between devices, fetch_shards(): far = lax.ppermute(mine, 'fsdp', flip_route(2, 1))  34 us
    ppermute x8, starting transfers between devices, passed_along(): return lax.ppermute(block, axis, route)  19.5 us
    ppermute x5, waiting for transfers between devices, exchange(): return lax.ppermute(block, 'fsdp', flip_route(2, 1))  14.8 us
    select_n x13, other arithmetic, summed_half(): jnp.where(bit == 0, jnp.concatenate([p, g], 0), jnp.concatenate([g, p], 0))  13.8 us
    ppermute x8, waiting for transfers between devices, passed_along(): return lax.ppermute(block, axis, route)  9.63 us
  transfers between devices with their start and end apart: 54, of which 27 were waited for; matrix products, arithmetic and copies ran while one was open for 9% of the time, Pallas kernels for 15%

profile of v2, /device:TPU:0, one launch (start us, length us, event | category | flops | bytes accessed | tf_op | source)
XLA Modules:
  0.0 344.1 jit_solution(974781676291470656)
XLA Ops:
  0.6 3.0 collective-permute-start.2
  13.1 3.7 %fusion.1 = (f32[8,256,32]{2,1,0:T(8,128)S(1)}, f32[8,256,32]{2,1,0:T(8,128)S(1)}, f32[8,256,32]{2,1,0:T(8,128)S(1)}) fusion(f32[32]{0:T(128)S(1)} %negate_power_fusion, f32[8,256]{1,0:T(8,128)S(1)} %convert_element_type.177), kind=kLoop, calls=%fused_computation.33 | loop fusion | flops 131072 | bytes 794752 | tf_op jit(solution)/shard_map/neg | solution.py:410
  16.8 3.0 pad_maximum_fusion.1
  19.8 14.0 %collective-permute-done.3.w_far = bf16[192,2304]{1,0:T(8,128)(2,1)} collective-permute-done((bf16[192,2304]{1,0:T(8,128)(2,1)S(1)}, bf16[192,2304]{1,0:T(8,128)(2,1)}, u32[]{:S(2)}, u32[]{:S(2)}) %collective-permute-start.3) | collective-permute-done | bytes 884768 | tf_op jit(solution)/shard_map/ppermute | solution.py:344
  34.0 3.8 %collective-permute-start = (bf16[8,64,768]{2,1,0:T(8,128)(2,1)S(1)}, bf16[8,64,768]{2,1,0:T(8,128)(2,1)}, u32[]{:S(2)}, u32[]{:S(2)}) collective-permute-start(bf16[8,64,768]{2,1,0:T(8,128)(2,1)S(1)} %copy-done.3), channel_id=1, source_target_pairs={{0,2},{2,4},{4,6},{6,8},{8,10},{10,12},{12,14},{14,16},{16,18},{18... | collective-permute-start | bytes 2359304 | tf_op jit(solution)/shard_map/ppermute | solution.py:26
  39.5 13.3 %collective-permute-done.7.in_far = bf16[192,2304]{1,0:T(8,128)(2,1)} collective-permute-done((bf16[192,2304]{1,0:T(8,128)(2,1)S(1)}, bf16[192,2304]{1,0:T(8,128)(2,1)}, u32[]{:S(2)}, u32[]{:S(2)}) %collective-permute-start.7) | collective-permute-done | bytes 884768 | tf_op jit(solution)/shard_map/ppermute | solution.py:344
  54.1 6.7 %collective-permute-done.9.down_far = bf16[288,768]{1,0:T(8,128)(2,1)S(1)} collective-permute-done((bf16[288,768]{1,0:T(8,128)(2,1)S(1)}, bf16[288,768]{1,0:T(8,128)(2,1)S(1)}, u32[]{:S(2)}, u32[]{:S(2)}) %collective-permute-start.9) | collective-permute-done | bytes 442400 | tf_op jit(solution)/shard_map/ppermute | solution.py:344
  61.2 26.4 %shard_map.135 = (bf16[8,128,768]{2,1,0:T(8,128)(2,1)}, bf16[8,256,768]{2,1,0:T(8,128)(2,1)}, bf16[8,256,768]{2,1,0:T(8,128)(2,1)}, bf16[8,256,768]{2,1,0:T(8,12...) custom-call(s32[2]{0:T(128)} %pad_add_fusion.1.place_ref, bf16[8,64,768]{2,1,0:T(8,128)(2,1)} %collective-permute-done.before, ...), custom_call_target="tpu_custom_call" | custom-call | flops 7247757312 | bytes 22481928 | tf_op jit(solution)/shard_map/pallas_call | solution.py:319
  88.9 27.1 %shard_map.136 = (bf16[1024,768]{1,0:T(8,128)(2,1)}, f32[1024,768]{1,0:T(8,128)}, bf16[1024,768]{1,0:T(8,128)(2,1)}, bf16[8,64,768]{2,1,0:T(8,128)(2,1)}, bf16[8...) custom-call(s32[2]{0:T(128)} %pad_add_fusion.1.place_ref, ...), custom_call_target="tpu_custom_call" | custom-call | flops 13287555072 | bytes 29387784 | tf_op jit(solution)/shard_map/pallas_call | solution.py:319
  119.5 4.0 %collective-permute-start.14 = (f32[8,16,128]{2,1,0:T(8,128)S(1)}, f32[8,16,128]{2,1,0:T(8,128)S(1)}, u32[]{:S(2)}, u32[]{:S(2)}) collective-permute-start(f32[8,16,128]{2,1,0:T(8,128)S(1)} %copy-done.9), channel_id=1, source_target_pairs={{0,2},{2,4},{4,6},{6,8},{8,10},{10,12},{12,14},{14,16},{16,18},{18... | collective-permute-start | bytes 196616 | tf_op jit(solution)/shard_map/ppermute | solution.py:26
  126.0 4.3 %collective-permute-start.16 = (f32[8,16,128]{2,1,0:T(8,128)}, f32[8,16,128]{2,1,0:T(8,128)S(1)}, u32[]{:S(2)}, u32[]{:S(2)}) collective-permute-start(f32[8,16,128]{2,1,0:T(8,128)} %get-tuple-element.35.delta_ref), channel_id=1, source_target_pairs={{0,2},{2,4},{4,6},{6,8},{8,10},{10,12},{12,14},{14,16},{16,18},{18... | collective-permute-start | bytes 196616 | tf_op jit(solution)/shard_map/ppermute | solution.py:26
  131.8 9.6 %collective-permute-done.15 = f32[8,16,128]{2,1,0:T(8,128)S(1)} collective-permute-done((f32[8,16,128]{2,1,0:T(8,128)}, f32[8,16,128]{2,1,0:T(8,128)S(1)}, u32[]{:S(2)}, u32[]{:S(2)}) %collective-permute-start.15) | collective-permute-done | bytes 65568 | tf_op jit(solution)/shard_map/ppermute | solution.py:26
  143.3 19.7 %shard_map.137 = bf16[8,128,2304]{2,1,0:T(8,128)(2,1)} custom-call(bf16[8,256,768]{2,1,0:T(8,128)(2,1)} %get-tuple-element.28.q_ref, bf16[8,256,768]{2,1,0:T(8,128)(2,1)} %get-tuple-element.29.k_ref, bf16[8,256,768]{2,1,0:T(8,128)(2,1)} %get-tuple-element.30.v_ref, bf16[8,128,768]{2,1,0:T(8,128)(2,1)} %bitcast.28, bf16[8,64,768]{2,1,0:T(8,128)(2,1)} %copy-done.4, ...), custom_call_target="tpu_custom_call" | custom-call | flops 5637144576 | bytes 21233664 | tf_op jit(solution)/shard_map/pallas_call | solution.py:319
  163.0 7.6 %shard_map.139 = bf16[768,2304]{1,0:T(8,128)(2,1)} custom-call(bf16[1024,768]{1,0:T(8,128)(2,1)} %bitcast.34, bf16[1024,2304]{1,0:T(8,128)(2,1)} %bitcast.22), custom_call_target="tpu_custom_call" | custom-call | flops 3623878656 | bytes 9830400 | tf_op jit(solution)/shard_map/pallas_call | solution.py:319
  172.3 3.7 %collective-permute-start.17 = (bf16[2,192,2304]{2,1,0:T(8,128)(2,1)S(1)}, bf16[2,192,2304]{2,1,0:T(8,128)(2,1)S(1)}, u32[]{:S(2)}, u32[]{:S(2)}) collective-permute-start(bf16[2,192,2304]{2,1,0:T(8,128)(2,1)S(1)} %constant_dynamic-slice_fusion.19), channel_id=1, source_target_pairs={{0,2},{2,0},{4,6},{6,4},{8,10},{10,8},{12,14},{14,12},{16,18},{18,... | collective-permute-start | bytes 5308424 | tf_op jit(solution)/shard_map/ppermute | solution.py:360
  176.0 14.1 %shard_map.140 = bf16[4224,768]{1,0:T(8,128)(2,1)} custom-call(bf16[1024,768]{1,0:T(8,128)(2,1)} %get-tuple-element.39.h2_ref, bf16[1024,2304]{1,0:T(8,128)(2,1)} %get-tuple-element.40.dup_ref, bf16[1024,1152]{1,0:T(8,128)(2,1)} %get-tuple-element.41.mid_ref, bf16[1024,768]{1,0:T(8,128)(2,1)} %bitcast.30, bf16[1024,768]{1,0:T(8,128)(2,1)} %bitcast.33, ...), custom_call_target="tpu_custom_call" | custom-call | flops 6643777536 | bytes 19857408 | tf_op jit(solution)/shard_map/pallas_call | solution.py:319
  195.6 7.4 %collective-permute-done.25 = bf16[2,96,1152]{2,1,0:T(8,128)(2,1)S(1)} collective-permute-done((bf16[2,96,1152]{2,1,0:T(8,128)(2,1)S(1)}, bf16[2,96,1152]{2,1,0:T(8,128)(2,1)S(1)}, u32[]{:S(2)}, u32[]{:S(2)}) %collective-permute-start.25) | collective-permute-done | bytes 442400 | tf_op jit(solution)/shard_map/ppermute | solution.py:360
  203.7 4.4 %collective-permute-done.18 = bf16[1,192,1152]{2,1,0:T(8,128)(2,1)S(1)} collective-permute-done((bf16[1,192,1152]{2,1,0:T(8,128)(2,1)S(1)}, bf16[1,192,1152]{2,1,0:T(8,128)(2,1)S(1)}, u32[]{:S(2)}, u32[]{:S(2)}) %collective-permute-start.18) | collective-permute-done | bytes 442400 | tf_op jit(solution)/shard_map/ppermute | solution.py:359
  208.7 3.6 %collective-permute-done.26 = bf16[1,96,1152]{2,1,0:T(8,128)(2,1)S(1)} collective-permute-done((bf16[1,96,1152]{2,1,0:T(8,128)(2,1)S(1)}, bf16[1,96,1152]{2,1,0:T(8,128)(2,1)S(1)}, u32[]{:S(2)}, u32[]{:S(2)}) %collective-permute-start.26) | collective-permute-done | bytes 221216 | tf_op jit(solution)/shard_map/ppermute | solution.py:359
  216.6 3.7 %add_convert_fusion = bf16[2,1056,768]{2,1,0:T(8,128)(2,1)S(1)} fusion(bf16[2,1056,768]{2,1,0:T(8,128)(2,1)} %collective-permute-done.33, bf16[2,2112,768]{2,1,0:T(8,128)(2,1)} %bitcast.20, s32[]{:T(128)S(6)} %select_n.246), kind=kLoop, calls=%fused_computation | loop fusion | flops 6488064 | bytes 9732100 | tf_op jit(solution)/shard_map/convert_element_type | solution.py:372
  232.7 3.0 collective-permute-done.22
  235.8 3.1 collective-permute-done.41
  242.4 5.2 %collective-permute-done.42 = bf16[1,528,384]{2,1,0:T(8,128)(2,1)S(1)} collective-permute-done((bf16[1,528,384]{2,1,0:T(8,128)(2,1)S(1)}, bf16[1,528,384]{2,1,0:T(8,128)(2,1)S(1)}, u32[]{:S(2)}, u32[]{:S(2)}) %collective-permute-start.42) | collective-permute-done | bytes 405536 | tf_op jit(solution)/shard_map/ppermute | solution.py:359
  254.8 3.7 %collective-permute-start.44 = (bf16[1,132,384]{2,1,0:T(8,128)(2,1)S(1)}, bf16[1,132,384]{2,1,0:T(8,128)(2,1)S(1)}, u32[]{:S(2)}, u32[]{:S(2)}) collective-permute-start(bf16[1,132,384]{2,1,0:T(8,128)(2,1)S(1)} %constant_dynamic-slice_fusion.2), channel_id=1, source_target_pairs={{0,16},{2,18},{4,20},{6,22},{8,24},{10,26},{12,28},{14,30},{16,0},... | collective-permute-start | bytes 304136 | tf_op jit(solution)/shard_map/ppermute | solution.py:360
  261.6 4.5 %collective-permute-done.44 = bf16[1,132,384]{2,1,0:T(8,128)(2,1)S(1)} collective-permute-done((bf16[1,132,384]{2,1,0:T(8,128)(2,1)S(1)}, bf16[1,132,384]{2,1,0:T(8,128)(2,1)S(1)}, u32[]{:S(2)}, u32[]{:S(2)}) %collective-permute-start.44) | collective-permute-done | bytes 101408 | tf_op jit(solution)/shard_map/ppermute | solution.py:360
  272.1 3.4 collective-permute-start.24
  277.9 3.3 collective-permute-start.47
  283.5 4.9 %collective-permute-done.47 = bf16[528,384]{1,0:T(8,128)(2,1)S(1)} collective-permute-done((bf16[528,384]{1,0:T(8,128)(2,1)S(1)}, bf16[528,384]{1,0:T(8,128)(2,1)S(1)}, u32[]{:S(2)}, u32[]{:S(2)}) %collective-permute-start.47) | collective-permute-done | bytes 405536 | tf_op jit(solution)/shard_map/ppermute | solution.py:360
  288.7 4.0 %collective-permute-done.40 = bf16[528,384]{1,0:T(8,128)(2,1)S(1)} collective-permute-done((bf16[528,384]{1,0:T(8,128)(2,1)S(1)}, bf16[528,384]{1,0:T(8,128)(2,1)S(1)}, u32[]{:S(2)}, u32[]{:S(2)}) %collective-permute-start.40) | collective-permute-done | bytes 405536 | tf_op jit(solution)/shard_map/ppermute | solution.py:360
  295.0 9.8 %shard_map.138 = (bf16[1024,768]{1,0:T(8,128)(2,1)}, f32[8,768]{1,0:T(8,128)}) custom-call(s32[2]{0:T(128)} %pad_add_fusion.1.place_ref, bf16[1024,2304]{1,0:T(8,128)(2,1)} %bitcast.23, bf16[1024,768]{1,0:T(8,128)(2,1)} %bitcast.27, f32[1024,768]{1,0:T(8,128)} %get-tuple-element.36.dx1_ref, bf16[2,768]{1,0:T(2,128)(2,1)} %broadcast_select_fusion.2.gain_ref, ...), custom_call_target="tpu_custom_call" | custom-call | flops 3623878656 | bytes 14576648 | tf_op jit(solution)/shard_map/pallas_call | solution.py:319
  323.2 3.6 %fusion = f32[384,2304]{1,0:T(8,128)} fusion(bf16[192,2304]{1,0:T(8,128)(2,1)} %collective-permute-done.32, bf16[192,1152]{1,0:T(8,128)(2,1)S(1)} %maximum_select_fusion.5, bf16[192,1152]{1,0:T(8,128)(2,1)S(1)} %maximum_select_fusion.4, pred[]{:T(512)S(6)} %eq.14), kind=kLoop, calls=%fused_computation.4 | loop fusion | flops 12386304 | bytes 5308417 | tf_op jit(solution)/shard_map/convert_element_type | solution.py:631
  326.8 12.5 %maximum_select_fusion = bf16[2112,768]{1,0:T(8,128)(2,1)S(1)} fusion(bf16[1056,768]{1,0:T(8,128)(2,1)} %collective-permute-done.48, bf16[1056,384]{1,0:T(8,128)(2,1)S(1)} %maximum_select_fusion.3, bf16[1056,384]{1,0:T(8,128)(2,1)S(1)} %maximum_select_fusion.2, pred[]{:T(512)S(6)} %eq.14), kind=kLoop, calls=%fused_computation.2 | loop fusion | flops 21086208 | bytes 6488065 | tf_op jit(solution)/shard_map/jit(_where)/select_n | solution.py:391
  (215 shorter events, 98.2 us)
Async XLA Ops:
  0.6 33.4 %collective-permute-start.2 = (bf16[2,384]{1,0:T(2,128)(2,1)}, bf16[2,384]{1,0:T(2,128)(2,1)S(1)}, u32[]{:S(2)}, u32[]{:S(2)}) collective-permute-start(bf16[2,384]{1,0:T(2,128)(2,1)} %param.14), channel_id=1, source_target_pairs={{0,1},{1,0},{2,3},{3,2},{4,5},{5,4},{6,7},{7,6},{8,9},{9,8},{10,11... | collective-permute-start | bytes 4616 | tf_op jit(solution)/shard_map/ppermute | solution.py:452
  4.8 34.6 %collective-permute-start.5 = (bf16[192,768]{1,0:T(8,128)(2,1)S(1)}, bf16[192,768]{1,0:T(8,128)(2,1)S(1)}, u32[]{:S(2)}, u32[]{:S(2)}) collective-permute-start(bf16[192,768]{1,0:T(8,128)(2,1)S(1)} %constant_dynamic-slice_fusion.22), channel_id=1, source_target_pairs={{0,1},{1,0},{2,3},{3,2},{4,5},{5,4},{6,7},{7,6},{8,9},{9,8},{10,11... | collective-permute-start | bytes 884744 | tf_op jit(solution)/shard_map/ppermute | solution.py:344
  6.2 27.6 %collective-permute-start.3 = (bf16[192,2304]{1,0:T(8,128)(2,1)S(1)}, bf16[192,2304]{1,0:T(8,128)(2,1)}, u32[]{:S(2)}, u32[]{:S(2)}) collective-permute-start(bf16[192,2304]{1,0:T(8,128)(2,1)S(1)} %constant_dynamic-slice_fusion.23), channel_id=1, source_target_pairs={{0,1},{1,0},{2,3},{3,2},{4,5},{5,4},{6,7},{7,6},{8,9},{9,8},{10,11... | collective-permute-start | bytes 2654216 | tf_op jit(solution)/shard_map/ppermute | solution.py:344
  8.3 44.6 %collective-permute-start.7 = (bf16[192,2304]{1,0:T(8,128)(2,1)S(1)}, bf16[192,2304]{1,0:T(8,128)(2,1)}, u32[]{:S(2)}, u32[]{:S(2)}) collective-permute-start(bf16[192,2304]{1,0:T(8,128)(2,1)S(1)} %constant_dynamic-slice_fusion.21), channel_id=1, source_target_pairs={{0,1},{1,0},{2,3},{3,2},{4,5},{5,4},{6,7},{7,6},{8,9},{9,8},{10,11... | collective-permute-start | bytes 2654216 | tf_op jit(solution)/shard_map/ppermute | solution.py:344
  9.7 51.0 %collective-permute-start.1 = (bf16[8,64,768]{2,1,0:T(8,128)(2,1)}, bf16[8,64,768]{2,1,0:T(8,128)(2,1)}, u32[]{:S(2)}, u32[]{:S(2)}) collective-permute-start(bf16[8,64,768]{2,1,0:T(8,128)(2,1)} %get-tuple-element.59), channel_id=1, source_target_pairs={{2,0},{4,2},{6,4},{8,6},{10,8},{12,10},{14,12},{16,14},{18,16},{20... | collective-permute-start | bytes 2359304 | tf_op jit(solution)/shard_map/ppermute | solution.py:26
  33.9 27.4 %collective-permute-start.4 = (bf16[192,2304]{1,0:T(8,128)(2,1)}, bf16[192,2304]{1,0:T(8,128)(2,1)}, u32[]{:S(2)}, u32[]{:S(2)}) collective-permute-start(bf16[192,2304]{1,0:T(8,128)(2,1)} %collective-permute-done.3.w_far), channel_id=1, source_target_pairs={{0,2},{2,0},{4,6},{6,4},{8,10},{10,8},{12,14},{14,12},{16,18},{18,... | collective-permute-start | bytes 2654216 | tf_op jit(solution)/shard_map/ppermute | solution.py:345
  34.0 27.2 %collective-permute-start = (bf16[8,64,768]{2,1,0:T(8,128)(2,1)S(1)}, bf16[8,64,768]{2,1,0:T(8,128)(2,1)}, u32[]{:S(2)}, u32[]{:S(2)}) collective-permute-start(bf16[8,64,768]{2,1,0:T(8,128)(2,1)S(1)} %copy-done.3), channel_id=1, source_target_pairs={{0,2},{2,4},{4,6},{6,8},{8,10},{10,12},{12,14},{14,16},{16,18},{18... | collective-permute-start | bytes 2359304 | tf_op jit(solution)/shard_map/ppermute | solution.py:26
  39.4 21.3 %collective-permute-start.9 = (bf16[288,768]{1,0:T(8,128)(2,1)S(1)}, bf16[288,768]{1,0:T(8,128)(2,1)S(1)}, u32[]{:S(2)}, u32[]{:S(2)}) collective-permute-start(bf16[288,768]{1,0:T(8,128)(2,1)S(1)} %constant_dynamic-slice_fusion.20), channel_id=1, source_target_pairs={{0,1},{1,0},{2,3},{3,2},{4,5},{5,4},{6,7},{7,6},{8,9},{9,8},{10,11... | collective-permute-start | bytes 1327112 | tf_op jit(solution)/shard_map/ppermute | solution.py:344
  52.8 34.9 %collective-permute-start.8 = (bf16[192,2304]{1,0:T(8,128)(2,1)}, bf16[192,2304]{1,0:T(8,128)(2,1)S(1)}, u32[]{:S(2)}, u32[]{:S(2)}) collective-permute-start(bf16[192,2304]{1,0:T(8,128)(2,1)} %collective-permute-done.7.in_far), channel_id=1, source_target_pairs={{0,2},{2,0},{4,6},{6,4},{8,10},{10,8},{12,14},{14,12},{16,18},{18,... | collective-permute-start | bytes 2654216 | tf_op jit(solution)/shard_map/ppermute | solution.py:345
  60.7 27.0 %collective-permute-start.6 = (bf16[192,768]{1,0:T(8,128)(2,1)S(1)}, bf16[192,768]{1,0:T(8,128)(2,1)S(1)}, u32[]{:S(2)}, u32[]{:S(2)}) collective-permute-start(bf16[192,768]{1,0:T(8,128)(2,1)S(1)} %collective-permute-done.5.out_far), channel_id=1, source_target_pairs={{0,2},{2,0},{4,6},{6,4},{8,10},{10,8},{12,14},{14,12},{16,18},{18,... | collective-permute-start | bytes 884744 | tf_op jit(solution)/shard_map/ppermute | solution.py:345
  60.7 27.0 %collective-permute-start.10 = (bf16[288,768]{1,0:T(8,128)(2,1)S(1)}, bf16[288,768]{1,0:T(8,128)(2,1)S(1)}, u32[]{:S(2)}, u32[]{:S(2)}) collective-permute-start(bf16[288,768]{1,0:T(8,128)(2,1)S(1)} %collective-permute-done.9.down_far), channel_id=1, source_target_pairs={{0,2},{2,0},{4,6},{6,4},{8,10},{10,8},{12,14},{14,12},{16,18},{18,... | collective-permute-start | bytes 1327112 | tf_op jit(solution)/shard_map/ppermute | solution.py:345
  116.0 26.0 %collective-permute-start.11 = (bf16[8,64,768]{2,1,0:T(8,128)(2,1)}, bf16[8,64,768]{2,1,0:T(8,128)(2,1)S(1)}, u32[]{:S(2)}, u32[]{:S(2)}) collective-permute-start(bf16[8,64,768]{2,1,0:T(8,128)(2,1)} %get-tuple-element.32), channel_id=1, source_target_pairs={{0,2},{2,4},{4,6},{6,8},{8,10},{10,12},{12,14},{14,16},{16,18},{18... | collective-permute-start | bytes 2359304 | tf_op jit(solution)/shard_map/ppermute | solution.py:26
  118.1 24.0 %collective-permute-start.12 = (bf16[8,64,768]{2,1,0:T(8,128)(2,1)}, bf16[8,64,768]{2,1,0:T(8,128)(2,1)S(1)}, u32[]{:S(2)}, u32[]{:S(2)}) collective-permute-start(bf16[8,64,768]{2,1,0:T(8,128)(2,1)} %get-tuple-element.33), channel_id=1, source_target_pairs={{2,0},{4,2},{6,4},{8,6},{10,8},{12,10},{14,12},{16,14},{18,16},{20... | collective-permute-start | bytes 2359304 | tf_op jit(solution)/shard_map/ppermute | solution.py:26
  119.5 10.8 %collective-permute-start.14 = (f32[8,16,128]{2,1,0:T(8,128)S(1)}, f32[8,16,128]{2,1,0:T(8,128)S(1)}, u32[]{:S(2)}, u32[]{:S(2)}) collective-permute-start(f32[8,16,128]{2,1,0:T(8,128)S(1)} %copy-done.9), channel_id=1, source_target_pairs={{0,2},{2,4},{4,6},{6,8},{8,10},{10,12},{12,14},{14,16},{16,18},{18... | collective-permute-start | bytes 196616 | tf_op jit(solution)/shard_map/ppermute | solution.py:26
  130.3 11.1 %collective-permute-start.15 = (f32[8,16,128]{2,1,0:T(8,128)}, f32[8,16,128]{2,1,0:T(8,128)S(1)}, u32[]{:S(2)}, u32[]{:S(2)}) collective-permute-start(f32[8,16,128]{2,1,0:T(8,128)} %get-tuple-element.35.delta_ref), channel_id=1, source_target_pairs={{2,0},{4,2},{6,4},{8,6},{10,8},{12,10},{14,12},{16,14},{18,16},{20... | collective-permute-start | bytes 196616 | tf_op jit(solution)/shard_map/ppermute | solution.py:26
  172.3 17.8 %collective-permute-start.17 = (bf16[2,192,2304]{2,1,0:T(8,128)(2,1)S(1)}, bf16[2,192,2304]{2,1,0:T(8,128)(2,1)S(1)}, u32[]{:S(2)}, u32[]{:S(2)}) collective-permute-start(bf16[2,192,2304]{2,1,0:T(8,128)(2,1)S(1)} %constant_dynamic-slice_fusion.19), channel_id=1, source_target_pairs={{0,2},{2,0},{4,6},{6,4},{8,10},{10,8},{12,14},{14,12},{16,18},{18,... | collective-permute-start | bytes 5308424 | tf_op jit(solution)/shard_map/ppermute | solution.py:360
  190.7 12.2 %collective-permute-start.25 = (bf16[2,96,1152]{2,1,0:T(8,128)(2,1)S(1)}, bf16[2,96,1152]{2,1,0:T(8,128)(2,1)S(1)}, u32[]{:S(2)}, u32[]{:S(2)}) collective-permute-start(bf16[2,96,1152]{2,1,0:T(8,128)(2,1)S(1)} %constant_dynamic-slice_fusion.14), channel_id=1, source_target_pairs={{0,4},{2,6},{4,0},{6,2},{8,12},{10,14},{12,8},{14,10},{16,20},{18,... | collective-permute-start | bytes 1327112 | tf_op jit(solution)/shard_map/ppermute | solution.py:360
  194.9 21.7 %collective-permute-start.33 = (bf16[2,1056,768]{2,1,0:T(8,128)(2,1)}, bf16[2,1056,768]{2,1,0:T(8,128)(2,1)}, u32[]{:S(2)}, u32[]{:S(2)}) collective-permute-start(bf16[2,1056,768]{2,1,0:T(8,128)(2,1)} %constant_dynamic-slice_fusion.10), channel_id=1, source_target_pairs={{0,2},{2,0},{4,6},{6,4},{8,10},{10,8},{12,14},{14,12},{16,18},{18,... | collective-permute-start | bytes 9732104 | tf_op jit(solution)/shard_map/ppermute | solution.py:360
  195.0 13.0 %collective-permute-start.18 = (bf16[1,192,1152]{2,1,0:T(8,128)(2,1)S(1)}, bf16[1,192,1152]{2,1,0:T(8,128)(2,1)S(1)}, u32[]{:S(2)}, u32[]{:S(2)}) collective-permute-start(bf16[1,192,1152]{2,1,0:T(8,128)(2,1)S(1)} %constant_dynamic-slice_fusion.18), channel_id=1, source_target_pairs={{0,1},{1,0},{2,3},{3,2},{4,5},{5,4},{6,7},{7,6},{8,9},{9,8},{10,11... | collective-permute-start | bytes 1327112 | tf_op jit(solution)/shard_map/ppermute | solution.py:359
  203.1 9.2 %collective-permute-start.26 = (bf16[1,96,1152]{2,1,0:T(8,128)(2,1)S(1)}, bf16[1,96,1152]{2,1,0:T(8,128)(2,1)S(1)}, u32[]{:S(2)}, u32[]{:S(2)}) collective-permute-start(bf16[1,96,1152]{2,1,0:T(8,128)(2,1)S(1)} %constant_dynamic-slice_fusion.13), channel_id=1, source_target_pairs={{0,1},{1,0},{2,3},{3,2},{4,5},{5,4},{6,7},{7,6},{8,9},{9,8},{10,11... | collective-permute-start | bytes 663560 | tf_op jit(solution)/shard_map/ppermute | solution.py:359
  220.8 18.1 %collective-permute-start.41 = (bf16[2,528,384]{2,1,0:T(8,128)(2,1)S(1)}, bf16[2,528,384]{2,1,0:T(8,128)(2,1)S(1)}, u32[]{:S(2)}, u32[]{:S(2)}) collective-permute-start(bf16[2,528,384]{2,1,0:T(8,128)(2,1)S(1)} %constant_dynamic-slice_fusion.5), channel_id=1, source_target_pairs={{0,4},{2,6},{4,0},{6,2},{8,12},{10,14},{12,8},{14,10},{16,20},{18,... | collective-permute-start | bytes 2433032 | tf_op jit(solution)/shard_map/ppermute | solution.py:360
  221.1 18.6 %collective-permute-start.34 = (bf16[1,1056,384]{2,1,0:T(8,128)(2,1)S(1)}, bf16[1,1056,384]{2,1,0:T(8,128)(2,1)S(1)}, u32[]{:S(2)}, u32[]{:S(2)}) collective-permute-start(bf16[1,1056,384]{2,1,0:T(8,128)(2,1)S(1)} %constant_dynamic-slice_fusion.9), channel_id=1, source_target_pairs={{0,1},{1,0},{2,3},{3,2},{4,5},{5,4},{6,7},{7,6},{8,9},{9,8},{10,11... | collective-permute-start | bytes 2433032 | tf_op jit(solution)/shard_map/ppermute | solution.py:359
  232.5 9.8 %collective-permute-start.30 = (bf16[48,1152]{1,0:T(8,128)(2,1)S(1)}, bf16[48,1152]{1,0:T(8,128)(2,1)S(1)}, u32[]{:S(2)}, u32[]{:S(2)}) collective-permute-start(bf16[48,1152]{1,0:T(8,128)(2,1)S(1)} %maximum_select_fusion.13), channel_id=1, source_target_pairs={{0,8},{2,10},{4,12},{6,14},{8,0},{10,2},{12,4},{14,6},{16,24},{18,... | collective-permute-start | bytes 331784 | tf_op jit(solution)/shard_map/ppermute | solution.py:360
  235.7 36.4 %collective-permute-start.23 = (bf16[48,1152]{1,0:T(8,128)(2,1)S(1)}, bf16[48,1152]{1,0:T(8,128)(2,1)S(1)}, u32[]{:S(2)}, u32[]{:S(2)}) collective-permute-start(bf16[48,1152]{1,0:T(8,128)(2,1)S(1)} %maximum_select_fusion.12), channel_id=1, source_target_pairs={{0,8},{2,10},{4,12},{6,14},{8,0},{10,2},{12,4},{14,6},{16,24},{18,... | collective-permute-start | bytes 331784 | tf_op jit(solution)/shard_map/ppermute | solution.py:360
  239.9 10.5 %collective-permute-start.35 = (bf16[1,528,384]{2,1,0:T(8,128)(2,1)S(1)}, bf16[1,528,384]{2,1,0:T(8,128)(2,1)S(1)}, u32[]{:S(2)}, u32[]{:S(2)}) collective-permute-start(bf16[1,528,384]{2,1,0:T(8,128)(2,1)S(1)} %constant_dynamic-slice_fusion.8), channel_id=1, source_target_pairs={{0,4},{2,6},{4,0},{6,2},{8,12},{10,14},{12,8},{14,10},{16,20},{18,... | collective-permute-start | bytes 1216520 | tf_op jit(solution)/shard_map/ppermute | solution.py:360
  242.3 39.0 %collective-permute-start.31 = (bf16[96,1152]{1,0:T(8,128)(2,1)S(1)}, bf16[96,1152]{1,0:T(8,128)(2,1)S(1)}, u32[]{:S(2)}, u32[]{:S(2)}) collective-permute-start(bf16[96,1152]{1,0:T(8,128)(2,1)S(1)} %maximum_select_fusion.9), channel_id=1, source_target_pairs={{0,4},{2,6},{4,0},{6,2},{8,12},{10,14},{12,8},{14,10},{16,20},{18,... | collective-permute-start | bytes 663560 | tf_op jit(solution)/shard_map/ppermute | solution.py:360
  254.8 11.3 %collective-permute-start.44 = (bf16[1,132,384]{2,1,0:T(8,128)(2,1)S(1)}, bf16[1,132,384]{2,1,0:T(8,128)(2,1)S(1)}, u32[]{:S(2)}, u32[]{:S(2)}) collective-permute-start(bf16[1,132,384]{2,1,0:T(8,128)(2,1)S(1)} %constant_dynamic-slice_fusion.2), channel_id=1, source_target_pairs={{0,16},{2,18},{4,20},{6,22},{8,24},{10,26},{12,28},{14,30},{16,0},... | collective-permute-start | bytes 304136 | tf_op jit(solution)/shard_map/ppermute | solution.py:360
  272.1 11.3 %collective-permute-start.24 = (bf16[96,1152]{1,0:T(8,128)(2,1)S(1)}, bf16[96,1152]{1,0:T(8,128)(2,1)S(1)}, u32[]{:S(2)}, u32[]{:S(2)}) collective-permute-start(bf16[96,1152]{1,0:T(8,128)(2,1)S(1)} %maximum_select_fusion.8), channel_id=1, source_target_pairs={{0,4},{2,6},{4,0},{6,2},{8,12},{10,14},{12,8},{14,10},{16,20},{18,... | collective-permute-start | bytes 663560 | tf_op jit(solution)/shard_map/ppermute | solution.py:360
  277.9 10.5 %collective-permute-start.47 = (bf16[528,384]{1,0:T(8,128)(2,1)S(1)}, bf16[528,384]{1,0:T(8,128)(2,1)S(1)}, u32[]{:S(2)}, u32[]{:S(2)}) collective-permute-start(bf16[528,384]{1,0:T(8,128)(2,1)S(1)} %maximum_select_fusion.7), channel_id=1, source_target_pairs={{0,4},{2,6},{4,0},{6,2},{8,12},{10,14},{12,8},{14,10},{16,20},{18,... | collective-permute-start | bytes 1216520 | tf_op jit(solution)/shard_map/ppermute | solution.py:360
  281.6 11.2 %collective-permute-start.40 = (bf16[528,384]{1,0:T(8,128)(2,1)S(1)}, bf16[528,384]{1,0:T(8,128)(2,1)S(1)}, u32[]{:S(2)}, u32[]{:S(2)}) collective-permute-start(bf16[528,384]{1,0:T(8,128)(2,1)S(1)} %maximum_select_fusion.6), channel_id=1, source_target_pairs={{0,4},{2,6},{4,0},{6,2},{8,12},{10,14},{12,8},{14,10},{16,20},{18,... | collective-permute-start | bytes 1216520 | tf_op jit(solution)/shard_map/ppermute | solution.py:360
  294.4 32.4 %collective-permute-start.48 = (bf16[1056,768]{1,0:T(8,128)(2,1)}, bf16[1056,768]{1,0:T(8,128)(2,1)}, u32[]{:S(2)}, u32[]{:S(2)}) collective-permute-start(bf16[1056,768]{1,0:T(8,128)(2,1)} %pad_maximum_fusion), channel_id=1, source_target_pairs={{0,2},{2,0},{4,6},{6,4},{8,10},{10,8},{12,14},{14,12},{16,18},{18,... | collective-permute-start | bytes 4866056 | tf_op jit(solution)/shard_map/ppermute | solution.py:360
  294.5 28.7 %collective-permute-start.32 = (bf16[192,2304]{1,0:T(8,128)(2,1)S(1)}, bf16[192,2304]{1,0:T(8,128)(2,1)}, u32[]{:S(2)}, u32[]{:S(2)}) collective-permute-start(bf16[192,2304]{1,0:T(8,128)(2,1)S(1)} %pad_maximum_fusion.3), channel_id=1, source_target_pairs={{0,2},{2,0},{4,6},{6,4},{8,10},{10,8},{12,14},{14,12},{16,18},{18,... | collective-permute-start | bytes 2654216 | tf_op jit(solution)/shard_map/ppermute | solution.py:360
  (39 other events, 343.4 us)

commit v3 on v2

--- a/solution.py
+++ b/solution.py
@@ -1,3 +1,5 @@
+from functools import partial
+
 import jax
 import jax.numpy as jnp
 from jax import lax
@@ -60,8 +62,22 @@
     index, core = place_ref[0], place_ref[1]
     other = (1 - index) * rows
     whole[pl.ds(pl.multiple_of(index * rows, half), rows), :] = own[...]
-    whole[pl.ds(pl.multiple_of(other + core * half, half), half), :] = far[...]
-    whole[pl.ds(pl.multiple_of(other + (1 - core) * half, half), half), :] = near[...]
+    whole[pl.ds(pl.multiple_of(other + core * half, half), half), :] = far[:half]
+    whole[pl.ds(pl.multiple_of(other + (1 - core) * half, half), half), :] = near[:half]
+
+
+def place_folded(place_ref, whole, own, far, near, at):
+    rows, width = own.shape
+    third = rows // 6
+    index, core = place_ref[0], place_ref[1]
+    other = (1 - index) * rows
+    whole[pl.ds(pl.multiple_of(index * rows, third), rows), :] = own[...]
+    for i in range(3):
+        columns = slice(i * width, (i + 1) * width)
+        first = other + core * 3 * third + i * third
+        whole[pl.ds(pl.multiple_of(first, third), third), :] = far[at : at + third, columns]
+        first = other + (1 - core) * 3 * third + i * third
+        whole[pl.ds(pl.multiple_of(first, third), third), :] = near[at : at + third, columns]
 
 
 def attend_kernel(
@@ -119,17 +135,27 @@
     lse_ref[0] = jnp.transpose(log_totals)[:HEAD_ROWS]
 
 
+def three_parts(value):
+    parts = []
+    for _ in range(3):
+        parts.append(value.astype(bf16))
+        value = value - parts[-1].astype(f32)
+    return parts
+
+
 def feed_kernel(
-    place_ref, tok_ref, mix_ref, dy_ref, gain_ref,
-    out_own, out_far, out_near, in_own, in_far, in_near, down_own, down_far, down_near,
-    layer_ref, dx1_ref, do_ref, lo_ref, hi_ref, delta_ref, h2_ref, dup_ref, mid_ref, dmix_ref, gsum_ref,
+    place_ref, tok_ref, mix_ref, dy_ref, lse_ref, gain_ref,
+    out_own, in_own, down_own, far_ref, near_ref,
+    layer_ref, dx1_ref, do_ref, lo_ref, hi_ref, rows_ref, h2_ref, dup_ref, mid_ref, dmix_ref, gsum_ref,
     w_out, w_in, w_down,
 ):
     @pl.when(pl.program_id(0) == 0)
     def _():
-        place_weight(place_ref, w_out, out_own, out_far, out_near)
-        place_weight(place_ref, w_in, in_own, in_far, in_near)
-        place_weight(place_ref, w_down, down_own, down_far, down_near)
+        at = in_own.shape[0] // 2
+        place_weight(place_ref, w_in, in_own, far_ref, near_ref)
+        for whole, own in ((w_down, down_own), (w_out, out_own)):
+            place_folded(place_ref, whole, own, far_ref, near_ref, at)
+            at += own.shape[0] // 6
         gsum_ref[...] = jnp.zeros_like(gsum_ref)
 
     rows, width = tok_ref.shape
@@ -170,41 +196,159 @@
     delta = dot(high, pick) + dot(low, pick)
     for i in range(rows // block):
         piece = grad_mixed[i * block : (i + 1) * block]
-        lo_ref[i] = piece[:HALF_WINDOW]
-        hi_ref[i] = piece[HALF_WINDOW:]
-        delta_ref[i] = jnp.transpose(delta[i * block : (i + 1) * block])[:HEAD_ROWS]
-
-
-def grads_kernel(h2_ref, dup_ref, mid_ref, dy_ref, mix_ref, dmix_ref, out_ref):
+        inner_sum = jnp.transpose(delta[i * block : (i + 1) * block])[:HEAD_ROWS]
+        rows_ref[i, :HEAD_ROWS] = inner_sum
+        rows_ref[i, HEAD_ROWS:] = lse_ref[i]
+        parts = jnp.concatenate(three_parts(lse_ref[i]) + three_parts(inner_sum), 1)
+        for ref, own in ((lo_ref, piece[:HALF_WINDOW]), (hi_ref, piece[HALF_WINDOW:])):
+            ref[i, :HALF_WINDOW] = own
+            ref[i, HALF_WINDOW:] = parts
+
+
+def pack_first_kernel(place_ref, qkv_ref, gain_ref, out_ref):
+    half = qkv_ref.shape[0] // 2
+    count, width = gain_ref.shape
+    out_ref[:half] = qkv_ref[pl.ds(pl.multiple_of(place_ref[1] * half, half), half), :]
+    out_ref[half:] = jnp.zeros_like(out_ref[half:])
+    filler = jnp.zeros((out_ref.shape[0] - half - count, width), bf16)
+    out_ref[half:, :width] = jnp.concatenate([gain_ref[...], filler], 0)
+
+
+def pack_later_kernel(place_ref, out_w, in_w, down_w, tok_ref, later_ref, head_ref, tail_ref):
+    core = place_ref[1]
+    half = in_w.shape[0] // 2
+    width = out_w.shape[1]
+    later_ref[:half] = in_w[pl.ds(pl.multiple_of(core * half, half), half), :]
+    at = half
+    for ref in (down_w, out_w):
+        third = ref.shape[0] // 6
+        for i in range(3):
+            first = pl.multiple_of((core * 3 + i) * third, third)
+            later_ref[at : at + third, i * width : (i + 1) * width] = ref[pl.ds(first, third), :]
+        at += third
+    rows = tok_ref.shape[1]
+    for i in range(tok_ref.shape[0]):
+        head_ref[i] = tok_ref[i, :HALF_WINDOW]
+        tail_ref[i] = tok_ref[i, rows - HALF_WINDOW :]
+
+
+def part_rows(place_ref, whole, keep_ref, send_ref):
+    rows = keep_ref.shape[1]
+    core = place_ref[1]
+    for i in range(2):
+        keep_ref[i] = whole[pl.ds(pl.multiple_of((2 * i + core) * rows, 16), rows), :]
+        send_ref[i] = whole[pl.ds(pl.multiple_of((2 * i + 1 - core) * rows, 16), rows), :]
+
+
+def as_column(row_groups):
+    ones = jnp.ones((row_groups.shape[0], PAIR), bf16)
+    return sum(dot_left(part, ones) for part in three_parts(row_groups))
+
+
+def grad_qkv_kernel(place_ref, left_ref, right_ref, one_ref, two_ref, keep_ref, send_ref, whole):
+    step = pl.program_id(0)
+    whole[...] = dot_left(left_ref[...], right_ref[...]).astype(bf16)
+
+    @pl.when(step == pl.num_programs(0) - 1)
+    def _():
+        lane = lax.broadcasted_iota(jnp.int32, (1, PAIR), 1)
+        first, second = as_column(one_ref[...]), as_column(two_ref[...])
+        columns = jnp.where(lane == 0, first, jnp.where(lane == 1, second, 0.0)).astype(bf16)
+        at = whole.shape[1] - 2 * PAIR
+        whole[:, at : at + PAIR] = columns
+        whole[:, at + PAIR :] = jnp.zeros_like(columns)
+
+    part_rows(place_ref, whole, keep_ref, send_ref)
+
+
+def grads_kernel(place_ref, h2_ref, dup_ref, mid_ref, dy_ref, mix_ref, dmix_ref, keep_ref, send_ref, whole):
     step = pl.program_id(0)
     width = dy_ref.shape[1]
-    half = out_ref.shape[0] // 2
+    half = whole.shape[0] // 2
     part = width // 2
-    ffn_rows = mid_ref.shape[1]
-    ffn_part = 3 * ffn_rows // 2
+    third = mid_ref.shape[1] // 2
     grad = dot_left(h2_ref[...], dup_ref[...]).astype(bf16)
     at = pl.multiple_of(step * part, part)
-    out_ref[pl.ds(at, part), :] = grad[:part]
-    out_ref[pl.ds(half + at, part), :] = grad[part:]
+    whole[pl.ds(at, part), :] = grad[:part]
+    whole[pl.ds(half + at, part), :] = grad[part:]
     grad = dot_left(mid_ref[...], dy_ref[...]).astype(bf16)
-    third = ffn_rows // 2
     for i in range(2):
         index = 2 * step + i
         owner = index // 3
         at = pl.multiple_of(owner * half + 3 * part + (index - 3 * owner) * third, 64)
-        out_ref[pl.ds(at, third), :] = grad[i * third : (i + 1) * third]
+        whole[pl.ds(at, third), :] = grad[i * third : (i + 1) * third]
     grad = dot_left(mix_ref[...], dmix_ref[...]).astype(bf16)
     columns = pl.ds(pl.multiple_of(step * (width // 3), PAIR), width // 3)
-    at = 3 * part + ffn_part
-    out_ref[at : at + part, columns] = grad[:part]
-    out_ref[half + at : half + at + part, columns] = grad[part:]
+    at = 3 * part + 3 * third
+    whole[at : at + part, columns] = grad[:part]
+    whole[half + at : half + at + part, columns] = grad[part:]
+
+    @pl.when(step == pl.num_programs(0) - 1)
+    def _():
+        spare = half - at - part
+        if spare:
+            for start in (at + part, half + at + part):
+                whole[start : start + spare] = jnp.zeros((spare, width), bf16)
+        part_rows(place_ref, whole, keep_ref, send_ref)
+
+
+def total_of(*values):
+    total = values[0].astype(f32)
+    for value in values[1:]:
+        total += value.astype(f32)
+    return total.astype(bf16)
+
+
+def split_first_kernel(place_ref, held, got, hold_y, send_y, hold_x, send_x):
+    owner, bit = place_ref[0], place_ref[2]
+    width = held.shape[2] // 2
+    for j in range(2):
+        for to, ref in ((owner, hold_y), (1 - owner, send_y)):
+            ref[j] = total_of(held[2 * to + j, :, :width], got[2 * to + j, :, :width])
+        for to, ref in ((bit, hold_x), (1 - bit, send_x)):
+            ref[j] = total_of(held[2 * j + to, :, width:], got[2 * j + to, :, width:])
+
+
+def split_second_kernel(place_ref, hold_y, got_y, hold_x, got_x, keep, send_x, send_y):
+    owner, bit = place_ref[0], place_ref[2]
+    width = hold_y.shape[2]
+    keep[:, :width] = total_of(hold_y[bit], got_y[bit])
+    send_x[...] = total_of(hold_y[1 - bit], got_y[1 - bit])
+    keep[:, width:] = total_of(hold_x[owner], got_x[owner])
+    send_y[...] = total_of(hold_x[1 - owner], got_x[1 - owner])
+
+
+def split_third_kernel(place_ref, held, got_left, got_right, *refs, slot):
+    index = place_ref[slot]
+    width = got_left.shape[2]
+    for d, ref in enumerate(refs):
+        ref[:, :width] = total_of(held[index ^ d, :, :width], got_left[index ^ d])
+        ref[:, width:] = total_of(held[index ^ d, :, width:], got_right[index ^ d])
+
+
+def sum_cut_kernel(place_ref, held, *refs, slot, arrived):
+    index = place_ref[slot]
+    for d, out_ref in enumerate(refs[arrived:]):
+        total = held[index ^ d].astype(f32)
+        for got in refs[:arrived]:
+            total += got[index ^ d].astype(f32)
+        out_ref[...] = total.astype(bf16)
+
+
+def join_kernel(place_ref, *refs, slot):
+    index = place_ref[slot]
+    for d, ref in enumerate(refs[:-1]):
+        refs[-1][index ^ d] = ref[...]
 
 
 def attend_back_kernel(
-    q_ref, k_ref, v_ref, do_ref, do_before, do_after, lse_ref, lse_edge, delta_ref, delta_edge,
-    bias_ref, bias_edge, cos_ref, sin_ref, out_ref,
+    q_ref, k_ref, v_ref, do_ref, do_before, do_after, own_rows, rows_before, rows_after,
+    bias_ref, bias_edge, cos_ref, sin_ref, *refs,
 ):
+    out_ref, mark_ref = refs[-2:]
+    mark_ref[...] = jnp.zeros_like(mark_ref)
     rows, width = do_ref.shape[1], do_ref.shape[2]
+    out_ref[0, :, 3 * width :] = jnp.zeros((rows, 2 * PAIR), bf16)
     inner = slice(HALF_WINDOW, HALF_WINDOW + rows)
     lane = lax.broadcasted_iota(jnp.int32, (1, PAIR), 1)
     first_half = (lane % HEAD_DIM) < HEAD_DIM // 2
@@ -212,7 +356,7 @@
     top_rows = lax.broadcasted_iota(jnp.int32, (PAIR, 1), 0) < HEAD_DIM
     cosine, sine = cos_ref[0, inner], sin_ref[0, inner]
     bias = jnp.concatenate([bias_ref[0], bias_ref[0]], 1)
-    edge = jnp.concatenate([bias_edge[0], bias_edge[0]], 1)
+    offsets_edge = jnp.concatenate([bias_edge[0], bias_edge[0]], 1)
 
     def split(value):
         zero = jnp.zeros_like(value)
@@ -220,10 +364,22 @@
             [jnp.where(first_head, value, zero), jnp.where(first_head, zero, value)], 0
         )
 
-    def row_of(ref, pair):
-        return jnp.concatenate(
-            [ref[0, 2 * pair : 2 * pair + 1, :], ref[0, 2 * pair + 1 : 2 * pair + 2, :]], 1
-        )
+    after_lane = lane < HALF_WINDOW
+    edge = []
+    for base in (3 * PAIR, 0):
+        value = jnp.zeros((HEAD_ROWS, PAIR), f32)
+        for at in (base, base + PAIR, base + 2 * PAIR):
+            columns = slice(at, at + PAIR)
+            value += jnp.where(
+                after_lane, rows_after[0, :, columns].astype(f32), rows_before[0, :, columns].astype(f32)
+            )
+        edge.append(value)
+    edge_sum, edge_lse = edge
+    own_sum, own_lse = own_rows[0, :HEAD_ROWS], own_rows[0, HEAD_ROWS:]
+
+    def row_of(value, pair):
+        at = 2 * pair
+        return jnp.concatenate([value[at : at + 1, :], value[at + 1 : at + 2, :]], 1)
 
     def back(keys, values, query, grad_mixed, offsets, log_total, inner_sum):
         probs = jnp.exp(dot_right(keys, query) + offsets - log_total)
@@ -239,7 +395,8 @@
         query = split(q_ref[0, inner, columns])
         grad_mixed = split(do_ref[0, :, columns])
         probs, grad_scores = back(
-            keys, values, query, grad_mixed, bias, row_of(lse_ref, pair), row_of(delta_ref, pair)
+            keys, values, query, grad_mixed, bias,
+            row_of(own_lse, pair), row_of(own_sum, pair),
         )
         query_edge = split(
             jnp.concatenate(
@@ -252,8 +409,8 @@
         )
         grad_edge = split(jnp.concatenate([do_after[0, :, columns], do_before[0, :, columns]], 0))
         probs_edge, scores_edge = back(
-            keys[inner], values[inner], query_edge, grad_edge, edge,
-            row_of(lse_edge, pair), row_of(delta_edge, pair),
+            keys[inner], values[inner], query_edge, grad_edge, offsets_edge,
+            row_of(edge_lse, pair), row_of(edge_sum, pair),
         )
         grad_values = dot(
             jnp.concatenate([probs[inner], probs_edge], 1),
@@ -274,10 +431,6 @@
         )
 
 
-def grad_qkv_kernel(h1_ref, dqkv_ref, out_ref):
-    out_ref[...] = dot_left(h1_ref[...], dqkv_ref[...]).astype(bf16)
-
-
 def stream_back_kernel(
     place_ref, dqkv_ref, tok_ref, dx1_ref, gain_ref, w_own, w_far, w_near, out_ref, gsum_ref, weight
 ):
@@ -294,6 +447,36 @@
     out_ref[...] = (dx1_ref[...] + norm_back(grad_normed, normed, factor)).astype(bf16)
 
 
+def join_halves(place_ref, whole, mine, other):
+    rows = mine.shape[0]
+    core = place_ref[1]
+    whole[pl.ds(pl.multiple_of(core * rows, 16), rows), :] = mine[...]
+    whole[pl.ds(pl.multiple_of((1 - core) * rows, 16), rows), :] = other[...]
+
+
+def finish_qkv_kernel(place_ref, mine, other, out_ref, gain_ref, columns):
+    rows = mine.shape[0]
+    core = place_ref[1]
+    width = out_ref.shape[1]
+    for ref, at in ((mine, core * rows), (other, (1 - core) * rows)):
+        at = pl.ds(pl.multiple_of(at, 16), rows)
+        out_ref[at, :] = ref[:, :width].astype(f32)
+        columns[at, :] = ref[:, width : width + PAIR].astype(f32)
+    gain_ref[...] = columns[...].T[: gain_ref.shape[0]]
+
+
+def finish_three_kernel(place_ref, mine, other, in_ref, down_ref, out_ref, whole):
+    join_halves(place_ref, whole, mine, other)
+    width = whole.shape[1]
+    at = 0
+    for i in range(in_ref.shape[1] // width):
+        in_ref[:, i * width : (i + 1) * width] = whole[at : at + in_ref.shape[0]].astype(f32)
+        at += in_ref.shape[0]
+    for ref in (down_ref, out_ref):
+        ref[...] = whole[at : at + ref.shape[0]].astype(f32)
+        at += ref.shape[0]
+
+
 def shape_of(*dims, dtype=bf16):
     return jax.ShapeDtypeStruct(dims, dtype)
 
@@ -302,7 +485,14 @@
     return pl.BlockSpec(array.shape, lambda i: (0,) * array.ndim)
 
 
-def run(kernel, grid, inputs, outputs, scratch=(), flops=0, whole=()):
+def run(kernel, grid, inputs, outputs, scratch=(), aliases=None, later=()):
+    first = len(inputs)
+    later = jax.tree.leaves(later)
+    inputs = [*inputs, *[(x, pl.ANY) for x in later]]
+
+    def body(*refs):
+        kernel(*refs[:first], *refs[first + len(later) :])
+
     def spec(block, place):
         return pl.BlockSpec(block, place)
 
@@ -310,20 +500,22 @@
     for item in inputs:
         if item[1] is None and item[0].dtype == jnp.int32:
             specs.append(pl.BlockSpec(memory_space=pltpu.SMEM))
+        elif item[1] is pl.ANY:
+            specs.append(pl.BlockSpec(memory_space=pl.ANY))
         elif item[1] is None:
             specs.append(whole_spec(item[0]))
         else:
             specs.append(spec(item[1], item[2]))
     out_specs = [whole_spec(o[0]) if o[1] is None else spec(o[1], o[2]) for o in outputs]
-    moved = sum(x[0].size * x[0].dtype.itemsize for x in list(inputs) + list(outputs))
     return pl.pallas_call(
-        kernel,
+        body,
         grid=(grid,),
         in_specs=specs,
         out_specs=out_specs,
         out_shape=[o[0] for o in outputs],
         scratch_shapes=list(scratch),
-        cost_estimate=pl.CostEstimate(flops=flops, bytes_accessed=moved, transcendentals=0),
+        input_output_aliases=aliases or {},
+        cost_estimate=pl.CostEstimate(flops=1, bytes_accessed=1, transcendentals=0),
         compiler_params=pltpu.CompilerParams(
             dimension_semantics=("arbitrary",), vmem_limit_bytes=56 * MIB
         ),
@@ -334,71 +526,143 @@
     return [(i, i ^ bit) for i in range(size)]
 
 
-def fetch_shards(shards):
-    core = lax.axis_index("seq") % 2
-    seq = lax.axis_size("seq")
-    pieces = []
-    for shard in shards:
-        half = shard.shape[0] // 2
-        mine = lax.dynamic_slice_in_dim(shard, core * half, half, 0)
-        far = lax.ppermute(mine, "fsdp", flip_route(2, 1))
-        near = lax.ppermute(far, "seq", flip_route(seq, 1))
-        pieces.append((shard, far, near))
-    return pieces
-
-
-def keep_and_send(block, bit, dim):
-    half = block.shape[dim] // 2
-    keep = lax.dynamic_slice_in_dim(block, bit * half, half, dim)
-    send = lax.dynamic_slice_in_dim(block, (1 - bit) * half, half, dim)
-    return keep, send
-
-
-def exchange(block, stage):
-    if stage < 0:
+def swap_half(half):
+    return lax.ppermute(half, "seq", flip_route(lax.axis_size("seq"), 1))
+
+
+def exchange(block, distance):
+    if distance == 0:
         return lax.ppermute(block, "fsdp", flip_route(2, 1))
-    return lax.ppermute(block, "seq", flip_route(lax.axis_size("seq"), 1 << stage))
-
-
-def stage_bit(stage):
-    if stage < 0:
-        return lax.axis_index("fsdp")
-    return (lax.axis_index("seq") >> stage) & 1
-
-
-def reduce_stage(block, stage):
-    keep, send = keep_and_send(block, stage_bit(stage), 0 if stage < 0 else 1)
-    got = exchange(send.astype(jnp.bfloat16), stage)
-    return (keep.astype(jnp.float32) + got.astype(jnp.float32)).astype(jnp.bfloat16)
-
-
-def summed_half(bundle):
+    return lax.ppermute(block, "seq", flip_route(lax.axis_size("seq"), distance))
+
+
+def together(*values):
+    return lax.optimization_barrier(values)
+
+
+def column_steps(rows, columns):
+    return 3 if rows * columns > 400_000 and columns % (3 * PAIR) == 0 else 1
+
+
+def sum_cut(place, slot, held, gots, later):
+    parts, rows, columns = held.shape
+    return run(
+        partial(sum_cut_kernel, slot=slot, arrived=len(gots)),
+        1,
+        [(place, None), *[(x, None) for x in (held, *gots)]],
+        [(shape_of(rows, columns), None) for _ in range(parts)],
+        later=later,
+    )
+
+
+def split_run(kernel, place, rows, inputs, outputs, later):
+    steps = 3 if rows % 48 == 0 else 1
+
+    def item(array):
+        block = (*array.shape[:-2], rows // steps, array.shape[-1])
+        lead = (0,) * (len(block) - 2)
+        return (array, block, lambda i: (*lead, i, 0))
+
+    return run(kernel, steps, [(place, None), *map(item, inputs)], [item(x) for x in outputs], later=later)
+
+
+def join(place, slot, parts, later):
+    rows, columns = parts[0].shape
+    steps = column_steps(len(parts) * rows, columns)
+    (whole,) = run(
+        partial(join_kernel, slot=slot),
+        steps,
+        [(place, None), *[(x, (rows, columns // steps), lambda i: (0, i)) for x in parts]],
+        [
+            (
+                shape_of(len(parts), rows, columns),
+                (len(parts), rows, columns // steps),
+                lambda i: (0, 0, i),
+            )
+        ],
+        later=later,
+    )
+    return whole.reshape(len(parts) * rows, columns)
+
+
+def bit_groups():
     stages = (lax.axis_size("seq") - 1).bit_length()
-    width = bundle.shape[2] // 2
-    bundle = jnp.pad(bundle, ((0, 0), (0, -bundle.shape[1] % lax.axis_size("seq")), (0, 0)))
-    bundle = reduce_stage(bundle, 0)
-    parts = [bundle[:, :, :width], bundle[:, :, width:]]
-    orders = [[-1] + list(range(1, stages)), [1, -1] + list(range(2, stages))]
-    for step in range(stages):
-        parts = [reduce_stage(part, order[step]) for part, order in zip(parts, orders)]
-    parts = [part[0] for part in parts]
-    for stage in reversed(range(stages)):
-        if stage == 0:
-            parts = [jnp.concatenate(parts, 1)]
-        bit = stage_bit(stage)
-        got = [exchange(part, stage) for part in parts]
-        parts = [
-            jnp.where(bit == 0, jnp.concatenate([p, g], 0), jnp.concatenate([g, p], 0))
-            for p, g in zip(parts, got)
-        ]
-    return parts[0]
-
-
-def summed_small(value):
-    stages = (lax.axis_size("seq") - 1).bit_length()
-    for stage in range(-1, stages):
-        value = value + exchange(value, stage)
-    return value
+    return [(0, 1), (1, 1)] + [(at, min(2, stages - at)) for at in range(2, stages, 2)]
+
+
+def member(group):
+    at, bits = group
+    return (lax.axis_index("seq") >> at) & ((1 << bits) - 1)
+
+
+def sum_stages(place, keep, send):
+    (got,), later = yield [(send, 1)]
+    rows, columns = keep.shape[1] // 2, keep.shape[2]
+    four = (4, rows, columns)
+    part = shape_of(2, rows, columns // 2)
+    hold_y, send_y, hold_x, send_x = split_run(
+        split_first_kernel, place, rows, [keep.reshape(four), got.reshape(four)], [part] * 4,
+        later,
+    )
+    (got_y, got_x), later = yield [(send_y, 0), (send_x, 2)]
+    block, send_x, send_y = split_run(
+        split_second_kernel,
+        place,
+        rows,
+        [hold_y, got_y, hold_x, got_x],
+        [shape_of(rows, columns), *[shape_of(rows, columns // 2)] * 2],
+        later,
+    )
+    arrived, later = yield [(send_x, 2), (send_y, 0)]
+    groups = list(enumerate(bit_groups()[2:], 3))
+    for step, (slot, group) in enumerate(groups):
+        count = 1 << group[1]
+        size = block.shape[0] // count
+        if step == 0:
+            block, *sends = run(
+                partial(split_third_kernel, slot=slot),
+                1,
+                [
+                    (place, None),
+                    *[(x.reshape(count, size, x.shape[1]), None) for x in (block, *arrived)],
+                ],
+                [(shape_of(size, columns), None) for _ in range(count)],
+                later=later,
+            )
+        else:
+            shape = (count, size, columns)
+            block, *sends = sum_cut(
+                place, slot, block.reshape(shape), [x.reshape(shape) for x in arrived], later
+            )
+        arrived, later = yield [(x, (d + 1) << group[0]) for d, x in enumerate(sends)]
+    (block,) = sum_cut(place, len(groups) + 3, block[None], [x[None] for x in arrived], later)
+    for slot, group in reversed([(2, (1, 1)), *groups]):
+        held, later = yield [(block, d << group[0]) for d in range(1, 1 << group[1])]
+        block = join(place, slot, [block, *held], later)
+    (other,), _ = yield [(block, 1)]
+    return block, other
+
+
+class Chain:
+    def __init__(self, stages):
+        self.stages, self.result = stages, None
+        self.post(next(stages))
+
+    def post(self, sends, gate=None, arrived=0):
+        blocks = [block for block, _ in sends]
+        if gate is not None:
+            held = together(*blocks, *gate.got[:arrived])
+            blocks = list(held[: len(blocks)])
+            gate.got[:arrived] = held[len(blocks) :]
+        self.sent = blocks
+        self.got = [exchange(block, distance) for block, (_, distance) in zip(blocks, sends)]
+
+    def advance(self, *later, gate=None, arrived=0):
+        try:
+            self.post(self.stages.send((self.got, later)), gate, arrived)
+        except StopIteration as end:
+            self.result = end.value
+        return self.sent
 
 
 def window_tables(pos, rows, head_width):
@@ -446,19 +710,48 @@
     count = num_seqs * rows
     ffn = 2 * down_weight.shape[0]
     seq_index, own_y = lax.axis_index("seq"), lax.axis_index("fsdp")
-    place = jnp.stack([own_y, seq_index % 2]).astype(jnp.int32)
-    tok_before = passed_along(tokens[:, rows - HALF_WINDOW :], "seq", 1)
-    tok_after = passed_along(tokens[:, :HALF_WINDOW], "seq", -1)
-    gains_other = lax.ppermute(norm_gains, "fsdp", flip_route(2, 1))
+    place = jnp.stack(
+        [own_y, seq_index % 2, *[member(group) for group in bit_groups()[1:]], 0 * own_y]
+    ).astype(jnp.int32)
+
+    gain_width = norm_gains.shape[1]
+    half = qkv_weight.shape[0] // 2
+    (first_half,) = run(
+        pack_first_kernel,
+        1,
+        [(place, None), (qkv_weight, None), (norm_gains, None)],
+        [(shape_of(half + 16, qkv_weight.shape[1]), None)],
+    )
+    far_qkv = exchange(first_half, 0)
+    later_rows = half + down_weight.shape[0] // 6 + out_weight.shape[0] // 6
+    halo = shape_of(num_seqs, HALF_WINDOW, width)
+    later_half, tok_head, tok_tail = run(
+        pack_later_kernel,
+        1,
+        [
+            (place, None),
+            *[(x, None) for x in (out_weight, in_weight, down_weight)],
+            (tokens, None),
+        ],
+        [(shape_of(later_rows, in_weight.shape[1]), None), (halo, None), (halo, None)],
+        later=first_half,
+    )
+    far_later = exchange(later_half, 0)
+    tok_before = passed_along(tok_tail, "seq", 1)
+    tok_after = passed_along(tok_head, "seq", -1)
+    padded_pos = jnp.pad(positions, ((0, 0), (HALF_WINDOW, HALF_WINDOW)), constant_values=-1)
+    key_pos = lax.dynamic_slice_in_dim(padded_pos, seq_index * rows, span, 1)
+    cosine, sine, bias, bias_t, bias_edge = window_tables(key_pos, rows, HEAD_DIM)
+    far_qkv, tok_before, tok_after, cosine, sine, bias, bias_t, bias_edge = together(
+        far_qkv, tok_before, tok_after, cosine, sine, bias, bias_t, bias_edge
+    )
+    w_qkv = (qkv_weight, far_qkv, swap_half(far_qkv))
+    gains_other = far_qkv[qkv_weight.shape[0] // 2 :, :gain_width][: norm_gains.shape[0]]
     gains = jnp.where(
         own_y == 0,
         jnp.concatenate([norm_gains, gains_other], 1),
         jnp.concatenate([gains_other, norm_gains], 1),
     )
-    w_qkv, w_out, w_in, w_down = fetch_shards([qkv_weight, out_weight, in_weight, down_weight])
-    padded_pos = jnp.pad(positions, ((0, 0), (HALF_WINDOW, HALF_WINDOW)), constant_values=-1)
-    key_pos = lax.dynamic_slice_in_dim(padded_pos, seq_index * rows, span, 1)
-    cosine, sine, bias, bias_t, bias_edge = window_tables(key_pos, rows, HEAD_DIM)
 
     def per_seq(i):
         return (i, 0, 0)
@@ -494,17 +787,17 @@
             (shape_of(num_seqs, HEAD_ROWS, PAIR, dtype=f32), (1, HEAD_ROWS, PAIR), per_seq),
         ],
         [pltpu.VMEM((width, 3 * width), bf16)],
-        flops=2 * num_seqs * span * width * 3 * width,
-    )
-    lse_before = passed_along(log_total, "seq", 1)
-    lse_after = passed_along(log_total, "seq", -1)
+    )
+    far_later, mixed = together(far_later, mixed)
+    near_later = swap_half(far_later)
 
     flat_tokens = tokens.reshape(count, width)
     flat_dy = cotangent.reshape(count, width)
     flat_mixed = mixed.reshape(count, width)
     step = 2 * rows
     tok_block = (step, width)
-    half_block = (2, HALF_WINDOW, width)
+    pack = HALF_WINDOW + HEAD_ROWS
+    half_block = (2, pack, width)
     (
         layer_out, grad_stream, grad_mixed, grad_lo, grad_hi, inner_sum,
         hidden_two, grad_up, middle, grad_attn, gain_sum_two,
@@ -516,16 +809,17 @@
             (flat_tokens, tok_block, row_block),
             (flat_mixed, tok_block, row_block),
             (flat_dy, tok_block, row_block),
+            (log_total, (2, HEAD_ROWS, PAIR), per_seq),
             (gains, None),
-            *[(piece, None) for piece in (*w_out, *w_in, *w_down)],
+            *[(x, None) for x in (out_weight, in_weight, down_weight, far_later, near_later)],
         ],
         [
             (shape_of(count, width), tok_block, row_block),
             (shape_of(count, width, dtype=f32), tok_block, row_block),
             (shape_of(count, width), tok_block, row_block),
-            (shape_of(num_seqs, HALF_WINDOW, width), half_block, per_seq),
-            (shape_of(num_seqs, HALF_WINDOW, width), half_block, per_seq),
-            (shape_of(num_seqs, HEAD_ROWS, PAIR, dtype=f32), (2, HEAD_ROWS, PAIR), per_seq),
+            (shape_of(num_seqs, pack, width), half_block, per_seq),
+            (shape_of(num_seqs, pack, width), half_block, per_seq),
+            (shape_of(num_seqs, 2 * HEAD_ROWS, PAIR, dtype=f32), (2, 2 * HEAD_ROWS, PAIR), per_seq),
             (shape_of(count, width), tok_block, row_block),
             (shape_of(count, 2 * ffn), (step, 2 * ffn), row_block),
             (shape_of(count, ffn), (step, ffn), row_block),
@@ -537,18 +831,18 @@
             pltpu.VMEM((width, 2 * ffn), bf16),
             pltpu.VMEM((ffn, width), bf16),
         ],
-        flops=2 * count * width * (2 * width + 4 * ffn + 2 * ffn),
     )
     do_before = passed_along(grad_hi, "seq", 1)
     do_after = passed_along(grad_lo, "seq", -1)
-    sum_before = passed_along(inner_sum, "seq", 1)
-    sum_after = passed_along(inner_sum, "seq", -1)
-
-    bundle_rows = 2 * (3 * width // 2 + ffn // 2 + width // 2)
-    (bundle,) = run(
+
+    size = max(lax.axis_size("seq"), PAIR)
+    bundle_rows = -(-(3 * width // 2 + ffn // 2 + width // 2) // size) * size
+    bundle_part = shape_of(2, bundle_rows // 2, width)
+    keep, send = run(
         grads_kernel,
         3,
         [
+            (place, None),
             (hidden_two, None),
             (grad_up, (count, 2 * ffn // 3), column_block),
             (middle, (count, ffn // 3), column_block),
@@ -556,83 +850,137 @@
             (flat_mixed, None),
             (grad_attn, (count, width // 3), column_block),
         ],
-        [(shape_of(bundle_rows, width), None)],
-        flops=2 * count * width * (3 * ffn + width),
-    )
-    bundle_sum = summed_half(bundle.reshape(2, bundle_rows // 2, width))
-
-    after_lane = (jnp.arange(PAIR) < HALF_WINDOW)[None, None]
-    lse_edge = jnp.where(after_lane, lse_after, lse_before)
-    sum_edge = jnp.where(after_lane, sum_after, sum_before)
-    half = (1, HALF_WINDOW, width)
-    heads = (1, HEAD_ROWS, PAIR)
-    (grad_qkv_all,) = run(
-        attend_back_kernel,
-        num_seqs,
-        [
-            (query, wide, per_seq),
-            (keys, wide, per_seq),
-            (values, wide, per_seq),
-            (grad_mixed.reshape(num_seqs, rows, width), (1, rows, width), per_seq),
-            (do_before, half, per_seq),
-            (do_after, half, per_seq),
-            (log_total, heads, per_seq),
-            (lse_edge, heads, per_seq),
-            (inner_sum, heads, per_seq),
-            (sum_edge, heads, per_seq),
-            (bias_t, (1, span, rows), per_seq),
-            (bias_edge, (1, rows, PAIR), per_seq),
-            (cosine, (1, span, PAIR), per_seq),
-            (sine, (1, span, PAIR), per_seq),
-        ],
-        [(shape_of(num_seqs, rows, 3 * width), (1, rows, 3 * width), per_seq)],
-        flops=2 * num_seqs * (width // PAIR) * 7 * 256 * 256 * 128,
-    )
-    flat_grad = grad_qkv_all.reshape(count, 3 * width)
-    (grad_qkv,) = run(
-        grad_qkv_kernel,
-        3,
-        [
-            (hidden_one.reshape(count, width), None),
-            (flat_grad, (count, width), column_block),
-        ],
-        [(shape_of(width, 3 * width), (width, width), column_block)],
-        flops=2 * count * width * 3 * width,
-    )
-    qkv_sum = summed_half(grad_qkv.reshape(2, width // 2, 3 * width))
+        [(bundle_part, None), (bundle_part, None)],
+        [pltpu.VMEM((2 * bundle_rows, width), bf16)],
+    )
+    do_before, do_after, send = together(do_before, do_after, send)
+    chain_mlp = Chain(sum_stages(place, keep, send))
+    heads = (1, 2 * HEAD_ROWS, PAIR)
+    half_part = (1, HALF_WINDOW, width)
+    edge_pack = (1, HEAD_ROWS, width)
+
+    wider = 3 * width + 2 * PAIR
+
+    def back_part(first, many, later, earlier=None):
+        def at(i):
+            return (first + i, 0, 0)
+
+        def pack_rows(i):
+            return (first + i, HALF_WINDOW // HEAD_ROWS, 0)
+
+        return run(
+            attend_back_kernel,
+            many,
+            [
+                (query, wide, at),
+                (keys, wide, at),
+                (values, wide, at),
+                (grad_mixed.reshape(num_seqs, rows, width), (1, rows, width), at),
+                (do_before, half_part, at),
+                (do_after, half_part, at),
+                (inner_sum, heads, at),
+                (do_before, edge_pack, pack_rows),
+                (do_after, edge_pack, pack_rows),
+                (bias_t, (1, span, rows), at),
+                (bias_edge, (1, rows, PAIR), at),
+                (cosine, (1, span, PAIR), at),
+                (sine, (1, span, PAIR), at),
+                *([] if earlier is None else [(earlier, pl.ANY)]),
+            ],
+            [
+                (shape_of(num_seqs, rows, wider), (1, rows, wider), at),
+                (shape_of(8, PAIR, dtype=f32), None),
+            ],
+            aliases=None if earlier is None else {13: 0},
+            later=later,
+        )
+
+    few = num_seqs // 2
+    grads, mark = back_part(0, few, ())
+    grads, _ = back_part(few, num_seqs - few, chain_mlp.advance(mark), grads)
+    flat_grad = grads.reshape(count, wider)
+    large = 4 * rows
     grad_tokens, gain_sum_one = run(
         stream_back_kernel,
-        count // step,
+        count // large,
         [
             (place, None),
-            (flat_grad, (step, 3 * width), row_block),
-            (flat_tokens, tok_block, row_block),
-            (grad_stream, tok_block, row_block),
+            (flat_grad, (large, 3 * width), row_block),
+            (flat_tokens, (large, width), row_block),
+            (grad_stream, (large, width), row_block),
             (gains, None),
             *qkv_pieces,
         ],
         [
-            (shape_of(count, width), tok_block, row_block),
+            (shape_of(count, width), (large, width), row_block),
             (shape_of(8, width, dtype=f32), None),
         ],
         [pltpu.VMEM((width, 3 * width), bf16)],
-        flops=2 * count * width * 3 * width,
-    )
-    gain_sums = summed_small(jnp.stack([jnp.sum(gain_sum_one, 0), jnp.sum(gain_sum_two, 0)]))
-    gain_width = norm_gains.shape[1]
-    part = in_weight.shape[0]
-    in_sum = jnp.concatenate([bundle_sum[i * part : (i + 1) * part] for i in range(3)], 1)
-    down_rows = down_weight.shape[0]
-    down_sum = bundle_sum[3 * part : 3 * part + down_rows]
-    out_sum = bundle_sum[3 * part + down_rows : 4 * part + down_rows]
+    )
+    sent = chain_mlp.advance(gain_sum_one)
+    step_columns = wider // 2
+    part = shape_of(2, width // 4, wider)
+    block = (2, width // 4, step_columns)
+
+    def last_block(i):
+        return (0, 0, i)
+
+    keep, send = run(
+        grad_qkv_kernel,
+        wider // step_columns,
+        [
+            (place, None),
+            (hidden_one.reshape(count, width), None),
+            (flat_grad, (count, step_columns), column_block),
+            (gain_sum_one, None),
+            (gain_sum_two, None),
+        ],
+        [(part, block, last_block), (part, block, last_block)],
+        [pltpu.VMEM((width, step_columns), bf16)],
+        later=sent,
+    )
+    send, *chain_mlp.got = together(send, *chain_mlp.got)
+    chain_qkv = Chain(sum_stages(place, keep, send))
+    sent = chain_mlp.advance()
+    sent = chain_qkv.advance(sent, gate=chain_mlp, arrived=2)
+    sent = chain_mlp.advance(sent)
+    sent = chain_qkv.advance(sent)
+    while chain_mlp.result is None:
+        sent = chain_qkv.advance(sent)
+        sent = chain_mlp.advance(sent)
+    in_sum, down_sum, out_sum = run(
+        finish_three_kernel,
+        1,
+        [(place, None), *[(x, None) for x in chain_mlp.result]],
+        [
+            (shape_of(*in_weight.shape, dtype=f32), None),
+            (shape_of(*down_weight.shape, dtype=f32), None),
+            (shape_of(*out_weight.shape, dtype=f32), None),
+        ],
+        [pltpu.VMEM((bundle_rows, width), bf16)],
+        later=sent,
+    )
+    sent = down_sum
+    while chain_qkv.result is None:
+        sent = chain_qkv.advance(sent)
+    qkv_sum, gains_sum = run(
+        finish_qkv_kernel,
+        1,
+        [(place, None), *[(x, None) for x in chain_qkv.result]],
+        [
+            (shape_of(*qkv_weight.shape, dtype=f32), None),
+            (shape_of(*norm_gains.shape, dtype=f32), None),
+        ],
+        [pltpu.VMEM((qkv_weight.shape[0], PAIR), f32)],
+    )
     return (
         layer_out.reshape(tokens.shape),
         grad_tokens.reshape(tokens.shape),
-        qkv_sum.astype(f32),
-        out_sum.astype(f32),
-        in_sum.astype(f32),
-        down_sum.astype(f32),
-        lax.dynamic_slice_in_dim(gain_sums, own_y * gain_width, gain_width, 1),
+        qkv_sum,
+        out_sum,
+        in_sum,
+        down_sum,
+        gains_sum,
     )
 
 

time: 350 us -> 303 us (0.87); the launches traced: 344 us -> 302 us
  Pallas kernels: 105 us -> 160 us
  waiting for transfers between devices: 110 us -> 55.8 us
  other arithmetic: 43.6 us -> 15.5 us
  starting transfers between devices: 70.7 us -> 52.6 us
  local copies, waits for them, and re-layouts: 13.1 us -> 17.6 us
    pallas_call x6 -> x23, Pallas kernels: 105 us -> 160 us  [run(): pl.pallas_call(body, grid=(grid,), in_specs=specs, out_specs=out_specs, o...]
    ppermute x41 -> x24, waiting for transfers between devices: 85.8 us -> 54.8 us  [the longest x22 49.9 us: exchange(): lax.ppermute(block, 'seq', flip_route(lax.axis_size('seq'), distance))]
    select_n x14 -> x0, other arithmetic: 14.5 us -> none  [the longest x13 13.8 us: summed_half(): jnp.where(bit == 0, jnp.concatenate([p, g], 0), jnp.concatenate([g, p], 0))]
    ppermute x5 -> x6, waiting for transfers between devices: 14.8 us -> 0.97 us  [exchange(): return lax.ppermute(block, 'fsdp', flip_route(2, 1))]
    ppermute x8 -> x4, starting transfers between devices: 19.5 us -> 6.2 us  [passed_along(): return lax.ppermute(block, axis, route)]
    unnamed x34 -> x96, local copies, waits for them, and re-layouts: 4.54 us -> 16.8 us
    convert_element_type x17 -> x0, other arithmetic: 12.2 us -> none  [the longest x14 5.27 us: reduce_stage(): (keep.astype(jnp.float32) + got.astype(jnp.float32)).astype(jnp.bfloat16)]
    ppermute x8 -> x4, waiting for transfers between devices: 9.63 us -> 0.01 us  [passed_along(): return lax.ppermute(block, axis, route)]
  transfers between devices with their start and end apart: 54 -> 34, of which waited for: 27 -> 18; matrix products, arithmetic and copies ran while one was open for 9% -> 5% of each run, Pallas kernels for 15% -> 35%
where the time goes in v3:
time: 303 us; the launch traced here: 302 us
  Pallas kernels  160 us (53%)
  waiting for transfers between devices  55.8 us (18%)
  starting transfers between devices  52.6 us (17%)
  local copies, waits for them, and re-layouts  17.6 us (6%)
  other arithmetic  15.5 us (5%)
    pallas_call x23, Pallas kernels, run(): pl.pallas_call(body, grid=(grid,), in_specs=specs, out_specs=out_specs, o...  160 us
    ppermute x22, waiting for transfers between devices, exchange(): lax.ppermute(block, 'seq', flip_route(lax.axis_size('seq'), distance))  49.9 us
    ppermute x22, starting transfers between devices, exchange(): lax.ppermute(block, 'seq', flip_route(lax.axis_size('seq'), distance))  36.1 us
    unnamed x96, local copies, waits for them, and re-layouts  16.8 us
    ppermute x6, starting transfers between devices, exchange(): return lax.ppermute(block, 'fsdp', flip_route(2, 1))  7.4 us
    ppermute x4, starting transfers between devices, passed_along(): return lax.ppermute(block, axis, route)  6.2 us
  transfers between devices with their start and end apart: 34, of which 18 were waited for; matrix products, arithmetic and copies ran while one was open for 5% of the time, Pallas kernels for 35%

profile of v3, /device:TPU:0, one launch (start us, length us, event | category | flops | bytes accessed | tf_op | source)
XLA Modules:
  0.0 302.1 jit_solution(7359636976069034740)
XLA Ops:
  3.7 3.0 collective-permute-start.1
  6.7 4.2 %shard_map.136 = (bf16[352,2304]{1,0:T(8,128)(2,1)}, bf16[8,64,768]{2,1,0:T(8,128)(2,1)}, bf16[8,64,768]{2,1,0:T(8,128)(2,1)}) custom-call(s32[5]{0:T(128)} %stack.19.refs_0_, bf16[384,768]{1,0:T(8,128)(2,1)} %refs_6_.1, bf16[384,2304]{1,0:T(8,128)(2,1)} %refs_7_.1, bf16[576,768]{1,0:T(8,128)(2,1)} %refs_8_.3, bf16[8,128,768]{2,1,0:T(8,128)(2,1)} %refs_2_.5, ...), custom_call_target="tpu_custom_call" | custom-call | flops 1 | bytes 1 | tf_op jit(solution)/shard_map/pallas_call | solution.py:510
  17.4 4.3 %fusion = (f32[8,256,32]{2,1,0:T(8,128)S(1)}, f32[8,256,32]{2,1,0:T(8,128)S(1)}, f32[8,256,32]{2,1,0:T(8,128)S(1)}) fusion(f32[32]{0:T(128)} %negate_power_fusion, f32[8,256]{1,0:T(8,128)S(1)} %convert_element_type.3), kind=kLoop, calls=%fused_computation.7 | loop fusion | flops 131072 | bytes 794752 | tf_op jit(solution)/shard_map/neg | solution.py:674
  23.2 3.0 pad_maximum_fusion
  36.1 26.5 %shard_map.137 = (bf16[8,128,768]{2,1,0:T(8,128)(2,1)}, bf16[8,256,768]{2,1,0:T(8,128)(2,1)}, bf16[8,256,768]{2,1,0:T(8,128)(2,1)}, bf16[8,256,768]{2,1,0:T(8,12...) custom-call(s32[5]{0:T(128)} %stack.19.refs_0_, bf16[8,64,768]{2,1,0:T(8,128)(2,1)} %copy-done.15, ...), custom_call_target="tpu_custom_call" | custom-call | flops 1 | bytes 1 | tf_op jit(solution)/shard_map/pallas_call | solution.py:510
  63.1 3.3 %collective-permute-done.5.refs_10_ = bf16[352,2304]{1,0:T(8,128)(2,1)S(1)} collective-permute-done((bf16[352,2304]{1,0:T(8,128)(2,1)S(1)}, bf16[352,2304]{1,0:T(8,128)(2,1)S(1)}, u32[]{:S(2)}, u32[]{:S(2)}) %collective-permute-start.5) | collective-permute-done | bytes 1622048 | tf_op jit(solution)/shard_map/ppermute | solution.py:530
  67.5 27.3 %shard_map.138 = (bf16[1024,768]{1,0:T(8,128)(2,1)}, f32[1024,768]{1,0:T(8,128)}, bf16[1024,768]{1,0:T(8,128)(2,1)}, bf16[8,80,768]{2,1,0:T(8,128)(2,1)}, bf16[8...) custom-call(s32[5]{0:T(128)} %stack.19.refs_0_, ...), custom_call_target="tpu_custom_call" | custom-call | flops 1 | bytes 1 | tf_op jit(solution)/shard_map/pallas_call | solution.py:510
  98.3 14.9 %shard_map.139 = (bf16[2,1088,768]{2,1,0:T(8,128)(2,1)}, bf16[2,1088,768]{2,1,0:T(8,128)(2,1)}) custom-call(s32[5]{0:T(128)} %stack.19.refs_0_, bf16[1024,768]{1,0:T(8,128)(2,1)} %get-tuple-element.103.refs_1_, bf16[1024,2304]{1,0:T(8,128)(2,1)} %get-tuple-element.104.refs_2_, bf16[1024,1152]{1,0:T(8,128)(2,1)} %get-tuple-element.105.refs_3_, ...), custom_call_target="tpu_custom_call" | custom-call | flops 1 | bytes 1 | tf_op jit(solution)/shard_map/pallas_call | solution.py:510
  113.2 8.0 %collective-permute-start.8 = (bf16[2,1088,768]{2,1,0:T(8,128)(2,1)}, bf16[2,1088,768]{2,1,0:T(8,128)(2,1)S(1)}, u32[]{:S(2)}, u32[]{:S(2)}) collective-permute-start(bf16[2,1088,768]{2,1,0:T(8,128)(2,1)} %get-tuple-element.115), channel_id=1, source_target_pairs={{0,2},{2,0},{4,6},{6,4},{8,10},{10,8},{12,14},{14,12},{16,18},{18,... | collective-permute-start | bytes 10027016 | tf_op jit(solution)/shard_map/ppermute | solution.py:536
  121.2 11.0 %shard_map.140 = (bf16[8,128,2560]{2,1,0:T(8,128)(2,1)}, f32[8,128]{1,0:T(8,128)}) custom-call(bf16[8,256,768]{2,1,0:T(8,128)(2,1)} %get-tuple-element.97.refs_0_, bf16[8,256,768]{2,1,0:T(8,128)(2,1)} %get-tuple-element.98.refs_1_, bf16[8,256,768]{2,1,0:T(8,128)(2,1)} %get-tuple-element.99.refs_2_, bf16[8,128,768]{2,1,0:T(8,128)(2,1)} %bitcast.45, ...), custom_call_target="tpu_custom_call" | custom-call | flops 1 | bytes 1 | tf_op jit(solution)/shard_map/pallas_call | solution.py:510
  133.9 5.1 %shard_map.141 = (bf16[2,544,384]{2,1,0:T(8,128)(2,1)}, bf16[2,544,384]{2,1,0:T(8,128)(2,1)}, bf16[2,544,384]{2,1,0:T(8,128)(2,1)}, bf16[2,544,384]{2,1,0:T(8,128)(2,1)}) custom-call(s32[5]{0:T(128)} %stack.19.refs_0_, bf16[4,544,768]{2,1,0:T(8,128)(2,1)} %bitcast.53, bf16[4,544,768]{2,1,0:T(8,128)(2,1)} %bitcast.54, f32[8,128]{1,0:T(8,128)} %get-tuple-element.116.refs_3_), custom_call_target="tpu_custom_call" | custom-call | flops 1 | bytes 1 | tf_op jit(solution)/shard_map/pallas_call | solution.py:510
  140.0 3.5 %collective-permute-start.10 = (bf16[2,544,384]{2,1,0:T(8,128)(2,1)}, bf16[2,544,384]{2,1,0:T(8,128)(2,1)S(1)}, u32[]{:S(2)}, u32[]{:S(2)}) collective-permute-start(bf16[2,544,384]{2,1,0:T(8,128)(2,1)} %get-tuple-element.118.refs_15_), channel_id=1, source_target_pairs={{0,4},{2,6},{4,0},{6,2},{8,12},{10,14},{12,8},{14,10},{16,20},{18,... | collective-permute-start | bytes 2506760 | tf_op jit(solution)/shard_map/ppermute | solution.py:536
  143.5 11.0 %shard_map.142 = (bf16[8,128,2560]{2,1,0:T(8,128)(2,1)}, f32[8,128]{1,0:T(8,128)}) custom-call(bf16[8,256,768]{2,1,0:T(8,128)(2,1)} %get-tuple-element.97.refs_0_, bf16[8,256,768]{2,1,0:T(8,128)(2,1)} %get-tuple-element.98.refs_1_, bf16[8,256,768]{2,1,0:T(8,128)(2,1)} %get-tuple-element.99.refs_2_, ...), custom_call_target="tpu_custom_call", output_to_operand_aliasing={{0}: (13, {})} | custom-call | flops 1 | bytes 1 | tf_op jit(solution)/shard_map/pallas_call | solution.py:510
  154.5 10.0 %shard_map.143 = (bf16[1024,768]{1,0:T(8,128)(2,1)}, f32[8,768]{1,0:T(8,128)}) custom-call(s32[5]{0:T(128)} %stack.19.refs_0_, bf16[1024,2560]{1,0:T(8,128)(2,1)} %bitcast.34, bf16[1024,768]{1,0:T(8,128)(2,1)} %bitcast.41, f32[1024,768]{1,0:T(8,128)} %get-tuple-element.120.refs_3_, bf16[2,768]{1,0:T(2,128)(2,1)} %broadcast_select_fusion.refs_7_.refs_5_.refs_4_, ...), custom_call_target="tpu_custom_call" | custom-call | flops 1 | bytes 1 | tf_op jit(solution)/shard_map/pallas_call | solution.py:510
  165.6 3.3 %shard_map.144 = (bf16[544,768]{1,0:T(8,128)(2,1)}, bf16[544,384]{1,0:T(8,128)(2,1)}, bf16[544,384]{1,0:T(8,128)(2,1)}) custom-call(s32[5]{0:T(128)} %stack.19.refs_0_, bf16[2,544,384]{2,1,0:T(8,128)(2,1)} %get-tuple-element.125.refs_1_, bf16[2,544,384]{2,1,0:T(8,128)(2,1)} %copy-done.12, bf16[2,544,384]{2,1,0:T(8,128)(2,1)} %get-tuple-element.126.refs_3_, ...), custom_call_target="tpu_custom_call" | custom-call | flops 1 | bytes 1 | tf_op jit(solution)/shard_map/pallas_call | solution.py:510
  169.9 8.8 %shard_map.145 = (bf16[2,192,2560]{2,1,0:T(8,128)(2,1)}, bf16[2,192,2560]{2,1,0:T(8,128)(2,1)}) custom-call(s32[5]{0:T(128)} %stack.19.refs_0_, bf16[1024,768]{1,0:T(8,128)(2,1)} %bitcast.59, bf16[1024,2560]{1,0:T(8,128)(2,1)} %bitcast.35, f32[8,768]{1,0:T(8,128)} %get-tuple-element.123.refs_5_.refs_3_, f32[8,768]{1,0:T(8,128)} %get-tuple-element.124.refs_4_, ...), custom_call_target="tpu_custom_call" | custom-call | flops 1 | bytes 1 | tf_op jit(solution)/shard_map/pallas_call | solution.py:510
  182.7 3.6 %collective-permute-start.14 = (bf16[136,768]{1,0:T(8,128)(2,1)}, bf16[136,768]{1,0:T(8,128)(2,1)S(1)}, u32[]{:S(2)}, u32[]{:S(2)}) collective-permute-start(bf16[136,768]{1,0:T(8,128)(2,1)} %get-tuple-element.135.refs_3_), channel_id=1, source_target_pairs={{0,8},{2,10},{4,12},{6,14},{8,0},{10,2},{12,4},{14,6},{16,24},{18,... | collective-permute-start | bytes 626696 | tf_op jit(solution)/shard_map/ppermute | solution.py:536
  190.2 4.3 %shard_map.147 = (bf16[2,96,1280]{2,1,0:T(8,128)(2,1)}, bf16[2,96,1280]{2,1,0:T(8,128)(2,1)}, bf16[2,96,1280]{2,1,0:T(8,128)(2,1)}, bf16[2,96,1280]{2,1,0:T(8,128)(2,1)}) custom-call(s32[5]{0:T(128)} %stack.19.refs_0_, bf16[4,96,2560]{2,1,0:T(8,128)(2,1)} %bitcast.55, bf16[4,96,2560]{2,1,0:T(8,128)(2,1)} %bitcast.56, ...), custom_call_target="tpu_custom_call" | custom-call | flops 1 | bytes 1 | tf_op jit(solution)/shard_map/pallas_call | solution.py:510
  201.9 5.2 %collective-permute-done.18 = bf16[136,768]{1,0:T(8,128)(2,1)S(1)} collective-permute-done((bf16[136,768]{1,0:T(8,128)(2,1)S(1)}, bf16[136,768]{1,0:T(8,128)(2,1)S(1)}, u32[]{:S(2)}, u32[]{:S(2)}) %collective-permute-start.18) | collective-permute-done | bytes 208928 | tf_op jit(solution)/shard_map/ppermute | solution.py:536
  210.8 3.3 %shard_map.149 = (bf16[96,2560]{1,0:T(8,128)(2,1)}, bf16[96,1280]{1,0:T(8,128)(2,1)}, bf16[96,1280]{1,0:T(8,128)(2,1)}) custom-call(s32[5]{0:T(128)} %stack.19.refs_0_, bf16[2,96,1280]{2,1,0:T(8,128)(2,1)} %get-tuple-element.138.refs_1_, bf16[2,96,1280]{2,1,0:T(8,128)(2,1)} %copy-done.21, bf16[2,96,1280]{2,1,0:T(8,128)(2,1)} %get-tuple-element.142.refs_3_, ...), custom_call_target="tpu_custom_call" | custom-call | flops 1 | bytes 1 | tf_op jit(solution)/shard_map/pallas_call | solution.py:510
  227.3 8.7 %collective-permute-done.25.refs_3_ = bf16[136,768]{1,0:T(8,128)(2,1)S(1)} collective-permute-done((bf16[136,768]{1,0:T(8,128)(2,1)S(1)}, bf16[136,768]{1,0:T(8,128)(2,1)S(1)}, u32[]{:S(2)}, u32[]{:S(2)}) %collective-permute-start.25) | collective-permute-done | bytes 208928 | tf_op jit(solution)/shard_map/ppermute | solution.py:536
  236.7 3.0 shard_map.151
  245.3 6.3 %collective-permute-done.22 = bf16[24,2560]{1,0:T(8,128)(2,1)S(1)} collective-permute-done((bf16[24,2560]{1,0:T(8,128)(2,1)S(1)}, bf16[24,2560]{1,0:T(8,128)(2,1)S(1)}, u32[]{:S(2)}, u32[]{:S(2)}) %collective-permute-start.22) | collective-permute-done | bytes 122912 | tf_op jit(solution)/shard_map/ppermute | solution.py:536
  254.1 5.3 %collective-permute-done.30.refs_2_ = bf16[544,768]{1,0:T(8,128)(2,1)S(1)} collective-permute-done((bf16[544,768]{1,0:T(8,128)(2,1)}, bf16[544,768]{1,0:T(8,128)(2,1)S(1)}, u32[]{:S(2)}, u32[]{:S(2)}) %collective-permute-start.30) | collective-permute-done | bytes 835616 | tf_op jit(solution)/shard_map/ppermute | solution.py:536
  260.3 3.4 %shard_map.153 = bf16[2,544,768]{2,1,0:T(8,128)(2,1)} custom-call(s32[5]{0:T(128)} %stack.19.refs_0_, bf16[544,768]{1,0:T(8,128)(2,1)} %bitcast.44, bf16[544,768]{1,0:T(8,128)(2,1)} %copy-done.14, bf16[24,2560]{1,0:T(8,128)(2,1)} %shard_map.152.refs_3_.refs_4_.refs_5_.refs_1_, bf16[24,2560]{1,0:T(8,128)(2,1)} %shard_map.152.refs_3_.refs_4_.refs_5_.refs_1_, ...), custom_call_target="tpu_custom_call" | custom-call | flops 1 | bytes 1 | tf_op jit(solution)/shard_map/pallas_call | solution.py:510
  263.9 4.3 %collective-permute-start.27 = (bf16[24,2560]{1,0:T(8,128)(2,1)S(1)}, bf16[24,2560]{1,0:T(8,128)(2,1)S(1)}, u32[]{:S(2)}, u32[]{:S(2)}) collective-permute-start(bf16[24,2560]{1,0:T(8,128)(2,1)S(1)} %copy-done.6), channel_id=1, source_target_pairs={{0,8},{2,10},{4,12},{6,14},{8,0},{10,2},{12,4},{14,6},{16,24},{18,... | collective-permute-start | bytes 368648 | tf_op jit(solution)/shard_map/ppermute | solution.py:536
  268.2 3.7 %collective-permute-done.29.refs_4_ = bf16[24,2560]{1,0:T(8,128)(2,1)S(1)} collective-permute-done((bf16[24,2560]{1,0:T(8,128)(2,1)S(1)}, bf16[24,2560]{1,0:T(8,128)(2,1)S(1)}, u32[]{:S(2)}, u32[]{:S(2)}) %collective-permute-start.29) | collective-permute-done | bytes 122912 | tf_op jit(solution)/shard_map/ppermute | solution.py:536
  271.9 3.8 %collective-permute-done.28.refs_3_ = bf16[24,2560]{1,0:T(8,128)(2,1)S(1)} collective-permute-done((bf16[24,2560]{1,0:T(8,128)(2,1)S(1)}, bf16[24,2560]{1,0:T(8,128)(2,1)S(1)}, u32[]{:S(2)}, u32[]{:S(2)}) %collective-permute-start.28) | collective-permute-done | bytes 122912 | tf_op jit(solution)/shard_map/ppermute | solution.py:536
  280.4 5.0 %shard_map.155 = (f32[384,2304]{1,0:T(8,128)}, f32[576,768]{1,0:T(8,128)}, f32[384,768]{1,0:T(8,128)}) custom-call(s32[5]{0:T(128)} %stack.19.refs_0_, bf16[1088,768]{1,0:T(8,128)(2,1)} %bitcast.38, bf16[1088,768]{1,0:T(8,128)(2,1)} %copy-done.8, bf16[1088,768]{1,0:T(8,128)(2,1)} %bitcast.39), custom_call_target="tpu_custom_call" | custom-call | flops 1 | bytes 1 | tf_op jit(solution)/shard_map/pallas_call | solution.py:510
  285.5 6.3 %collective-permute-done.31.refs_2_ = bf16[96,2560]{1,0:T(8,128)(2,1)S(1)} collective-permute-done((bf16[96,2560]{1,0:T(8,128)(2,1)}, bf16[96,2560]{1,0:T(8,128)(2,1)S(1)}, u32[]{:S(2)}, u32[]{:S(2)}) %collective-permute-start.31) | collective-permute-done | bytes 491552 | tf_op jit(solution)/shard_map/ppermute | solution.py:536
  294.8 2.8 collective-permute-done.33.refs_2_
  298.5 3.6 %shard_map.157 = (f32[384,2304]{1,0:T(8,128)}, f32[2,384]{1,0:T(2,128)}) custom-call(s32[5]{0:T(128)} %stack.19.refs_0_, bf16[192,2560]{1,0:T(8,128)(2,1)} %bitcast.52, bf16[192,2560]{1,0:T(8,128)(2,1)} %copy-done.11), custom_call_target="tpu_custom_call" | custom-call | flops 1 | bytes 1 | tf_op jit(solution)/shard_map/pallas_call | solution.py:510
  (181 shorter events, 81.4 us)
Async XLA Ops:
  3.7 25.7 %collective-permute-start.1 = (bf16[208,2304]{1,0:T(8,128)(2,1)}, bf16[208,2304]{1,0:T(8,128)(2,1)S(1)}, u32[]{:S(2)}, u32[]{:S(2)}) collective-permute-start(bf16[208,2304]{1,0:T(8,128)(2,1)} %shard_map.135.refs_5_), channel_id=1, source_target_pairs={{0,1},{1,0},{2,3},{3,2},{4,5},{5,4},{6,7},{7,6},{8,9},{9,8},{10,11... | collective-permute-start | bytes 2875400 | tf_op jit(solution)/shard_map/ppermute | solution.py:535
  10.9 18.5 %collective-permute-start.2 = (bf16[8,64,768]{2,1,0:T(8,128)(2,1)}, bf16[8,64,768]{2,1,0:T(8,128)(2,1)S(1)}, u32[]{:S(2)}, u32[]{:S(2)}) collective-permute-start(bf16[8,64,768]{2,1,0:T(8,128)(2,1)} %get-tuple-element.84), channel_id=1, source_target_pairs={{0,2},{2,4},{4,6},{6,8},{8,10},{10,12},{12,14},{14,16},{16,18},{18... | collective-permute-start | bytes 2359304 | tf_op jit(solution)/shard_map/ppermute | solution.py:28
  12.4 17.0 %collective-permute-start.3 = (bf16[8,64,768]{2,1,0:T(8,128)(2,1)}, bf16[8,64,768]{2,1,0:T(8,128)(2,1)}, u32[]{:S(2)}, u32[]{:S(2)}) collective-permute-start(bf16[8,64,768]{2,1,0:T(8,128)(2,1)} %get-tuple-element.85), channel_id=1, source_target_pairs={{2,0},{4,2},{6,4},{8,6},{10,8},{12,10},{14,12},{16,14},{18,16},{20... | collective-permute-start | bytes 2359304 | tf_op jit(solution)/shard_map/ppermute | solution.py:28
  13.7 49.2 %collective-permute-start = (bf16[352,2304]{1,0:T(8,128)(2,1)}, bf16[352,2304]{1,0:T(8,128)(2,1)S(1)}, u32[]{:S(2)}, u32[]{:S(2)}) collective-permute-start(bf16[352,2304]{1,0:T(8,128)(2,1)} %get-tuple-element.83), channel_id=1, source_target_pairs={{0,1},{1,0},{2,3},{3,2},{4,5},{5,4},{6,7},{7,6},{8,9},{9,8},{10,11... | collective-permute-start | bytes 4866056 | tf_op jit(solution)/shard_map/ppermute | solution.py:535
  30.3 4.9 %collective-permute-start.4 = (bf16[208,2304]{1,0:T(8,128)(2,1)S(1)}, bf16[208,2304]{1,0:T(8,128)(2,1)S(1)}, u32[]{:S(2)}, u32[]{:S(2)}) collective-permute-start(bf16[208,2304]{1,0:T(8,128)(2,1)S(1)} %collective-permute-done.1.refs_9_.refs_6_), channel_id=1, source_target_pairs={{0,2},{2,0},{4,6},{6,4},{8,10},{10,8},{12,14},{14,12},{16,18},{18,... | collective-permute-start | bytes 2875400 | tf_op jit(solution)/shard_map/ppermute | solution.py:530
  94.8 18.3 %collective-permute-start.6 = (bf16[8,80,768]{2,1,0:T(8,128)(2,1)}, bf16[8,80,768]{2,1,0:T(8,128)(2,1)S(1)}, u32[]{:S(2)}, u32[]{:S(2)}) collective-permute-start(bf16[8,80,768]{2,1,0:T(8,128)(2,1)} %get-tuple-element.101), channel_id=1, source_target_pairs={{0,2},{2,4},{4,6},{6,8},{8,10},{10,12},{12,14},{14,16},{16,18},{18... | collective-permute-start | bytes 2949128 | tf_op jit(solution)/shard_map/ppermute | solution.py:28
  97.0 16.2 %collective-permute-start.7 = (bf16[8,80,768]{2,1,0:T(8,128)(2,1)}, bf16[8,80,768]{2,1,0:T(8,128)(2,1)S(1)}, u32[]{:S(2)}, u32[]{:S(2)}) collective-permute-start(bf16[8,80,768]{2,1,0:T(8,128)(2,1)} %get-tuple-element.102), channel_id=1, source_target_pairs={{2,0},{4,2},{6,4},{8,6},{10,8},{12,10},{14,12},{16,14},{18,16},{20... | collective-permute-start | bytes 2949128 | tf_op jit(solution)/shard_map/ppermute | solution.py:28
  113.2 19.0 %collective-permute-start.8 = (bf16[2,1088,768]{2,1,0:T(8,128)(2,1)}, bf16[2,1088,768]{2,1,0:T(8,128)(2,1)S(1)}, u32[]{:S(2)}, u32[]{:S(2)}) collective-permute-start(bf16[2,1088,768]{2,1,0:T(8,128)(2,1)} %get-tuple-element.115), channel_id=1, source_target_pairs={{0,2},{2,0},{4,6},{6,4},{8,10},{10,8},{12,14},{14,12},{16,18},{18,... | collective-permute-start | bytes 10027016 | tf_op jit(solution)/shard_map/ppermute | solution.py:536
  139.0 25.5 %collective-permute-start.9 = (bf16[2,544,384]{2,1,0:T(8,128)(2,1)}, bf16[2,544,384]{2,1,0:T(8,128)(2,1)S(1)}, u32[]{:S(2)}, u32[]{:S(2)}) collective-permute-start(bf16[2,544,384]{2,1,0:T(8,128)(2,1)} %get-tuple-element.117.refs_14_), channel_id=1, source_target_pairs={{0,1},{1,0},{2,3},{3,2},{4,5},{5,4},{6,7},{7,6},{8,9},{9,8},{10,11... | collective-permute-start | bytes 2506760 | tf_op jit(solution)/shard_map/ppermute | solution.py:535
  140.0 24.5 %collective-permute-start.10 = (bf16[2,544,384]{2,1,0:T(8,128)(2,1)}, bf16[2,544,384]{2,1,0:T(8,128)(2,1)S(1)}, u32[]{:S(2)}, u32[]{:S(2)}) collective-permute-start(bf16[2,544,384]{2,1,0:T(8,128)(2,1)} %get-tuple-element.118.refs_15_), channel_id=1, source_target_pairs={{0,4},{2,6},{4,0},{6,2},{8,12},{10,14},{12,8},{14,10},{16,20},{18,... | collective-permute-start | bytes 2506760 | tf_op jit(solution)/shard_map/ppermute | solution.py:536
  168.9 10.5 %collective-permute-start.11 = (bf16[544,384]{1,0:T(8,128)(2,1)}, bf16[544,384]{1,0:T(8,128)(2,1)S(1)}, u32[]{:S(2)}, u32[]{:S(2)}) collective-permute-start(bf16[544,384]{1,0:T(8,128)(2,1)} %get-tuple-element.127.refs_5_), channel_id=1, source_target_pairs={{0,4},{2,6},{4,0},{6,2},{8,12},{10,14},{12,8},{14,10},{16,20},{18,... | collective-permute-start | bytes 1253384 | tf_op jit(solution)/shard_map/ppermute | solution.py:536
  168.9 10.7 %collective-permute-start.12 = (bf16[544,384]{1,0:T(8,128)(2,1)}, bf16[544,384]{1,0:T(8,128)(2,1)S(1)}, u32[]{:S(2)}, u32[]{:S(2)}) collective-permute-start(bf16[544,384]{1,0:T(8,128)(2,1)} %get-tuple-element.128.refs_6_), channel_id=1, source_target_pairs={{0,1},{1,0},{2,3},{3,2},{4,5},{5,4},{6,7},{7,6},{8,9},{9,8},{10,11... | collective-permute-start | bytes 1253384 | tf_op jit(solution)/shard_map/ppermute | solution.py:535
  179.6 9.4 %collective-permute-start.13 = (bf16[2,192,2560]{2,1,0:T(8,128)(2,1)}, bf16[2,192,2560]{2,1,0:T(8,128)(2,1)S(1)}, u32[]{:S(2)}, u32[]{:S(2)}) collective-permute-start(bf16[2,192,2560]{2,1,0:T(8,128)(2,1)} %get-tuple-element.131), channel_id=1, source_target_pairs={{0,2},{2,0},{4,6},{6,4},{8,10},{10,8},{12,14},{14,12},{16,18},{18,... | collective-permute-start | bytes 5898248 | tf_op jit(solution)/shard_map/ppermute | solution.py:536
  182.7 13.3 %collective-permute-start.14 = (bf16[136,768]{1,0:T(8,128)(2,1)}, bf16[136,768]{1,0:T(8,128)(2,1)S(1)}, u32[]{:S(2)}, u32[]{:S(2)}) collective-permute-start(bf16[136,768]{1,0:T(8,128)(2,1)} %get-tuple-element.135.refs_3_), channel_id=1, source_target_pairs={{0,8},{2,10},{4,12},{6,14},{8,0},{10,2},{12,4},{14,6},{16,24},{18,... | collective-permute-start | bytes 626696 | tf_op jit(solution)/shard_map/ppermute | solution.py:536
  186.4 12.2 %collective-permute-start.15 = (bf16[136,768]{1,0:T(8,128)(2,1)}, bf16[136,768]{1,0:T(8,128)(2,1)S(1)}, u32[]{:S(2)}, u32[]{:S(2)}) collective-permute-start(bf16[136,768]{1,0:T(8,128)(2,1)} %get-tuple-element.136.refs_4_), channel_id=1, source_target_pairs={{0,16},{2,18},{4,20},{6,22},{8,24},{10,26},{12,28},{14,30},{16,0},... | collective-permute-start | bytes 626696 | tf_op jit(solution)/shard_map/ppermute | solution.py:536
  198.6 11.3 %collective-permute-start.16 = (bf16[2,96,1280]{2,1,0:T(8,128)(2,1)}, bf16[2,96,1280]{2,1,0:T(8,128)(2,1)S(1)}, u32[]{:S(2)}, u32[]{:S(2)}) collective-permute-start(bf16[2,96,1280]{2,1,0:T(8,128)(2,1)} %get-tuple-element.141.refs_5_), channel_id=1, source_target_pairs={{0,1},{1,0},{2,3},{3,2},{4,5},{5,4},{6,7},{7,6},{8,9},{9,8},{10,11... | collective-permute-start | bytes 1474568 | tf_op jit(solution)/shard_map/ppermute | solution.py:535
  199.1 10.8 %collective-permute-start.17 = (bf16[2,96,1280]{2,1,0:T(8,128)(2,1)}, bf16[2,96,1280]{2,1,0:T(8,128)(2,1)S(1)}, u32[]{:S(2)}, u32[]{:S(2)}) collective-permute-start(bf16[2,96,1280]{2,1,0:T(8,128)(2,1)} %get-tuple-element.143.refs_6_), channel_id=1, source_target_pairs={{0,4},{2,6},{4,0},{6,2},{8,12},{10,14},{12,8},{14,10},{16,20},{18,... | collective-permute-start | bytes 1474568 | tf_op jit(solution)/shard_map/ppermute | solution.py:536
  199.4 7.7 %collective-permute-start.18 = (bf16[136,768]{1,0:T(8,128)(2,1)S(1)}, bf16[136,768]{1,0:T(8,128)(2,1)S(1)}, u32[]{:S(2)}, u32[]{:S(2)}) collective-permute-start(bf16[136,768]{1,0:T(8,128)(2,1)S(1)} %copy-done.35), channel_id=1, source_target_pairs={{0,24},{2,26},{4,28},{6,30},{8,16},{10,18},{12,20},{14,22},{16,8},... | collective-permute-start | bytes 626696 | tf_op jit(solution)/shard_map/ppermute | solution.py:536
  214.1 7.6 %collective-permute-start.19 = (bf16[96,1280]{1,0:T(8,128)(2,1)}, bf16[96,1280]{1,0:T(8,128)(2,1)S(1)}, u32[]{:S(2)}, u32[]{:S(2)}) collective-permute-start(bf16[96,1280]{1,0:T(8,128)(2,1)} %get-tuple-element.148.refs_4_), channel_id=1, source_target_pairs={{0,4},{2,6},{4,0},{6,2},{8,12},{10,14},{12,8},{14,10},{16,20},{18,... | collective-permute-start | bytes 737288 | tf_op jit(solution)/shard_map/ppermute | solution.py:536
  215.8 6.4 %collective-permute-start.20 = (bf16[96,1280]{1,0:T(8,128)(2,1)}, bf16[96,1280]{1,0:T(8,128)(2,1)S(1)}, u32[]{:S(2)}, u32[]{:S(2)}) collective-permute-start(bf16[96,1280]{1,0:T(8,128)(2,1)} %get-tuple-element.149.refs_5_), channel_id=1, source_target_pairs={{0,1},{1,0},{2,3},{3,2},{4,5},{5,4},{6,7},{7,6},{8,9},{9,8},{10,11... | collective-permute-start | bytes 737288 | tf_op jit(solution)/shard_map/ppermute | solution.py:535
  217.3 9.9 %collective-permute-start.26 = (bf16[136,768]{1,0:T(8,128)(2,1)S(1)}, bf16[136,768]{1,0:T(8,128)(2,1)S(1)}, u32[]{:S(2)}, u32[]{:S(2)}) collective-permute-start(bf16[136,768]{1,0:T(8,128)(2,1)S(1)} %copy-done.2), channel_id=1, source_target_pairs={{0,24},{2,26},{4,28},{6,30},{8,16},{10,18},{12,20},{14,22},{16,8},... | collective-permute-start | bytes 626696 | tf_op jit(solution)/shard_map/ppermute | solution.py:536
  219.8 16.1 %collective-permute-start.25 = (bf16[136,768]{1,0:T(8,128)(2,1)S(1)}, bf16[136,768]{1,0:T(8,128)(2,1)S(1)}, u32[]{:S(2)}, u32[]{:S(2)}) collective-permute-start(bf16[136,768]{1,0:T(8,128)(2,1)S(1)} %copy-done.2), channel_id=1, source_target_pairs={{0,16},{2,18},{4,20},{6,22},{8,24},{10,26},{12,28},{14,30},{16,0},... | collective-permute-start | bytes 626696 | tf_op jit(solution)/shard_map/ppermute | solution.py:536
  221.0 14.9 %collective-permute-start.24 = (bf16[136,768]{1,0:T(8,128)(2,1)S(1)}, bf16[136,768]{1,0:T(8,128)(2,1)S(1)}, u32[]{:S(2)}, u32[]{:S(2)}) collective-permute-start(bf16[136,768]{1,0:T(8,128)(2,1)S(1)} %copy-done.2), channel_id=1, source_target_pairs={{0,8},{2,10},{4,12},{6,14},{8,0},{10,2},{12,4},{14,6},{16,24},{18,... | collective-permute-start | bytes 626696 | tf_op jit(solution)/shard_map/ppermute | solution.py:536
  239.7 19.8 %collective-permute-start.30 = (bf16[544,768]{1,0:T(8,128)(2,1)}, bf16[544,768]{1,0:T(8,128)(2,1)S(1)}, u32[]{:S(2)}, u32[]{:S(2)}) collective-permute-start(bf16[544,768]{1,0:T(8,128)(2,1)} %bitcast.42), channel_id=1, source_target_pairs={{0,4},{2,6},{4,0},{6,2},{8,12},{10,14},{12,8},{14,10},{16,20},{18,... | collective-permute-start | bytes 2506760 | tf_op jit(solution)/shard_map/ppermute | solution.py:536
  240.0 5.3 %collective-permute-start.21 = (bf16[24,2560]{1,0:T(8,128)(2,1)S(1)}, bf16[24,2560]{1,0:T(8,128)(2,1)S(1)}, u32[]{:S(2)}, u32[]{:S(2)}) collective-permute-start(bf16[24,2560]{1,0:T(8,128)(2,1)S(1)} %copy-done.38), channel_id=1, source_target_pairs={{0,8},{2,10},{4,12},{6,14},{8,0},{10,2},{12,4},{14,6},{16,24},{18,... | collective-permute-start | bytes 368648 | tf_op jit(solution)/shard_map/ppermute | solution.py:536
  240.0 11.6 %collective-permute-start.22 = (bf16[24,2560]{1,0:T(8,128)(2,1)S(1)}, bf16[24,2560]{1,0:T(8,128)(2,1)S(1)}, u32[]{:S(2)}, u32[]{:S(2)}) collective-permute-start(bf16[24,2560]{1,0:T(8,128)(2,1)S(1)} %copy-done.37), channel_id=1, source_target_pairs={{0,16},{2,18},{4,20},{6,22},{8,24},{10,26},{12,28},{14,30},{16,0},... | collective-permute-start | bytes 368648 | tf_op jit(solution)/shard_map/ppermute | solution.py:536
  241.8 9.9 %collective-permute-start.23 = (bf16[24,2560]{1,0:T(8,128)(2,1)S(1)}, bf16[24,2560]{1,0:T(8,128)(2,1)S(1)}, u32[]{:S(2)}, u32[]{:S(2)}) collective-permute-start(bf16[24,2560]{1,0:T(8,128)(2,1)S(1)} %copy-done.36), channel_id=1, source_target_pairs={{0,24},{2,26},{4,28},{6,30},{8,16},{10,18},{12,20},{14,22},{16,8},... | collective-permute-start | bytes 368648 | tf_op jit(solution)/shard_map/ppermute | solution.py:536
  263.7 15.5 %collective-permute-start.32 = (bf16[1088,768]{1,0:T(8,128)(2,1)}, bf16[1088,768]{1,0:T(8,128)(2,1)S(1)}, u32[]{:S(2)}, u32[]{:S(2)}) collective-permute-start(bf16[1088,768]{1,0:T(8,128)(2,1)} %bitcast.36), channel_id=1, source_target_pairs={{0,2},{2,0},{4,6},{6,4},{8,10},{10,8},{12,14},{14,12},{16,18},{18,... | collective-permute-start | bytes 5013512 | tf_op jit(solution)/shard_map/ppermute | solution.py:536
  263.8 8.1 %collective-permute-start.29 = (bf16[24,2560]{1,0:T(8,128)(2,1)S(1)}, bf16[24,2560]{1,0:T(8,128)(2,1)S(1)}, u32[]{:S(2)}, u32[]{:S(2)}) collective-permute-start(bf16[24,2560]{1,0:T(8,128)(2,1)S(1)} %copy-done.6), channel_id=1, source_target_pairs={{0,24},{2,26},{4,28},{6,30},{8,16},{10,18},{12,20},{14,22},{16,8},... | collective-permute-start | bytes 368648 | tf_op jit(solution)/shard_map/ppermute | solution.py:536
  263.8 11.9 %collective-permute-start.28 = (bf16[24,2560]{1,0:T(8,128)(2,1)S(1)}, bf16[24,2560]{1,0:T(8,128)(2,1)S(1)}, u32[]{:S(2)}, u32[]{:S(2)}) collective-permute-start(bf16[24,2560]{1,0:T(8,128)(2,1)S(1)} %copy-done.6), channel_id=1, source_target_pairs={{0,16},{2,18},{4,20},{6,22},{8,24},{10,26},{12,28},{14,30},{16,0},... | collective-permute-start | bytes 368648 | tf_op jit(solution)/shard_map/ppermute | solution.py:536
  263.9 11.8 %collective-permute-start.27 = (bf16[24,2560]{1,0:T(8,128)(2,1)S(1)}, bf16[24,2560]{1,0:T(8,128)(2,1)S(1)}, u32[]{:S(2)}, u32[]{:S(2)}) collective-permute-start(bf16[24,2560]{1,0:T(8,128)(2,1)S(1)} %copy-done.6), channel_id=1, source_target_pairs={{0,8},{2,10},{4,12},{6,14},{8,0},{10,2},{12,4},{14,6},{16,24},{18,... | collective-permute-start | bytes 368648 | tf_op jit(solution)/shard_map/ppermute | solution.py:536
  278.9 12.9 %collective-permute-start.31 = (bf16[96,2560]{1,0:T(8,128)(2,1)}, bf16[96,2560]{1,0:T(8,128)(2,1)S(1)}, u32[]{:S(2)}, u32[]{:S(2)}) collective-permute-start(bf16[96,2560]{1,0:T(8,128)(2,1)} %bitcast.57), channel_id=1, source_target_pairs={{0,4},{2,6},{4,0},{6,2},{8,12},{10,14},{12,8},{14,10},{16,20},{18,... | collective-permute-start | bytes 1474568 | tf_op jit(solution)/shard_map/ppermute | solution.py:536
  (50 other events, 212.2 us)

commit v4 on v3

--- a/solution.py
+++ b/solution.py
@@ -1,3 +1,4 @@
+import math
 from functools import partial
 
 import jax
@@ -485,7 +486,7 @@
     return pl.BlockSpec(array.shape, lambda i: (0,) * array.ndim)
 
 
-def run(kernel, grid, inputs, outputs, scratch=(), aliases=None, later=()):
+def run(kernel, grid, inputs, outputs, scratch=(), aliases=None, later=(), spare=4):
     first = len(inputs)
     later = jax.tree.leaves(later)
     inputs = [*inputs, *[(x, pl.ANY) for x in later]]
@@ -506,6 +507,12 @@
             specs.append(whole_spec(item[0]))
         else:
             specs.append(spec(item[1], item[2]))
+    held = sum(
+        math.prod(x[1] or x[0].shape) * x[0].dtype.itemsize
+        for x in (*inputs, *outputs)
+        if x[1] is not pl.ANY
+    )
+    kept = sum(math.prod(x.shape) * jnp.dtype(x.dtype).itemsize for x in scratch)
     out_specs = [whole_spec(o[0]) if o[1] is None else spec(o[1], o[2]) for o in outputs]
     return pl.pallas_call(
         body,
@@ -517,7 +524,8 @@
         input_output_aliases=aliases or {},
         cost_estimate=pl.CostEstimate(flops=1, bytes_accessed=1, transcendentals=0),
         compiler_params=pltpu.CompilerParams(
-            dimension_semantics=("arbitrary",), vmem_limit_bytes=56 * MIB
+            dimension_semantics=("arbitrary",),
+            vmem_limit_bytes=min(56 * MIB, 2 * held + kept + spare * MIB),
         ),
     )(*[x[0] for x in inputs])
 
@@ -721,6 +729,7 @@
         1,
         [(place, None), (qkv_weight, None), (norm_gains, None)],
         [(shape_of(half + 16, qkv_weight.shape[1]), None)],
+        spare=56,
     )
     far_qkv = exchange(first_half, 0)
     later_rows = half + down_weight.shape[0] // 6 + out_weight.shape[0] // 6
@@ -735,6 +744,7 @@
         ],
         [(shape_of(later_rows, in_weight.shape[1]), None), (halo, None), (halo, None)],
         later=first_half,
+        spare=56,
     )
     far_later = exchange(later_half, 0)
     tok_before = passed_along(tok_tail, "seq", 1)
@@ -787,6 +797,7 @@
             (shape_of(num_seqs, HEAD_ROWS, PAIR, dtype=f32), (1, HEAD_ROWS, PAIR), per_seq),
         ],
         [pltpu.VMEM((width, 3 * width), bf16)],
+        spare=56,
     )
     far_later, mixed = together(far_later, mixed)
     near_later = swap_half(far_later)
@@ -831,6 +842,7 @@
             pltpu.VMEM((width, 2 * ffn), bf16),
             pltpu.VMEM((ffn, width), bf16),
         ],
+        spare=56,
     )
     do_before = passed_along(grad_hi, "seq", 1)
     do_after = passed_along(grad_lo, "seq", -1)
@@ -852,6 +864,7 @@
         ],
         [(bundle_part, None), (bundle_part, None)],
         [pltpu.VMEM((2 * bundle_rows, width), bf16)],
+        spare=56,
     )
     do_before, do_after, send = together(do_before, do_after, send)
     chain_mlp = Chain(sum_stages(place, keep, send))
@@ -893,6 +906,7 @@
             ],
             aliases=None if earlier is None else {13: 0},
             later=later,
+            spare=56,
         )
 
     few = num_seqs // 2
@@ -916,6 +930,7 @@
             (shape_of(8, width, dtype=f32), None),
         ],
         [pltpu.VMEM((width, 3 * width), bf16)],
+        spare=12,
     )
     sent = chain_mlp.advance(gain_sum_one)
     step_columns = wider // 2
@@ -938,6 +953,7 @@
         [(part, block, last_block), (part, block, last_block)],
         [pltpu.VMEM((width, step_columns), bf16)],
         later=sent,
+        spare=12,
     )
     send, *chain_mlp.got = together(send, *chain_mlp.got)
     chain_qkv = Chain(sum_stages(place, keep, send))
@@ -947,7 +963,7 @@
     sent = chain_qkv.advance(sent)
     while chain_mlp.result is None:
         sent = chain_qkv.advance(sent)
-        sent = chain_mlp.advance(sent)
+        sent = chain_mlp.advance(sent, gate=chain_qkv, arrived=len(chain_qkv.got))
     in_sum, down_sum, out_sum = run(
         finish_three_kernel,
         1,

time: 303 us -> 280 us (0.924)
  Pallas kernels: 160 us -> 129 us
  waiting for transfers between devices: 55.8 us -> 62.4 us
  starting transfers between devices: 52.6 us -> 59.1 us
  local copies, waits for them, and re-layouts: 17.6 us -> 12.2 us
    pallas_call x23, Pallas kernels: 160 us -> 129 us  [run(): pl.pallas_call(body, grid=(grid,), in_specs=specs, out_specs=out_specs, o...]
    ppermute x22, starting transfers between devices: 36.1 us -> 43.3 us  [exchange(): lax.ppermute(block, 'seq', flip_route(lax.axis_size('seq'), distance))]
    ppermute x22, waiting for transfers between devices: 49.9 us -> 55.8 us  [exchange(): lax.ppermute(block, 'seq', flip_route(lax.axis_size('seq'), distance))]
    unnamed x96 -> x68, local copies, waits for them, and re-layouts: 16.8 us -> 11.4 us
  transfers between devices with their start and end apart: 34 -> 34, of which waited for: 18 -> 17; matrix products, arithmetic and copies ran while one was open for 5% -> 6% of each run, Pallas kernels for 35% -> 33%
where the time goes in v4:
time: 280 us; the launch traced here: 279 us
  Pallas kernels  129 us (46%)
  waiting for transfers between devices  62.4 us (22%)
  starting transfers between devices  59.1 us (21%)
  other arithmetic  15.5 us (6%)
  local copies, waits for them, and re-layouts  12.2 us (4%)
    pallas_call x23, Pallas kernels, run(): pl.pallas_call(body, grid=(grid,), in_specs=specs, out_specs=out_specs, o...  129 us
    ppermute x22, waiting for transfers between devices, exchange(): lax.ppermute(block, 'seq', flip_route(lax.axis_size('seq'), distance))  55.8 us
    ppermute x22, starting transfers between devices, exchange(): lax.ppermute(block, 'seq', flip_route(lax.axis_size('seq'), distance))  43.3 us
    unnamed x68, local copies, waits for them, and re-layouts  11.4 us
    ppermute x6, starting transfers between devices, exchange(): return lax.ppermute(block, 'fsdp', flip_route(2, 1))  6.79 us
    ppermute x4, starting transfers between devices, passed_along(): return lax.ppermute(block, axis, route)  6.18 us
  transfers between devices with their start and end apart: 34, of which 17 were waited for; matrix products, arithmetic and copies ran while one was open for 6% of the time, Pallas kernels for 33%

profile of v4, /device:TPU:0, one launch (start us, length us, event | category | flops | bytes accessed | tf_op | source)
XLA Modules:
  0.0 279.4 jit_solution(9023486165286783254)
XLA Ops:
  1.2 2.5 shard_map.135.refs_5_
  3.7 3.0 %collective-permute-start.1 = (bf16[208,2304]{1,0:T(8,128)(2,1)}, bf16[208,2304]{1,0:T(8,128)(2,1)S(1)}, u32[]{:S(2)}, u32[]{:S(2)}) collective-permute-start(bf16[208,2304]{1,0:T(8,128)(2,1)} %shard_map.135.refs_5_), channel_id=1, source_target_pairs={{0,1},{1,0},{2,3},{3,2},{4,5},{5,4},{6,7},{7,6},{8,9},{9,8},{10,11... | collective-permute-start | bytes 2875400 | tf_op jit(solution)/shard_map/ppermute | solution.py:543
  6.7 4.2 %shard_map.136 = (bf16[352,2304]{1,0:T(8,128)(2,1)}, bf16[8,64,768]{2,1,0:T(8,128)(2,1)}, bf16[8,64,768]{2,1,0:T(8,128)(2,1)}) custom-call(s32[5]{0:T(128)} %stack.19.refs_0_, bf16[384,768]{1,0:T(8,128)(2,1)} %refs_6_.1, bf16[384,2304]{1,0:T(8,128)(2,1)} %refs_7_.1, bf16[576,768]{1,0:T(8,128)(2,1)} %refs_8_.3, bf16[8,128,768]{2,1,0:T(8,128)(2,1)} %refs_2_.5, ...), custom_call_target="tpu_custom_call" | custom-call | flops 1 | bytes 1 | tf_op jit(solution)/shard_map/pallas_call | solution.py:517
  17.4 4.3 %fusion = (f32[8,256,32]{2,1,0:T(8,128)S(1)}, f32[8,256,32]{2,1,0:T(8,128)S(1)}, f32[8,256,32]{2,1,0:T(8,128)S(1)}) fusion(f32[32]{0:T(128)} %negate_power_fusion, f32[8,256]{1,0:T(8,128)S(1)} %convert_element_type.3), kind=kLoop, calls=%fused_computation.7 | loop fusion | flops 131072 | bytes 794752 | tf_op jit(solution)/shard_map/neg | solution.py:682
  23.3 3.0 %pad_maximum_fusion = (f32[8,256,128]{2,1,0:T(8,128)}, f32[8,256,128]{2,1,0:T(8,128)}) fusion(f32[8,256,32]{2,1,0:T(8,128)S(1)} %get-tuple-element.185, f32[8,256,32]{2,1,0:T(8,128)S(1)} %get-tuple-element.184, f32[8,256,32]{2,1,0:T(8,128)S(1)} %get-tuple-element.183), kind=kLoop, calls=%fused_computation.2 | loop fusion | flops 1572864 | bytes 2883584 | tf_op jit(solution)/shard_map/concatenate | solution.py:681
  30.2 2.7 collective-permute-start.4
  36.1 26.5 %shard_map.137 = (bf16[8,128,768]{2,1,0:T(8,128)(2,1)}, bf16[8,256,768]{2,1,0:T(8,128)(2,1)}, bf16[8,256,768]{2,1,0:T(8,128)(2,1)}, bf16[8,256,768]{2,1,0:T(8,12...) custom-call(s32[5]{0:T(128)} %stack.19.refs_0_, bf16[8,64,768]{2,1,0:T(8,128)(2,1)} %copy-done.24, ...), custom_call_target="tpu_custom_call" | custom-call | flops 1 | bytes 1 | tf_op jit(solution)/shard_map/pallas_call | solution.py:517
  63.0 3.4 %collective-permute-done.5.refs_10_ = bf16[352,2304]{1,0:T(8,128)(2,1)S(1)} collective-permute-done((bf16[352,2304]{1,0:T(8,128)(2,1)S(1)}, bf16[352,2304]{1,0:T(8,128)(2,1)S(1)}, u32[]{:S(2)}, u32[]{:S(2)}) %collective-permute-start.5) | collective-permute-done | bytes 1622048 | tf_op jit(solution)/shard_map/ppermute | solution.py:538
  67.5 27.3 %shard_map.138 = (bf16[1024,768]{1,0:T(8,128)(2,1)}, f32[1024,768]{1,0:T(8,128)}, bf16[1024,768]{1,0:T(8,128)(2,1)}, bf16[8,80,768]{2,1,0:T(8,128)(2,1)}, bf16[8...) custom-call(s32[5]{0:T(128)} %stack.19.refs_0_, ...), custom_call_target="tpu_custom_call" | custom-call | flops 1 | bytes 1 | tf_op jit(solution)/shard_map/pallas_call | solution.py:517
  98.3 14.7 %shard_map.139 = (bf16[2,1088,768]{2,1,0:T(8,128)(2,1)}, bf16[2,1088,768]{2,1,0:T(8,128)(2,1)}) custom-call(s32[5]{0:T(128)} %stack.19.refs_0_, bf16[1024,768]{1,0:T(8,128)(2,1)} %get-tuple-element.111.refs_1_, bf16[1024,2304]{1,0:T(8,128)(2,1)} %get-tuple-element.112.refs_2_, bf16[1024,1152]{1,0:T(8,128)(2,1)} %get-tuple-element.113.refs_3_, ...), custom_call_target="tpu_custom_call" | custom-call | flops 1 | bytes 1 | tf_op jit(solution)/shard_map/pallas_call | solution.py:517
  113.0 8.1 %collective-permute-start.8 = (bf16[2,1088,768]{2,1,0:T(8,128)(2,1)}, bf16[2,1088,768]{2,1,0:T(8,128)(2,1)S(1)}, u32[]{:S(2)}, u32[]{:S(2)}) collective-permute-start(bf16[2,1088,768]{2,1,0:T(8,128)(2,1)} %get-tuple-element.123), channel_id=1, source_target_pairs={{0,2},{2,0},{4,6},{6,4},{8,10},{10,8},{12,14},{14,12},{16,18},{18,... | collective-permute-start | bytes 10027016 | tf_op jit(solution)/shard_map/ppermute | solution.py:544
  121.1 11.1 %shard_map.140 = (bf16[8,128,2560]{2,1,0:T(8,128)(2,1)}, f32[8,128]{1,0:T(8,128)}) custom-call(bf16[8,256,768]{2,1,0:T(8,128)(2,1)} %get-tuple-element.105.refs_0_, bf16[8,256,768]{2,1,0:T(8,128)(2,1)} %get-tuple-element.106.refs_1_, bf16[8,256,768]{2,1,0:T(8,128)(2,1)} %get-tuple-element.107.refs_2_, bf16[8,128,768]{2,1,0:T(8,128)(2,1)} %bitcast.68, ...), custom_call_target="tpu_custom_call" | custom-call | flops 1 | bytes 1 | tf_op jit(solution)/shard_map/pallas_call | solution.py:517
  137.9 3.5 %collective-permute-start.10 = (bf16[2,544,384]{2,1,0:T(8,128)(2,1)S(1)}, bf16[2,544,384]{2,1,0:T(8,128)(2,1)}, u32[]{:S(2)}, u32[]{:S(2)}) collective-permute-start(bf16[2,544,384]{2,1,0:T(8,128)(2,1)S(1)} %get-tuple-element.126.refs_15_), channel_id=1, source_target_pairs={{0,4},{2,6},{4,0},{6,2},{8,12},{10,14},{12,8},{14,10},{16,20},{18,... | collective-permute-start | bytes 2506760 | tf_op jit(solution)/shard_map/ppermute | solution.py:544
  141.4 11.2 %shard_map.142 = (bf16[8,128,2560]{2,1,0:T(8,128)(2,1)}, f32[8,128]{1,0:T(8,128)}) custom-call(bf16[8,256,768]{2,1,0:T(8,128)(2,1)} %get-tuple-element.105.refs_0_, bf16[8,256,768]{2,1,0:T(8,128)(2,1)} %get-tuple-element.106.refs_1_, bf16[8,256,768]{2,1,0:T(8,128)(2,1)} %get-tuple-element.107.refs_2_, ...), custom_call_target="tpu_custom_call", output_to_operand_aliasing={{0}: (13, {})} | custom-call | flops 1 | bytes 1 | tf_op jit(solution)/shard_map/pallas_call | solution.py:517
  152.6 2.5 copy-done
  157.0 7.0 %shard_map.143 = (bf16[1024,768]{1,0:T(8,128)(2,1)}, f32[8,768]{1,0:T(8,128)S(1)}) custom-call(s32[5]{0:T(128)S(1)} %copy-done.16, bf16[1024,2560]{1,0:T(8,128)(2,1)S(1)} %bitcast.34, bf16[1024,768]{1,0:T(8,128)(2,1)S(1)} %bitcast.41, f32[1024,768]{1,0:T(8,128)S(1)} %copy-done.8, bf16[2,768]{1,0:T(2,128)(2,1)S(1)} %copy-done.17, ...), custom_call_target="tpu_custom_call" | custom-call | flops 1 | bytes 1 | tf_op jit(solution)/shard_map/pallas_call | solution.py:517
  167.3 6.3 %shard_map.145 = (bf16[2,192,2560]{2,1,0:T(8,128)(2,1)S(1)}, bf16[2,192,2560]{2,1,0:T(8,128)(2,1)S(1)}) custom-call(s32[5]{0:T(128)S(1)} %copy-done.16, bf16[1024,768]{1,0:T(8,128)(2,1)S(1)} %bitcast.53, bf16[1024,2560]{1,0:T(8,128)(2,1)S(1)} %bitcast.35, f32[8,768]{1,0:T(8,128)S(1)} %get-tuple-element.131.refs_5_.refs_3_, f32[8,768]{1,0:T(8,128)S(1)} %copy-done.18, ...), custom_call_target="tpu_custom_call" | custom-call | flops 1 | bytes 1 | tf_op jit(solution)/shard_map/pallas_call | solution.py:517
  173.5 2.9 %collective-permute-done.11 = bf16[544,384]{1,0:T(8,128)(2,1)S(1)} collective-permute-done((bf16[544,384]{1,0:T(8,128)(2,1)S(1)}, bf16[544,384]{1,0:T(8,128)(2,1)S(1)}, u32[]{:S(2)}, u32[]{:S(2)}) %collective-permute-start.11) | collective-permute-done | bytes 417824 | tf_op jit(solution)/shard_map/ppermute | solution.py:544
  177.4 3.7 %collective-permute-start.14 = (bf16[136,768]{1,0:T(8,128)(2,1)S(1)}, bf16[136,768]{1,0:T(8,128)(2,1)S(1)}, u32[]{:S(2)}, u32[]{:S(2)}) collective-permute-start(bf16[136,768]{1,0:T(8,128)(2,1)S(1)} %get-tuple-element.143.refs_3_), channel_id=1, source_target_pairs={{0,8},{2,10},{4,12},{6,14},{8,0},{10,2},{12,4},{14,6},{16,24},{18,... | collective-permute-start | bytes 626696 | tf_op jit(solution)/shard_map/ppermute | solution.py:544
  181.1 2.6 collective-permute-start.15
  185.0 6.2 %collective-permute-done.14 = bf16[136,768]{1,0:T(8,128)(2,1)S(1)} collective-permute-done((bf16[136,768]{1,0:T(8,128)(2,1)S(1)}, bf16[136,768]{1,0:T(8,128)(2,1)S(1)}, u32[]{:S(2)}, u32[]{:S(2)}) %collective-permute-start.14) | collective-permute-done | bytes 208928 | tf_op jit(solution)/shard_map/ppermute | solution.py:544
  191.2 2.5 collective-permute-done.15
  197.7 5.2 %collective-permute-done.18 = bf16[136,768]{1,0:T(8,128)(2,1)S(1)} collective-permute-done((bf16[136,768]{1,0:T(8,128)(2,1)S(1)}, bf16[136,768]{1,0:T(8,128)(2,1)S(1)}, u32[]{:S(2)}, u32[]{:S(2)}) %collective-permute-start.18) | collective-permute-done | bytes 208928 | tf_op jit(solution)/shard_map/ppermute | solution.py:544
  207.5 4.5 %collective-permute-start.23 = (bf16[136,768]{1,0:T(8,128)(2,1)S(1)}, bf16[136,768]{1,0:T(8,128)(2,1)S(1)}, u32[]{:S(2)}, u32[]{:S(2)}) collective-permute-start(bf16[136,768]{1,0:T(8,128)(2,1)S(1)} %shard_map.148.refs_5_.refs_6_.refs_7_.refs_1_), channel_id=1, source_target_pairs={{0,24},{2,26},{4,28},{6,30},{8,16},{10,18},{12,20},{14,22},{16,8},... | collective-permute-start | bytes 626696 | tf_op jit(solution)/shard_map/ppermute | solution.py:544
  213.5 3.4 %collective-permute-start.24 = (bf16[24,2560]{1,0:T(8,128)(2,1)S(1)}, bf16[24,2560]{1,0:T(8,128)(2,1)S(1)}, u32[]{:S(2)}, u32[]{:S(2)}) collective-permute-start(bf16[24,2560]{1,0:T(8,128)(2,1)S(1)} %get-tuple-element.159.refs_5_), channel_id=1, source_target_pairs={{0,8},{2,10},{4,12},{6,14},{8,0},{10,2},{12,4},{14,6},{16,24},{18,... | collective-permute-start | bytes 368648 | tf_op jit(solution)/shard_map/ppermute | solution.py:544
  218.5 3.3 %collective-permute-start.26 = (bf16[24,2560]{1,0:T(8,128)(2,1)S(1)}, bf16[24,2560]{1,0:T(8,128)(2,1)S(1)}, u32[]{:S(2)}, u32[]{:S(2)}) collective-permute-start(bf16[24,2560]{1,0:T(8,128)(2,1)S(1)} %get-tuple-element.161.refs_7_), channel_id=1, source_target_pairs={{0,24},{2,26},{4,28},{6,30},{8,16},{10,18},{12,20},{14,22},{16,8},... | collective-permute-start | bytes 368648 | tf_op jit(solution)/shard_map/ppermute | solution.py:544
  221.8 11.9 %collective-permute-done.22.refs_3_ = bf16[136,768]{1,0:T(8,128)(2,1)S(1)} collective-permute-done((bf16[136,768]{1,0:T(8,128)(2,1)S(1)}, bf16[136,768]{1,0:T(8,128)(2,1)S(1)}, u32[]{:S(2)}, u32[]{:S(2)}) %collective-permute-start.22) | collective-permute-done | bytes 208928 | tf_op jit(solution)/shard_map/ppermute | solution.py:544
  243.1 13.7 %collective-permute-done.27.refs_2_ = bf16[544,768]{1,0:T(8,128)(2,1)S(1)} collective-permute-done((bf16[544,768]{1,0:T(8,128)(2,1)S(1)}, bf16[544,768]{1,0:T(8,128)(2,1)S(1)}, u32[]{:S(2)}, u32[]{:S(2)}) %collective-permute-start.27) | collective-permute-done | bytes 835616 | tf_op jit(solution)/shard_map/ppermute | solution.py:544
  261.3 3.6 %shard_map.155 = (f32[384,2304]{1,0:T(8,128)}, f32[576,768]{1,0:T(8,128)}, f32[384,768]{1,0:T(8,128)}) custom-call(s32[5]{0:T(128)S(1)} %copy-done.16, bf16[1088,768]{1,0:T(8,128)(2,1)S(1)} %bitcast.38, bf16[1088,768]{1,0:T(8,128)(2,1)S(1)} %collective-permute-done.32.refs_2_, bf16[1088,768]{1,0:T(8,128)(2,1)S(1)} %bitcast.39), custom_call_target="tpu_custom_call" | custom-call | flops 1 | bytes 1 | tf_op jit(solution)/shard_map/pallas_call | solution.py:517
  265.0 7.1 %collective-permute-done.31.refs_2_ = bf16[96,2560]{1,0:T(8,128)(2,1)S(1)} collective-permute-done((bf16[96,2560]{1,0:T(8,128)(2,1)S(1)}, bf16[96,2560]{1,0:T(8,128)(2,1)S(1)}, u32[]{:S(2)}, u32[]{:S(2)}) %collective-permute-start.31) | collective-permute-done | bytes 491552 | tf_op jit(solution)/shard_map/ppermute | solution.py:544
  274.3 2.6 collective-permute-done.33.refs_2_
  276.8 2.6 shard_map.157
  (153 shorter events, 61.3 us)
Async XLA Ops:
  3.7 25.6 %collective-permute-start.1 = (bf16[208,2304]{1,0:T(8,128)(2,1)}, bf16[208,2304]{1,0:T(8,128)(2,1)S(1)}, u32[]{:S(2)}, u32[]{:S(2)}) collective-permute-start(bf16[208,2304]{1,0:T(8,128)(2,1)} %shard_map.135.refs_5_), channel_id=1, source_target_pairs={{0,1},{1,0},{2,3},{3,2},{4,5},{5,4},{6,7},{7,6},{8,9},{9,8},{10,11... | collective-permute-start | bytes 2875400 | tf_op jit(solution)/shard_map/ppermute | solution.py:543
  10.9 18.4 %collective-permute-start.2 = (bf16[8,64,768]{2,1,0:T(8,128)(2,1)}, bf16[8,64,768]{2,1,0:T(8,128)(2,1)S(1)}, u32[]{:S(2)}, u32[]{:S(2)}) collective-permute-start(bf16[8,64,768]{2,1,0:T(8,128)(2,1)} %get-tuple-element.92), channel_id=1, source_target_pairs={{0,2},{2,4},{4,6},{6,8},{8,10},{10,12},{12,14},{14,16},{16,18},{18... | collective-permute-start | bytes 2359304 | tf_op jit(solution)/shard_map/ppermute | solution.py:29
  12.4 16.9 %collective-permute-start.3 = (bf16[8,64,768]{2,1,0:T(8,128)(2,1)}, bf16[8,64,768]{2,1,0:T(8,128)(2,1)}, u32[]{:S(2)}, u32[]{:S(2)}) collective-permute-start(bf16[8,64,768]{2,1,0:T(8,128)(2,1)} %get-tuple-element.93), channel_id=1, source_target_pairs={{2,0},{4,2},{6,4},{8,6},{10,8},{12,10},{14,12},{16,14},{18,16},{20... | collective-permute-start | bytes 2359304 | tf_op jit(solution)/shard_map/ppermute | solution.py:29
  13.7 49.2 %collective-permute-start = (bf16[352,2304]{1,0:T(8,128)(2,1)}, bf16[352,2304]{1,0:T(8,128)(2,1)S(1)}, u32[]{:S(2)}, u32[]{:S(2)}) collective-permute-start(bf16[352,2304]{1,0:T(8,128)(2,1)} %get-tuple-element.91), channel_id=1, source_target_pairs={{0,1},{1,0},{2,3},{3,2},{4,5},{5,4},{6,7},{7,6},{8,9},{9,8},{10,11... | collective-permute-start | bytes 4866056 | tf_op jit(solution)/shard_map/ppermute | solution.py:543
  30.2 4.9 %collective-permute-start.4 = (bf16[208,2304]{1,0:T(8,128)(2,1)S(1)}, bf16[208,2304]{1,0:T(8,128)(2,1)S(1)}, u32[]{:S(2)}, u32[]{:S(2)}) collective-permute-start(bf16[208,2304]{1,0:T(8,128)(2,1)S(1)} %collective-permute-done.1.refs_9_.refs_6_), channel_id=1, source_target_pairs={{0,2},{2,0},{4,6},{6,4},{8,10},{10,8},{12,14},{14,12},{16,18},{18,... | collective-permute-start | bytes 2875400 | tf_op jit(solution)/shard_map/ppermute | solution.py:538
  94.9 18.1 %collective-permute-start.6 = (bf16[8,80,768]{2,1,0:T(8,128)(2,1)}, bf16[8,80,768]{2,1,0:T(8,128)(2,1)S(1)}, u32[]{:S(2)}, u32[]{:S(2)}) collective-permute-start(bf16[8,80,768]{2,1,0:T(8,128)(2,1)} %get-tuple-element.109), channel_id=1, source_target_pairs={{0,2},{2,4},{4,6},{6,8},{8,10},{10,12},{12,14},{14,16},{16,18},{18... | collective-permute-start | bytes 2949128 | tf_op jit(solution)/shard_map/ppermute | solution.py:29
  97.0 16.0 %collective-permute-start.7 = (bf16[8,80,768]{2,1,0:T(8,128)(2,1)}, bf16[8,80,768]{2,1,0:T(8,128)(2,1)S(1)}, u32[]{:S(2)}, u32[]{:S(2)}) collective-permute-start(bf16[8,80,768]{2,1,0:T(8,128)(2,1)} %get-tuple-element.110), channel_id=1, source_target_pairs={{2,0},{4,2},{6,4},{8,6},{10,8},{12,10},{14,12},{16,14},{18,16},{20... | collective-permute-start | bytes 2949128 | tf_op jit(solution)/shard_map/ppermute | solution.py:29
  113.0 19.3 %collective-permute-start.8 = (bf16[2,1088,768]{2,1,0:T(8,128)(2,1)}, bf16[2,1088,768]{2,1,0:T(8,128)(2,1)S(1)}, u32[]{:S(2)}, u32[]{:S(2)}) collective-permute-start(bf16[2,1088,768]{2,1,0:T(8,128)(2,1)} %get-tuple-element.123), channel_id=1, source_target_pairs={{0,2},{2,0},{4,6},{6,4},{8,10},{10,8},{12,14},{14,12},{16,18},{18,... | collective-permute-start | bytes 10027016 | tf_op jit(solution)/shard_map/ppermute | solution.py:544
  136.9 27.1 %collective-permute-start.9 = (bf16[2,544,384]{2,1,0:T(8,128)(2,1)}, bf16[2,544,384]{2,1,0:T(8,128)(2,1)}, u32[]{:S(2)}, u32[]{:S(2)}) collective-permute-start(bf16[2,544,384]{2,1,0:T(8,128)(2,1)} %get-tuple-element.125.refs_14_), channel_id=1, source_target_pairs={{0,1},{1,0},{2,3},{3,2},{4,5},{5,4},{6,7},{7,6},{8,9},{9,8},{10,11... | collective-permute-start | bytes 2506760 | tf_op jit(solution)/shard_map/ppermute | solution.py:543
  137.9 26.2 %collective-permute-start.10 = (bf16[2,544,384]{2,1,0:T(8,128)(2,1)S(1)}, bf16[2,544,384]{2,1,0:T(8,128)(2,1)}, u32[]{:S(2)}, u32[]{:S(2)}) collective-permute-start(bf16[2,544,384]{2,1,0:T(8,128)(2,1)S(1)} %get-tuple-element.126.refs_15_), channel_id=1, source_target_pairs={{0,4},{2,6},{4,0},{6,2},{8,12},{10,14},{12,8},{14,10},{16,20},{18,... | collective-permute-start | bytes 2506760 | tf_op jit(solution)/shard_map/ppermute | solution.py:544
  166.0 10.4 %collective-permute-start.11 = (bf16[544,384]{1,0:T(8,128)(2,1)S(1)}, bf16[544,384]{1,0:T(8,128)(2,1)S(1)}, u32[]{:S(2)}, u32[]{:S(2)}) collective-permute-start(bf16[544,384]{1,0:T(8,128)(2,1)S(1)} %get-tuple-element.135.refs_5_), channel_id=1, source_target_pairs={{0,4},{2,6},{4,0},{6,2},{8,12},{10,14},{12,8},{14,10},{16,20},{18,... | collective-permute-start | bytes 1253384 | tf_op jit(solution)/shard_map/ppermute | solution.py:544
  166.1 10.5 %collective-permute-start.12 = (bf16[544,384]{1,0:T(8,128)(2,1)S(1)}, bf16[544,384]{1,0:T(8,128)(2,1)S(1)}, u32[]{:S(2)}, u32[]{:S(2)}) collective-permute-start(bf16[544,384]{1,0:T(8,128)(2,1)S(1)} %get-tuple-element.136.refs_6_), channel_id=1, source_target_pairs={{0,1},{1,0},{2,3},{3,2},{4,5},{5,4},{6,7},{7,6},{8,9},{9,8},{10,11... | collective-permute-start | bytes 1253384 | tf_op jit(solution)/shard_map/ppermute | solution.py:543
  176.6 7.0 %collective-permute-start.13 = (bf16[2,192,2560]{2,1,0:T(8,128)(2,1)S(1)}, bf16[2,192,2560]{2,1,0:T(8,128)(2,1)S(1)}, u32[]{:S(2)}, u32[]{:S(2)}) collective-permute-start(bf16[2,192,2560]{2,1,0:T(8,128)(2,1)S(1)} %get-tuple-element.139), channel_id=1, source_target_pairs={{0,2},{2,0},{4,6},{6,4},{8,10},{10,8},{12,14},{14,12},{16,18},{18,... | collective-permute-start | bytes 5898248 | tf_op jit(solution)/shard_map/ppermute | solution.py:544
  177.4 13.8 %collective-permute-start.14 = (bf16[136,768]{1,0:T(8,128)(2,1)S(1)}, bf16[136,768]{1,0:T(8,128)(2,1)S(1)}, u32[]{:S(2)}, u32[]{:S(2)}) collective-permute-start(bf16[136,768]{1,0:T(8,128)(2,1)S(1)} %get-tuple-element.143.refs_3_), channel_id=1, source_target_pairs={{0,8},{2,10},{4,12},{6,14},{8,0},{10,2},{12,4},{14,6},{16,24},{18,... | collective-permute-start | bytes 626696 | tf_op jit(solution)/shard_map/ppermute | solution.py:544
  181.1 12.7 %collective-permute-start.15 = (bf16[136,768]{1,0:T(8,128)(2,1)S(1)}, bf16[136,768]{1,0:T(8,128)(2,1)S(1)}, u32[]{:S(2)}, u32[]{:S(2)}) collective-permute-start(bf16[136,768]{1,0:T(8,128)(2,1)S(1)} %get-tuple-element.144.refs_4_), channel_id=1, source_target_pairs={{0,16},{2,18},{4,20},{6,22},{8,24},{10,26},{12,28},{14,30},{16,0},... | collective-permute-start | bytes 626696 | tf_op jit(solution)/shard_map/ppermute | solution.py:544
  193.8 10.5 %collective-permute-start.16 = (bf16[2,96,1280]{2,1,0:T(8,128)(2,1)S(1)}, bf16[2,96,1280]{2,1,0:T(8,128)(2,1)S(1)}, u32[]{:S(2)}, u32[]{:S(2)}) collective-permute-start(bf16[2,96,1280]{2,1,0:T(8,128)(2,1)S(1)} %get-tuple-element.149.refs_5_), channel_id=1, source_target_pairs={{0,1},{1,0},{2,3},{3,2},{4,5},{5,4},{6,7},{7,6},{8,9},{9,8},{10,11... | collective-permute-start | bytes 1474568 | tf_op jit(solution)/shard_map/ppermute | solution.py:543
  194.3 10.3 %collective-permute-start.17 = (bf16[2,96,1280]{2,1,0:T(8,128)(2,1)S(1)}, bf16[2,96,1280]{2,1,0:T(8,128)(2,1)S(1)}, u32[]{:S(2)}, u32[]{:S(2)}) collective-permute-start(bf16[2,96,1280]{2,1,0:T(8,128)(2,1)S(1)} %get-tuple-element.151.refs_6_), channel_id=1, source_target_pairs={{0,4},{2,6},{4,0},{6,2},{8,12},{10,14},{12,8},{14,10},{16,20},{18,... | collective-permute-start | bytes 1474568 | tf_op jit(solution)/shard_map/ppermute | solution.py:544
  195.2 7.7 %collective-permute-start.18 = (bf16[136,768]{1,0:T(8,128)(2,1)S(1)}, bf16[136,768]{1,0:T(8,128)(2,1)S(1)}, u32[]{:S(2)}, u32[]{:S(2)}) collective-permute-start(bf16[136,768]{1,0:T(8,128)(2,1)S(1)} %get-tuple-element.145.refs_5_), channel_id=1, source_target_pairs={{0,24},{2,26},{4,28},{6,30},{8,16},{10,18},{12,20},{14,22},{16,8},... | collective-permute-start | bytes 626696 | tf_op jit(solution)/shard_map/ppermute | solution.py:544
  205.6 6.9 %collective-permute-start.19 = (bf16[96,1280]{1,0:T(8,128)(2,1)S(1)}, bf16[96,1280]{1,0:T(8,128)(2,1)S(1)}, u32[]{:S(2)}, u32[]{:S(2)}) collective-permute-start(bf16[96,1280]{1,0:T(8,128)(2,1)S(1)} %get-tuple-element.156.refs_4_), channel_id=1, source_target_pairs={{0,4},{2,6},{4,0},{6,2},{8,12},{10,14},{12,8},{14,10},{16,20},{18,... | collective-permute-start | bytes 737288 | tf_op jit(solution)/shard_map/ppermute | solution.py:544
  206.6 6.2 %collective-permute-start.20 = (bf16[96,1280]{1,0:T(8,128)(2,1)S(1)}, bf16[96,1280]{1,0:T(8,128)(2,1)S(1)}, u32[]{:S(2)}, u32[]{:S(2)}) collective-permute-start(bf16[96,1280]{1,0:T(8,128)(2,1)S(1)} %get-tuple-element.157.refs_5_), channel_id=1, source_target_pairs={{0,1},{1,0},{2,3},{3,2},{4,5},{5,4},{6,7},{7,6},{8,9},{9,8},{10,11... | collective-permute-start | bytes 737288 | tf_op jit(solution)/shard_map/ppermute | solution.py:543
  207.5 11.0 %collective-permute-start.23 = (bf16[136,768]{1,0:T(8,128)(2,1)S(1)}, bf16[136,768]{1,0:T(8,128)(2,1)S(1)}, u32[]{:S(2)}, u32[]{:S(2)}) collective-permute-start(bf16[136,768]{1,0:T(8,128)(2,1)S(1)} %shard_map.148.refs_5_.refs_6_.refs_7_.refs_1_), channel_id=1, source_target_pairs={{0,24},{2,26},{4,28},{6,30},{8,16},{10,18},{12,20},{14,22},{16,8},... | collective-permute-start | bytes 626696 | tf_op jit(solution)/shard_map/ppermute | solution.py:544
  211.9 21.8 %collective-permute-start.22 = (bf16[136,768]{1,0:T(8,128)(2,1)S(1)}, bf16[136,768]{1,0:T(8,128)(2,1)S(1)}, u32[]{:S(2)}, u32[]{:S(2)}) collective-permute-start(bf16[136,768]{1,0:T(8,128)(2,1)S(1)} %shard_map.148.refs_5_.refs_6_.refs_7_.refs_1_), channel_id=1, source_target_pairs={{0,16},{2,18},{4,20},{6,22},{8,24},{10,26},{12,28},{14,30},{16,0},... | collective-permute-start | bytes 626696 | tf_op jit(solution)/shard_map/ppermute | solution.py:544
  212.1 21.6 %collective-permute-start.21 = (bf16[136,768]{1,0:T(8,128)(2,1)S(1)}, bf16[136,768]{1,0:T(8,128)(2,1)S(1)}, u32[]{:S(2)}, u32[]{:S(2)}) collective-permute-start(bf16[136,768]{1,0:T(8,128)(2,1)S(1)} %shard_map.148.refs_5_.refs_6_.refs_7_.refs_1_), channel_id=1, source_target_pairs={{0,8},{2,10},{4,12},{6,14},{8,0},{10,2},{12,4},{14,6},{16,24},{18,... | collective-permute-start | bytes 626696 | tf_op jit(solution)/shard_map/ppermute | solution.py:544
  213.5 21.0 %collective-permute-start.24 = (bf16[24,2560]{1,0:T(8,128)(2,1)S(1)}, bf16[24,2560]{1,0:T(8,128)(2,1)S(1)}, u32[]{:S(2)}, u32[]{:S(2)}) collective-permute-start(bf16[24,2560]{1,0:T(8,128)(2,1)S(1)} %get-tuple-element.159.refs_5_), channel_id=1, source_target_pairs={{0,8},{2,10},{4,12},{6,14},{8,0},{10,2},{12,4},{14,6},{16,24},{18,... | collective-permute-start | bytes 368648 | tf_op jit(solution)/shard_map/ppermute | solution.py:544
  216.8 19.5 %collective-permute-start.25 = (bf16[24,2560]{1,0:T(8,128)(2,1)S(1)}, bf16[24,2560]{1,0:T(8,128)(2,1)S(1)}, u32[]{:S(2)}, u32[]{:S(2)}) collective-permute-start(bf16[24,2560]{1,0:T(8,128)(2,1)S(1)} %get-tuple-element.160.refs_6_), channel_id=1, source_target_pairs={{0,16},{2,18},{4,20},{6,22},{8,24},{10,26},{12,28},{14,30},{16,0},... | collective-permute-start | bytes 368648 | tf_op jit(solution)/shard_map/ppermute | solution.py:544
  218.5 17.8 %collective-permute-start.26 = (bf16[24,2560]{1,0:T(8,128)(2,1)S(1)}, bf16[24,2560]{1,0:T(8,128)(2,1)S(1)}, u32[]{:S(2)}, u32[]{:S(2)}) collective-permute-start(bf16[24,2560]{1,0:T(8,128)(2,1)S(1)} %get-tuple-element.161.refs_7_), channel_id=1, source_target_pairs={{0,24},{2,26},{4,28},{6,30},{8,16},{10,18},{12,20},{14,22},{16,8},... | collective-permute-start | bytes 368648 | tf_op jit(solution)/shard_map/ppermute | solution.py:544
  236.3 20.4 %collective-permute-start.27 = (bf16[544,768]{1,0:T(8,128)(2,1)S(1)}, bf16[544,768]{1,0:T(8,128)(2,1)S(1)}, u32[]{:S(2)}, u32[]{:S(2)}) collective-permute-start(bf16[544,768]{1,0:T(8,128)(2,1)S(1)} %bitcast.42), channel_id=1, source_target_pairs={{0,4},{2,6},{4,0},{6,2},{8,12},{10,14},{12,8},{14,10},{16,20},{18,... | collective-permute-start | bytes 2506760 | tf_op jit(solution)/shard_map/ppermute | solution.py:544
  238.6 19.1 %collective-permute-start.30 = (bf16[24,2560]{1,0:T(8,128)(2,1)S(1)}, bf16[24,2560]{1,0:T(8,128)(2,1)S(1)}, u32[]{:S(2)}, u32[]{:S(2)}) collective-permute-start(bf16[24,2560]{1,0:T(8,128)(2,1)S(1)} %shard_map.152.refs_3_.refs_4_.refs_5_.refs_1_), channel_id=1, source_target_pairs={{0,24},{2,26},{4,28},{6,30},{8,16},{10,18},{12,20},{14,22},{16,8},... | collective-permute-start | bytes 368648 | tf_op jit(solution)/shard_map/ppermute | solution.py:544
  241.0 16.7 %collective-permute-start.29 = (bf16[24,2560]{1,0:T(8,128)(2,1)S(1)}, bf16[24,2560]{1,0:T(8,128)(2,1)S(1)}, u32[]{:S(2)}, u32[]{:S(2)}) collective-permute-start(bf16[24,2560]{1,0:T(8,128)(2,1)S(1)} %shard_map.152.refs_3_.refs_4_.refs_5_.refs_1_), channel_id=1, source_target_pairs={{0,16},{2,18},{4,20},{6,22},{8,24},{10,26},{12,28},{14,30},{16,0},... | collective-permute-start | bytes 368648 | tf_op jit(solution)/shard_map/ppermute | solution.py:544
  243.0 14.7 %collective-permute-start.28 = (bf16[24,2560]{1,0:T(8,128)(2,1)S(1)}, bf16[24,2560]{1,0:T(8,128)(2,1)S(1)}, u32[]{:S(2)}, u32[]{:S(2)}) collective-permute-start(bf16[24,2560]{1,0:T(8,128)(2,1)S(1)} %shard_map.152.refs_3_.refs_4_.refs_5_.refs_1_), channel_id=1, source_target_pairs={{0,8},{2,10},{4,12},{6,14},{8,0},{10,2},{12,4},{14,6},{16,24},{18,... | collective-permute-start | bytes 368648 | tf_op jit(solution)/shard_map/ppermute | solution.py:544
  257.7 3.6 %collective-permute-start.32 = (bf16[1088,768]{1,0:T(8,128)(2,1)S(1)}, bf16[1088,768]{1,0:T(8,128)(2,1)S(1)}, u32[]{:S(2)}, u32[]{:S(2)}) collective-permute-start(bf16[1088,768]{1,0:T(8,128)(2,1)S(1)} %bitcast.36), channel_id=1, source_target_pairs={{0,2},{2,0},{4,6},{6,4},{8,10},{10,8},{12,14},{14,12},{16,18},{18,... | collective-permute-start | bytes 5013512 | tf_op jit(solution)/shard_map/ppermute | solution.py:544
  258.4 13.7 %collective-permute-start.31 = (bf16[96,2560]{1,0:T(8,128)(2,1)S(1)}, bf16[96,2560]{1,0:T(8,128)(2,1)S(1)}, u32[]{:S(2)}, u32[]{:S(2)}) collective-permute-start(bf16[96,2560]{1,0:T(8,128)(2,1)S(1)} %bitcast.51), channel_id=1, source_target_pairs={{0,4},{2,6},{4,0},{6,2},{8,12},{10,14},{12,8},{14,10},{16,20},{18,... | collective-permute-start | bytes 1474568 | tf_op jit(solution)/shard_map/ppermute | solution.py:544
  (36 other events, 194.5 us)

commit v5 on v4

--- a/solution.py
+++ b/solution.py
@@ -246,16 +246,38 @@
     return sum(dot_left(part, ones) for part in three_parts(row_groups))
 
 
-def grad_qkv_kernel(place_ref, left_ref, right_ref, one_ref, two_ref, keep_ref, send_ref, whole):
+def grad_qkv_kernel(
+    place_ref, left_ref, right_ref, gain_ref, two_ref, w_own, w_far, w_near,
+    keep_ref, send_ref, whole, weight, terms,
+):
     step = pl.program_id(0)
-    whole[...] = dot_left(left_ref[...], right_ref[...]).astype(bf16)
+
+    @pl.when(step == 0)
+    def _():
+        place_weight(place_ref, weight, w_own, w_far, w_near)
+        terms[...] = jnp.zeros_like(terms)
+
+    grad = dot_left(left_ref[...], right_ref[...])
+    whole[...] = grad.astype(bf16)
+    width = whole.shape[1]
+    for start in range(0, weight.shape[1], width):
+        size = min(width, weight.shape[1] - start)
+
+        @pl.when(step == start // width)
+        def _():
+            total = terms[...]
+            for at in range(0, size, PAIR):
+                total += grad[:, at : at + PAIR] * weight[:, start + at : start + at + PAIR].astype(f32)
+            terms[...] = total
 
     @pl.when(step == pl.num_programs(0) - 1)
     def _():
         lane = lax.broadcasted_iota(jnp.int32, (1, PAIR), 1)
-        first, second = as_column(one_ref[...]), as_column(two_ref[...])
+        pick = jnp.where(lax.broadcasted_iota(jnp.int32, (2, PAIR), 0) == 0, 1.0, 0.0).astype(bf16)
+        first = jnp.sum(terms[...], -1, keepdims=True) / dot_left(gain_ref[...], pick)
+        second = as_column(two_ref[...])
         columns = jnp.where(lane == 0, first, jnp.where(lane == 1, second, 0.0)).astype(bf16)
-        at = whole.shape[1] - 2 * PAIR
+        at = width - 2 * PAIR
         whole[:, at : at + PAIR] = columns
         whole[:, at + PAIR :] = jnp.zeros_like(columns)
 
@@ -433,17 +455,14 @@
 
 
 def stream_back_kernel(
-    place_ref, dqkv_ref, tok_ref, dx1_ref, gain_ref, w_own, w_far, w_near, out_ref, gsum_ref, weight
+    place_ref, dqkv_ref, tok_ref, dx1_ref, gain_ref, w_own, w_far, w_near, out_ref, weight
 ):
     @pl.when(pl.program_id(0) == 0)
     def _():
         place_weight(place_ref, weight, w_own, w_far, w_near)
-        gsum_ref[...] = jnp.zeros_like(gsum_ref)
-
-    rows, width = tok_ref.shape
+
     grad_hidden = dot_right(dqkv_ref[...], weight[...])
     normed, factor = norm_parts(tok_ref[...].astype(f32))
-    gsum_ref[...] += jnp.sum((grad_hidden * normed).reshape(rows // 8, 8, width), 0)
     grad_normed = grad_hidden * gain_ref[0:1, :].astype(f32)
     out_ref[...] = (dx1_ref[...] + norm_back(grad_normed, normed, factor)).astype(bf16)
 
@@ -913,8 +932,39 @@
     grads, mark = back_part(0, few, ())
     grads, _ = back_part(few, num_seqs - few, chain_mlp.advance(mark), grads)
     flat_grad = grads.reshape(count, wider)
+    step_columns = wider // 2
+    part = shape_of(2, width // 4, wider)
+    block = (2, width // 4, step_columns)
+
+    def last_block(i):
+        return (0, 0, i)
+
+    keep, send = run(
+        grad_qkv_kernel,
+        wider // step_columns,
+        [
+            (place, None),
+            (hidden_one.reshape(count, width), None),
+            (flat_grad, (count, step_columns), column_block),
+            (gains, None),
+            (gain_sum_two, None),
+            *qkv_pieces,
+        ],
+        [(part, block, last_block), (part, block, last_block)],
+        [
+            pltpu.VMEM((width, step_columns), bf16),
+            pltpu.VMEM((width, 3 * width), bf16),
+            pltpu.VMEM((width, PAIR), f32),
+        ],
+        spare=16,
+    )
+    send, *chain_mlp.got = together(send, *chain_mlp.got)
+    chain_qkv = Chain(sum_stages(place, keep, send))
+    sent = chain_mlp.advance(keep)
+    sent = chain_qkv.advance(sent)
+    sent = chain_mlp.advance(sent)
     large = 4 * rows
-    grad_tokens, gain_sum_one = run(
+    (grad_tokens,) = run(
         stream_back_kernel,
         count // large,
         [
@@ -925,42 +975,13 @@
             (gains, None),
             *qkv_pieces,
         ],
-        [
-            (shape_of(count, width), (large, width), row_block),
-            (shape_of(8, width, dtype=f32), None),
-        ],
+        [(shape_of(count, width), (large, width), row_block)],
         [pltpu.VMEM((width, 3 * width), bf16)],
-        spare=12,
-    )
-    sent = chain_mlp.advance(gain_sum_one)
-    step_columns = wider // 2
-    part = shape_of(2, width // 4, wider)
-    block = (2, width // 4, step_columns)
-
-    def last_block(i):
-        return (0, 0, i)
-
-    keep, send = run(
-        grad_qkv_kernel,
-        wider // step_columns,
-        [
-            (place, None),
-            (hidden_one.reshape(count, width), None),
-            (flat_grad, (count, step_columns), column_block),
-            (gain_sum_one, None),
-            (gain_sum_two, None),
-        ],
-        [(part, block, last_block), (part, block, last_block)],
-        [pltpu.VMEM((width, step_columns), bf16)],
         later=sent,
         spare=12,
     )
-    send, *chain_mlp.got = together(send, *chain_mlp.got)
-    chain_qkv = Chain(sum_stages(place, keep, send))
-    sent = chain_mlp.advance()
-    sent = chain_qkv.advance(sent, gate=chain_mlp, arrived=2)
+    sent = chain_qkv.advance(grad_tokens, gate=chain_mlp, arrived=2)
     sent = chain_mlp.advance(sent)
-    sent = chain_qkv.advance(sent)
     while chain_mlp.result is None:
         sent = chain_qkv.advance(sent)
         sent = chain_mlp.advance(sent, gate=chain_qkv, arrived=len(chain_qkv.got))

time: 280 us -> 270 us (0.964)
  starting transfers between devices: 59.1 us -> 53.4 us
  waiting for transfers between devices: 62.4 us -> 57.5 us
    ppermute x22, starting transfers between devices: 43.3 us -> 37.3 us  [exchange(): lax.ppermute(block, 'seq', flip_route(lax.axis_size('seq'), distance))]
    ppermute x22, waiting for transfers between devices: 55.8 us -> 51.8 us  [exchange(): lax.ppermute(block, 'seq', flip_route(lax.axis_size('seq'), distance))]
    unnamed x68 -> x72, local copies, waits for them, and re-layouts: 11.4 us -> 8.5 us
  transfers between devices with their start and end apart: 34 -> 34, of which waited for: 17 -> 15; matrix products, arithmetic and copies ran while one was open for 6% -> 6% of each run, Pallas kernels for 33% -> 36%
where the time goes in v5:
time: 270 us; the launch traced here: 268 us
  Pallas kernels  131 us (49%)
  waiting for transfers between devices  57.5 us (21%)
  starting transfers between devices  53.4 us (20%)
  other arithmetic  15.5 us (6%)
  local copies, waits for them, and re-layouts  9.41 us (3%)
    pallas_call x23, Pallas kernels, run(): pl.pallas_call(body, grid=(grid,), in_specs=specs, out_specs=out_specs, o...  131 us
    ppermute x22, waiting for transfers between devices, exchange(): lax.ppermute(block, 'seq', flip_route(lax.axis_size('seq'), distance))  51.8 us
    ppermute x22, starting transfers between devices, exchange(): lax.ppermute(block, 'seq', flip_route(lax.axis_size('seq'), distance))  37.3 us
    unnamed x72, local copies, waits for them, and re-layouts  8.5 us
    ppermute x6, starting transfers between devices, exchange(): return lax.ppermute(block, 'fsdp', flip_route(2, 1))  7.12 us
    ppermute x4, starting transfers between devices, passed_along(): return lax.ppermute(block, axis, route)  6.19 us
  transfers between devices with their start and end apart: 34, of which 15 were waited for; matrix products, arithmetic and copies ran while one was open for 6% of the time, Pallas kernels for 36%

profile of v5, /device:TPU:0, one launch (start us, length us, event | category | flops | bytes accessed | tf_op | source)
XLA Modules:
  0.0 267.8 jit_solution(13836166231776980329)
XLA Ops:
  1.3 2.5 shard_map.135.refs_5_
  3.8 3.0 %collective-permute-start.1 = (bf16[208,2304]{1,0:T(8,128)(2,1)}, bf16[208,2304]{1,0:T(8,128)(2,1)S(1)}, u32[]{:S(2)}, u32[]{:S(2)}) collective-permute-start(bf16[208,2304]{1,0:T(8,128)(2,1)} %shard_map.135.refs_5_), channel_id=1, source_target_pairs={{0,1},{1,0},{2,3},{3,2},{4,5},{5,4},{6,7},{7,6},{8,9},{9,8},{10,11... | collective-permute-start | bytes 2875400 | tf_op jit(solution)/shard_map/ppermute | solution.py:562
  6.8 4.2 %shard_map.136 = (bf16[352,2304]{1,0:T(8,128)(2,1)}, bf16[8,64,768]{2,1,0:T(8,128)(2,1)}, bf16[8,64,768]{2,1,0:T(8,128)(2,1)}) custom-call(s32[5]{0:T(128)} %stack.19.refs_0_, bf16[384,768]{1,0:T(8,128)(2,1)} %refs_6_.1, bf16[384,2304]{1,0:T(8,128)(2,1)} %refs_7_.1, bf16[576,768]{1,0:T(8,128)(2,1)} %refs_8_.3, bf16[8,128,768]{2,1,0:T(8,128)(2,1)} %refs_2_.5, ...), custom_call_target="tpu_custom_call" | custom-call | flops 1 | bytes 1 | tf_op jit(solution)/shard_map/pallas_call | solution.py:536
  17.5 4.3 %fusion = (f32[8,256,32]{2,1,0:T(8,128)S(1)}, f32[8,256,32]{2,1,0:T(8,128)S(1)}, f32[8,256,32]{2,1,0:T(8,128)S(1)}) fusion(f32[32]{0:T(128)} %negate_power_fusion, f32[8,256]{1,0:T(8,128)S(1)} %convert_element_type.3), kind=kLoop, calls=%fused_computation.7 | loop fusion | flops 131072 | bytes 794752 | tf_op jit(solution)/shard_map/neg | solution.py:701
  23.3 3.0 %pad_maximum_fusion = (f32[8,256,128]{2,1,0:T(8,128)}, f32[8,256,128]{2,1,0:T(8,128)}) fusion(f32[8,256,32]{2,1,0:T(8,128)S(1)} %get-tuple-element.181, f32[8,256,32]{2,1,0:T(8,128)S(1)} %get-tuple-element.180, f32[8,256,32]{2,1,0:T(8,128)S(1)} %get-tuple-element.179), kind=kLoop, calls=%fused_computation.2 | loop fusion | flops 1572864 | bytes 2883584 | tf_op jit(solution)/shard_map/concatenate | solution.py:700
  30.3 2.8 %collective-permute-start.4 = (bf16[208,2304]{1,0:T(8,128)(2,1)S(1)}, bf16[208,2304]{1,0:T(8,128)(2,1)S(1)}, u32[]{:S(2)}, u32[]{:S(2)}) collective-permute-start(bf16[208,2304]{1,0:T(8,128)(2,1)S(1)} %collective-permute-done.1.refs_9_.refs_6_), channel_id=1, source_target_pairs={{0,2},{2,0},{4,6},{6,4},{8,10},{10,8},{12,14},{14,12},{16,18},{18,... | collective-permute-start | bytes 2875400 | tf_op jit(solution)/shard_map/ppermute | solution.py:557
  36.1 26.5 %shard_map.137 = (bf16[8,128,768]{2,1,0:T(8,128)(2,1)}, bf16[8,256,768]{2,1,0:T(8,128)(2,1)}, bf16[8,256,768]{2,1,0:T(8,128)(2,1)}, bf16[8,256,768]{2,1,0:T(8,12...) custom-call(s32[5]{0:T(128)} %stack.19.refs_0_, bf16[8,64,768]{2,1,0:T(8,128)(2,1)} %copy-done.24, ...), custom_call_target="tpu_custom_call" | custom-call | flops 1 | bytes 1 | tf_op jit(solution)/shard_map/pallas_call | solution.py:536
  63.1 3.4 %collective-permute-done.5.refs_10_ = bf16[352,2304]{1,0:T(8,128)(2,1)S(1)} collective-permute-done((bf16[352,2304]{1,0:T(8,128)(2,1)S(1)}, bf16[352,2304]{1,0:T(8,128)(2,1)S(1)}, u32[]{:S(2)}, u32[]{:S(2)}) %collective-permute-start.5) | collective-permute-done | bytes 1622048 | tf_op jit(solution)/shard_map/ppermute | solution.py:557
  67.6 27.3 %shard_map.138 = (bf16[1024,768]{1,0:T(8,128)(2,1)}, f32[1024,768]{1,0:T(8,128)}, bf16[1024,768]{1,0:T(8,128)(2,1)}, bf16[8,80,768]{2,1,0:T(8,128)(2,1)}, bf16[8...) custom-call(s32[5]{0:T(128)} %stack.19.refs_0_, ...), custom_call_target="tpu_custom_call" | custom-call | flops 1 | bytes 1 | tf_op jit(solution)/shard_map/pallas_call | solution.py:536
  94.9 2.1 collective-permute-start.6
  98.3 14.7 %shard_map.139 = (bf16[2,1088,768]{2,1,0:T(8,128)(2,1)}, bf16[2,1088,768]{2,1,0:T(8,128)(2,1)}) custom-call(s32[5]{0:T(128)} %stack.19.refs_0_, bf16[1024,768]{1,0:T(8,128)(2,1)} %get-tuple-element.109.refs_1_, bf16[1024,2304]{1,0:T(8,128)(2,1)} %get-tuple-element.110.refs_2_, bf16[1024,1152]{1,0:T(8,128)(2,1)} %get-tuple-element.111.refs_3_, ...), custom_call_target="tpu_custom_call" | custom-call | flops 1 | bytes 1 | tf_op jit(solution)/shard_map/pallas_call | solution.py:536
  113.0 8.2 %collective-permute-start.8 = (bf16[2,1088,768]{2,1,0:T(8,128)(2,1)}, bf16[2,1088,768]{2,1,0:T(8,128)(2,1)S(1)}, u32[]{:S(2)}, u32[]{:S(2)}) collective-permute-start(bf16[2,1088,768]{2,1,0:T(8,128)(2,1)} %get-tuple-element.121), channel_id=1, source_target_pairs={{0,2},{2,0},{4,6},{6,4},{8,10},{10,8},{12,14},{14,12},{16,18},{18,... | collective-permute-start | bytes 10027016 | tf_op jit(solution)/shard_map/ppermute | solution.py:563
  121.2 11.2 %shard_map.140 = (bf16[8,128,2560]{2,1,0:T(8,128)(2,1)}, f32[8,128]{1,0:T(8,128)}) custom-call(bf16[8,256,768]{2,1,0:T(8,128)(2,1)} %get-tuple-element.103.refs_0_, bf16[8,256,768]{2,1,0:T(8,128)(2,1)} %get-tuple-element.104.refs_1_, bf16[8,256,768]{2,1,0:T(8,128)(2,1)} %get-tuple-element.105.refs_2_, bf16[8,128,768]{2,1,0:T(8,128)(2,1)} %bitcast.71, ...), custom_call_target="tpu_custom_call" | custom-call | flops 1 | bytes 1 | tf_op jit(solution)/shard_map/pallas_call | solution.py:536
  133.1 2.1 shard_map.141
  138.0 3.5 %collective-permute-start.10 = (bf16[2,544,384]{2,1,0:T(8,128)(2,1)S(1)}, bf16[2,544,384]{2,1,0:T(8,128)(2,1)}, u32[]{:S(2)}, u32[]{:S(2)}) collective-permute-start(bf16[2,544,384]{2,1,0:T(8,128)(2,1)S(1)} %get-tuple-element.124.refs_15_), channel_id=1, source_target_pairs={{0,4},{2,6},{4,0},{6,2},{8,12},{10,14},{12,8},{14,10},{16,20},{18,... | collective-permute-start | bytes 2506760 | tf_op jit(solution)/shard_map/ppermute | solution.py:563
  141.6 11.2 %shard_map.142 = (bf16[8,128,2560]{2,1,0:T(8,128)(2,1)}, f32[8,128]{1,0:T(8,128)}) custom-call(bf16[8,256,768]{2,1,0:T(8,128)(2,1)} %get-tuple-element.103.refs_0_, bf16[8,256,768]{2,1,0:T(8,128)(2,1)} %get-tuple-element.104.refs_1_, bf16[8,256,768]{2,1,0:T(8,128)(2,1)} %get-tuple-element.105.refs_2_, ...), custom_call_target="tpu_custom_call", output_to_operand_aliasing={{0}: (13, {})} | custom-call | flops 1 | bytes 1 | tf_op jit(solution)/shard_map/pallas_call | solution.py:536
  152.9 8.2 %shard_map.143 = (bf16[2,192,2560]{2,1,0:T(8,128)(2,1)S(1)}, bf16[2,192,2560]{2,1,0:T(8,128)(2,1)S(1)}) custom-call(s32[5]{0:T(128)S(1)} %copy-done.16, bf16[1024,768]{1,0:T(8,128)(2,1)S(1)} %bitcast.56, bf16[1024,2560]{1,0:T(8,128)(2,1)} %bitcast.34, bf16[2,768]{1,0:T(2,128)(2,1)S(1)} %copy-done.17, f32[8,768]{1,0:T(8,128)S(1)} %copy-done.18, ...), custom_call_target="tpu_custom_call" | custom-call | flops 1 | bytes 1 | tf_op jit(solution)/shard_map/pallas_call | solution.py:536
  168.8 6.9 %collective-permute-done.11 = bf16[544,384]{1,0:T(8,128)(2,1)S(1)} collective-permute-done((bf16[544,384]{1,0:T(8,128)(2,1)S(1)}, bf16[544,384]{1,0:T(8,128)(2,1)S(1)}, u32[]{:S(2)}, u32[]{:S(2)}) %collective-permute-start.11) | collective-permute-done | bytes 417824 | tf_op jit(solution)/shard_map/ppermute | solution.py:563
  176.6 2.9 %collective-permute-start.16 = (bf16[136,768]{1,0:T(8,128)(2,1)S(1)}, bf16[136,768]{1,0:T(8,128)(2,1)S(1)}, u32[]{:S(2)}, u32[]{:S(2)}) collective-permute-start(bf16[136,768]{1,0:T(8,128)(2,1)S(1)} %get-tuple-element.141.refs_8_), channel_id=1, source_target_pairs={{0,8},{2,10},{4,12},{6,14},{8,0},{10,2},{12,4},{14,6},{16,24},{18,... | collective-permute-start | bytes 626696 | tf_op jit(solution)/shard_map/ppermute | solution.py:563
  179.5 2.6 collective-permute-start.17
  182.1 6.9 %shard_map.147.refs_5_ = bf16[1024,768]{1,0:T(8,128)(2,1)} custom-call(s32[5]{0:T(128)S(1)} %copy-done.16, bf16[1024,2560]{1,0:T(8,128)(2,1)S(1)} %bitcast.37, bf16[1024,768]{1,0:T(8,128)(2,1)S(1)} %bitcast.43, f32[1024,768]{1,0:T(8,128)S(1)} %copy-done.8, bf16[2,768]{1,0:T(2,128)(2,1)S(1)} %copy-done.17, bf16[384,2304]{1,0:T(8,128)(2,1)S(1)} %copy-done, ...), custom_call_target="tpu_custom_call" | custom-call | flops 1 | bytes 1 | tf_op jit(solution)/shard_map/pallas_call | solution.py:536
  191.4 5.5 %collective-permute-done.17 = bf16[136,768]{1,0:T(8,128)(2,1)S(1)} collective-permute-done((bf16[136,768]{1,0:T(8,128)(2,1)S(1)}, bf16[136,768]{1,0:T(8,128)(2,1)S(1)}, u32[]{:S(2)}, u32[]{:S(2)}) %collective-permute-start.17) | collective-permute-done | bytes 208928 | tf_op jit(solution)/shard_map/ppermute | solution.py:563
  199.5 2.0 collective-permute-start.23
  201.5 2.6 collective-permute-start.22
  209.3 2.1 collective-permute-start.26
  211.3 14.7 %collective-permute-done.22.refs_3_ = bf16[136,768]{1,0:T(8,128)(2,1)S(1)} collective-permute-done((bf16[136,768]{1,0:T(8,128)(2,1)S(1)}, bf16[136,768]{1,0:T(8,128)(2,1)S(1)}, u32[]{:S(2)}, u32[]{:S(2)}) %collective-permute-start.22) | collective-permute-done | bytes 208928 | tf_op jit(solution)/shard_map/ppermute | solution.py:563
  229.7 2.2 collective-permute-start.30
  234.2 11.0 %collective-permute-done.27.refs_2_ = bf16[544,768]{1,0:T(8,128)(2,1)S(1)} collective-permute-done((bf16[544,768]{1,0:T(8,128)(2,1)S(1)}, bf16[544,768]{1,0:T(8,128)(2,1)S(1)}, u32[]{:S(2)}, u32[]{:S(2)}) %collective-permute-start.27) | collective-permute-done | bytes 835616 | tf_op jit(solution)/shard_map/ppermute | solution.py:563
  249.8 3.6 %shard_map.155 = (f32[384,2304]{1,0:T(8,128)}, f32[576,768]{1,0:T(8,128)}, f32[384,768]{1,0:T(8,128)}) custom-call(s32[5]{0:T(128)S(1)} %copy-done.16, bf16[1088,768]{1,0:T(8,128)(2,1)S(1)} %bitcast.40, bf16[1088,768]{1,0:T(8,128)(2,1)S(1)} %collective-permute-done.32.refs_2_, bf16[1088,768]{1,0:T(8,128)(2,1)S(1)} %bitcast.41), custom_call_target="tpu_custom_call" | custom-call | flops 1 | bytes 1 | tf_op jit(solution)/shard_map/pallas_call | solution.py:536
  253.4 7.1 %collective-permute-done.31.refs_2_ = bf16[96,2560]{1,0:T(8,128)(2,1)S(1)} collective-permute-done((bf16[96,2560]{1,0:T(8,128)(2,1)S(1)}, bf16[96,2560]{1,0:T(8,128)(2,1)S(1)}, u32[]{:S(2)}, u32[]{:S(2)}) %collective-permute-start.31) | collective-permute-done | bytes 491552 | tf_op jit(solution)/shard_map/ppermute | solution.py:563
  262.7 2.6 collective-permute-done.33.refs_2_
  265.3 2.6 shard_map.157
  (158 shorter events, 53.4 us)
Async XLA Ops:
  3.8 25.6 %collective-permute-start.1 = (bf16[208,2304]{1,0:T(8,128)(2,1)}, bf16[208,2304]{1,0:T(8,128)(2,1)S(1)}, u32[]{:S(2)}, u32[]{:S(2)}) collective-permute-start(bf16[208,2304]{1,0:T(8,128)(2,1)} %shard_map.135.refs_5_), channel_id=1, source_target_pairs={{0,1},{1,0},{2,3},{3,2},{4,5},{5,4},{6,7},{7,6},{8,9},{9,8},{10,11... | collective-permute-start | bytes 2875400 | tf_op jit(solution)/shard_map/ppermute | solution.py:562
  11.0 18.4 %collective-permute-start.2 = (bf16[8,64,768]{2,1,0:T(8,128)(2,1)}, bf16[8,64,768]{2,1,0:T(8,128)(2,1)S(1)}, u32[]{:S(2)}, u32[]{:S(2)}) collective-permute-start(bf16[8,64,768]{2,1,0:T(8,128)(2,1)} %get-tuple-element.90), channel_id=1, source_target_pairs={{0,2},{2,4},{4,6},{6,8},{8,10},{10,12},{12,14},{14,16},{16,18},{18... | collective-permute-start | bytes 2359304 | tf_op jit(solution)/shard_map/ppermute | solution.py:29
  12.5 16.9 %collective-permute-start.3 = (bf16[8,64,768]{2,1,0:T(8,128)(2,1)}, bf16[8,64,768]{2,1,0:T(8,128)(2,1)}, u32[]{:S(2)}, u32[]{:S(2)}) collective-permute-start(bf16[8,64,768]{2,1,0:T(8,128)(2,1)} %get-tuple-element.91), channel_id=1, source_target_pairs={{2,0},{4,2},{6,4},{8,6},{10,8},{12,10},{14,12},{16,14},{18,16},{20... | collective-permute-start | bytes 2359304 | tf_op jit(solution)/shard_map/ppermute | solution.py:29
  13.8 49.2 %collective-permute-start = (bf16[352,2304]{1,0:T(8,128)(2,1)}, bf16[352,2304]{1,0:T(8,128)(2,1)S(1)}, u32[]{:S(2)}, u32[]{:S(2)}) collective-permute-start(bf16[352,2304]{1,0:T(8,128)(2,1)} %get-tuple-element.89), channel_id=1, source_target_pairs={{0,1},{1,0},{2,3},{3,2},{4,5},{5,4},{6,7},{7,6},{8,9},{9,8},{10,11... | collective-permute-start | bytes 4866056 | tf_op jit(solution)/shard_map/ppermute | solution.py:562
  30.3 4.9 %collective-permute-start.4 = (bf16[208,2304]{1,0:T(8,128)(2,1)S(1)}, bf16[208,2304]{1,0:T(8,128)(2,1)S(1)}, u32[]{:S(2)}, u32[]{:S(2)}) collective-permute-start(bf16[208,2304]{1,0:T(8,128)(2,1)S(1)} %collective-permute-done.1.refs_9_.refs_6_), channel_id=1, source_target_pairs={{0,2},{2,0},{4,6},{6,4},{8,10},{10,8},{12,14},{14,12},{16,18},{18,... | collective-permute-start | bytes 2875400 | tf_op jit(solution)/shard_map/ppermute | solution.py:557
  94.9 18.1 %collective-permute-start.6 = (bf16[8,80,768]{2,1,0:T(8,128)(2,1)}, bf16[8,80,768]{2,1,0:T(8,128)(2,1)S(1)}, u32[]{:S(2)}, u32[]{:S(2)}) collective-permute-start(bf16[8,80,768]{2,1,0:T(8,128)(2,1)} %get-tuple-element.107), channel_id=1, source_target_pairs={{0,2},{2,4},{4,6},{6,8},{8,10},{10,12},{12,14},{14,16},{16,18},{18... | collective-permute-start | bytes 2949128 | tf_op jit(solution)/shard_map/ppermute | solution.py:29
  97.0 16.0 %collective-permute-start.7 = (bf16[8,80,768]{2,1,0:T(8,128)(2,1)}, bf16[8,80,768]{2,1,0:T(8,128)(2,1)S(1)}, u32[]{:S(2)}, u32[]{:S(2)}) collective-permute-start(bf16[8,80,768]{2,1,0:T(8,128)(2,1)} %get-tuple-element.108), channel_id=1, source_target_pairs={{2,0},{4,2},{6,4},{8,6},{10,8},{12,10},{14,12},{16,14},{18,16},{20... | collective-permute-start | bytes 2949128 | tf_op jit(solution)/shard_map/ppermute | solution.py:29
  113.0 19.3 %collective-permute-start.8 = (bf16[2,1088,768]{2,1,0:T(8,128)(2,1)}, bf16[2,1088,768]{2,1,0:T(8,128)(2,1)S(1)}, u32[]{:S(2)}, u32[]{:S(2)}) collective-permute-start(bf16[2,1088,768]{2,1,0:T(8,128)(2,1)} %get-tuple-element.121), channel_id=1, source_target_pairs={{0,2},{2,0},{4,6},{6,4},{8,10},{10,8},{12,14},{14,12},{16,18},{18,... | collective-permute-start | bytes 10027016 | tf_op jit(solution)/shard_map/ppermute | solution.py:563
  137.1 24.0 %collective-permute-start.9 = (bf16[2,544,384]{2,1,0:T(8,128)(2,1)}, bf16[2,544,384]{2,1,0:T(8,128)(2,1)}, u32[]{:S(2)}, u32[]{:S(2)}) collective-permute-start(bf16[2,544,384]{2,1,0:T(8,128)(2,1)} %get-tuple-element.123.refs_14_), channel_id=1, source_target_pairs={{0,1},{1,0},{2,3},{3,2},{4,5},{5,4},{6,7},{7,6},{8,9},{9,8},{10,11... | collective-permute-start | bytes 2506760 | tf_op jit(solution)/shard_map/ppermute | solution.py:562
  138.0 23.1 %collective-permute-start.10 = (bf16[2,544,384]{2,1,0:T(8,128)(2,1)S(1)}, bf16[2,544,384]{2,1,0:T(8,128)(2,1)}, u32[]{:S(2)}, u32[]{:S(2)}) collective-permute-start(bf16[2,544,384]{2,1,0:T(8,128)(2,1)S(1)} %get-tuple-element.124.refs_15_), channel_id=1, source_target_pairs={{0,4},{2,6},{4,0},{6,2},{8,12},{10,14},{12,8},{14,10},{16,20},{18,... | collective-permute-start | bytes 2506760 | tf_op jit(solution)/shard_map/ppermute | solution.py:563
  161.1 4.0 %collective-permute-start.13 = (bf16[2,192,2560]{2,1,0:T(8,128)(2,1)S(1)}, bf16[2,192,2560]{2,1,0:T(8,128)(2,1)S(1)}, u32[]{:S(2)}, u32[]{:S(2)}) collective-permute-start(bf16[2,192,2560]{2,1,0:T(8,128)(2,1)S(1)} %get-tuple-element.138), channel_id=1, source_target_pairs={{0,2},{2,0},{4,6},{6,4},{8,10},{10,8},{12,14},{14,12},{16,18},{18,... | collective-permute-start | bytes 5898248 | tf_op jit(solution)/shard_map/ppermute | solution.py:563
  163.2 12.5 %collective-permute-start.11 = (bf16[544,384]{1,0:T(8,128)(2,1)S(1)}, bf16[544,384]{1,0:T(8,128)(2,1)S(1)}, u32[]{:S(2)}, u32[]{:S(2)}) collective-permute-start(bf16[544,384]{1,0:T(8,128)(2,1)S(1)} %get-tuple-element.136.refs_3_), channel_id=1, source_target_pairs={{0,4},{2,6},{4,0},{6,2},{8,12},{10,14},{12,8},{14,10},{16,20},{18,... | collective-permute-start | bytes 1253384 | tf_op jit(solution)/shard_map/ppermute | solution.py:563
  163.3 12.5 %collective-permute-start.12 = (bf16[544,384]{1,0:T(8,128)(2,1)S(1)}, bf16[544,384]{1,0:T(8,128)(2,1)S(1)}, u32[]{:S(2)}, u32[]{:S(2)}) collective-permute-start(bf16[544,384]{1,0:T(8,128)(2,1)S(1)} %get-tuple-element.137.refs_4_), channel_id=1, source_target_pairs={{0,1},{1,0},{2,3},{3,2},{4,5},{5,4},{6,7},{7,6},{8,9},{9,8},{10,11... | collective-permute-start | bytes 1253384 | tf_op jit(solution)/shard_map/ppermute | solution.py:562
  166.6 22.4 %collective-permute-start.14 = (bf16[2,96,1280]{2,1,0:T(8,128)(2,1)S(1)}, bf16[2,96,1280]{2,1,0:T(8,128)(2,1)S(1)}, u32[]{:S(2)}, u32[]{:S(2)}) collective-permute-start(bf16[2,96,1280]{2,1,0:T(8,128)(2,1)S(1)} %get-tuple-element.139.refs_4_), channel_id=1, source_target_pairs={{0,1},{1,0},{2,3},{3,2},{4,5},{5,4},{6,7},{7,6},{8,9},{9,8},{10,11... | collective-permute-start | bytes 1474568 | tf_op jit(solution)/shard_map/ppermute | solution.py:562
  167.7 21.2 %collective-permute-start.15 = (bf16[2,96,1280]{2,1,0:T(8,128)(2,1)S(1)}, bf16[2,96,1280]{2,1,0:T(8,128)(2,1)S(1)}, u32[]{:S(2)}, u32[]{:S(2)}) collective-permute-start(bf16[2,96,1280]{2,1,0:T(8,128)(2,1)S(1)} %get-tuple-element.140.refs_5_), channel_id=1, source_target_pairs={{0,4},{2,6},{4,0},{6,2},{8,12},{10,14},{12,8},{14,10},{16,20},{18,... | collective-permute-start | bytes 1474568 | tf_op jit(solution)/shard_map/ppermute | solution.py:563
  176.6 14.8 %collective-permute-start.16 = (bf16[136,768]{1,0:T(8,128)(2,1)S(1)}, bf16[136,768]{1,0:T(8,128)(2,1)S(1)}, u32[]{:S(2)}, u32[]{:S(2)}) collective-permute-start(bf16[136,768]{1,0:T(8,128)(2,1)S(1)} %get-tuple-element.141.refs_8_), channel_id=1, source_target_pairs={{0,8},{2,10},{4,12},{6,14},{8,0},{10,2},{12,4},{14,6},{16,24},{18,... | collective-permute-start | bytes 626696 | tf_op jit(solution)/shard_map/ppermute | solution.py:563
  179.5 17.4 %collective-permute-start.17 = (bf16[136,768]{1,0:T(8,128)(2,1)S(1)}, bf16[136,768]{1,0:T(8,128)(2,1)S(1)}, u32[]{:S(2)}, u32[]{:S(2)}) collective-permute-start(bf16[136,768]{1,0:T(8,128)(2,1)S(1)} %get-tuple-element.142.refs_9_), channel_id=1, source_target_pairs={{0,16},{2,18},{4,20},{6,22},{8,24},{10,26},{12,28},{14,30},{16,0},... | collective-permute-start | bytes 626696 | tf_op jit(solution)/shard_map/ppermute | solution.py:563
  182.1 16.8 %collective-permute-start.20 = (bf16[136,768]{1,0:T(8,128)(2,1)S(1)}, bf16[136,768]{1,0:T(8,128)(2,1)S(1)}, u32[]{:S(2)}, u32[]{:S(2)}) collective-permute-start(bf16[136,768]{1,0:T(8,128)(2,1)S(1)} %get-tuple-element.143.refs_10_), channel_id=1, source_target_pairs={{0,24},{2,26},{4,28},{6,30},{8,16},{10,18},{12,20},{14,22},{16,8},... | collective-permute-start | bytes 626696 | tf_op jit(solution)/shard_map/ppermute | solution.py:563
  196.9 7.3 %collective-permute-start.18 = (bf16[96,1280]{1,0:T(8,128)(2,1)S(1)}, bf16[96,1280]{1,0:T(8,128)(2,1)S(1)}, u32[]{:S(2)}, u32[]{:S(2)}) collective-permute-start(bf16[96,1280]{1,0:T(8,128)(2,1)S(1)} %get-tuple-element.149.refs_5_), channel_id=1, source_target_pairs={{0,4},{2,6},{4,0},{6,2},{8,12},{10,14},{12,8},{14,10},{16,20},{18,... | collective-permute-start | bytes 737288 | tf_op jit(solution)/shard_map/ppermute | solution.py:563
  198.3 6.2 %collective-permute-start.19 = (bf16[96,1280]{1,0:T(8,128)(2,1)S(1)}, bf16[96,1280]{1,0:T(8,128)(2,1)S(1)}, u32[]{:S(2)}, u32[]{:S(2)}) collective-permute-start(bf16[96,1280]{1,0:T(8,128)(2,1)S(1)} %get-tuple-element.150.refs_6_), channel_id=1, source_target_pairs={{0,1},{1,0},{2,3},{3,2},{4,5},{5,4},{6,7},{7,6},{8,9},{9,8},{10,11... | collective-permute-start | bytes 737288 | tf_op jit(solution)/shard_map/ppermute | solution.py:562
  199.5 9.8 %collective-permute-start.23 = (bf16[136,768]{1,0:T(8,128)(2,1)S(1)}, bf16[136,768]{1,0:T(8,128)(2,1)S(1)}, u32[]{:S(2)}, u32[]{:S(2)}) collective-permute-start(bf16[136,768]{1,0:T(8,128)(2,1)S(1)} %shard_map.149.refs_4_.refs_5_.refs_6_.refs_1_), channel_id=1, source_target_pairs={{0,24},{2,26},{4,28},{6,30},{8,16},{10,18},{12,20},{14,22},{16,8},... | collective-permute-start | bytes 626696 | tf_op jit(solution)/shard_map/ppermute | solution.py:563
  201.5 24.5 %collective-permute-start.22 = (bf16[136,768]{1,0:T(8,128)(2,1)S(1)}, bf16[136,768]{1,0:T(8,128)(2,1)S(1)}, u32[]{:S(2)}, u32[]{:S(2)}) collective-permute-start(bf16[136,768]{1,0:T(8,128)(2,1)S(1)} %shard_map.149.refs_4_.refs_5_.refs_6_.refs_1_), channel_id=1, source_target_pairs={{0,16},{2,18},{4,20},{6,22},{8,24},{10,26},{12,28},{14,30},{16,0},... | collective-permute-start | bytes 626696 | tf_op jit(solution)/shard_map/ppermute | solution.py:563
  204.1 21.9 %collective-permute-start.21 = (bf16[136,768]{1,0:T(8,128)(2,1)S(1)}, bf16[136,768]{1,0:T(8,128)(2,1)S(1)}, u32[]{:S(2)}, u32[]{:S(2)}) collective-permute-start(bf16[136,768]{1,0:T(8,128)(2,1)S(1)} %shard_map.149.refs_4_.refs_5_.refs_6_.refs_1_), channel_id=1, source_target_pairs={{0,8},{2,10},{4,12},{6,14},{8,0},{10,2},{12,4},{14,6},{16,24},{18,... | collective-permute-start | bytes 626696 | tf_op jit(solution)/shard_map/ppermute | solution.py:563
  205.2 21.7 %collective-permute-start.24 = (bf16[24,2560]{1,0:T(8,128)(2,1)S(1)}, bf16[24,2560]{1,0:T(8,128)(2,1)S(1)}, u32[]{:S(2)}, u32[]{:S(2)}) collective-permute-start(bf16[24,2560]{1,0:T(8,128)(2,1)S(1)} %get-tuple-element.155.refs_5_), channel_id=1, source_target_pairs={{0,8},{2,10},{4,12},{6,14},{8,0},{10,2},{12,4},{14,6},{16,24},{18,... | collective-permute-start | bytes 368648 | tf_op jit(solution)/shard_map/ppermute | solution.py:563
  206.9 20.8 %collective-permute-start.25 = (bf16[24,2560]{1,0:T(8,128)(2,1)S(1)}, bf16[24,2560]{1,0:T(8,128)(2,1)S(1)}, u32[]{:S(2)}, u32[]{:S(2)}) collective-permute-start(bf16[24,2560]{1,0:T(8,128)(2,1)S(1)} %get-tuple-element.156.refs_6_), channel_id=1, source_target_pairs={{0,16},{2,18},{4,20},{6,22},{8,24},{10,26},{12,28},{14,30},{16,0},... | collective-permute-start | bytes 368648 | tf_op jit(solution)/shard_map/ppermute | solution.py:563
  209.3 18.4 %collective-permute-start.26 = (bf16[24,2560]{1,0:T(8,128)(2,1)S(1)}, bf16[24,2560]{1,0:T(8,128)(2,1)S(1)}, u32[]{:S(2)}, u32[]{:S(2)}) collective-permute-start(bf16[24,2560]{1,0:T(8,128)(2,1)S(1)} %get-tuple-element.157.refs_7_), channel_id=1, source_target_pairs={{0,24},{2,26},{4,28},{6,30},{8,16},{10,18},{12,20},{14,22},{16,8},... | collective-permute-start | bytes 368648 | tf_op jit(solution)/shard_map/ppermute | solution.py:563
  227.7 17.5 %collective-permute-start.27 = (bf16[544,768]{1,0:T(8,128)(2,1)S(1)}, bf16[544,768]{1,0:T(8,128)(2,1)S(1)}, u32[]{:S(2)}, u32[]{:S(2)}) collective-permute-start(bf16[544,768]{1,0:T(8,128)(2,1)S(1)} %bitcast.45), channel_id=1, source_target_pairs={{0,4},{2,6},{4,0},{6,2},{8,12},{10,14},{12,8},{14,10},{16,20},{18,... | collective-permute-start | bytes 2506760 | tf_op jit(solution)/shard_map/ppermute | solution.py:563
  229.7 16.4 %collective-permute-start.30 = (bf16[24,2560]{1,0:T(8,128)(2,1)S(1)}, bf16[24,2560]{1,0:T(8,128)(2,1)S(1)}, u32[]{:S(2)}, u32[]{:S(2)}) collective-permute-start(bf16[24,2560]{1,0:T(8,128)(2,1)S(1)} %shard_map.152.refs_3_.refs_4_.refs_5_.refs_1_), channel_id=1, source_target_pairs={{0,24},{2,26},{4,28},{6,30},{8,16},{10,18},{12,20},{14,22},{16,8},... | collective-permute-start | bytes 368648 | tf_op jit(solution)/shard_map/ppermute | solution.py:563
  231.9 14.3 %collective-permute-start.29 = (bf16[24,2560]{1,0:T(8,128)(2,1)S(1)}, bf16[24,2560]{1,0:T(8,128)(2,1)S(1)}, u32[]{:S(2)}, u32[]{:S(2)}) collective-permute-start(bf16[24,2560]{1,0:T(8,128)(2,1)S(1)} %shard_map.152.refs_3_.refs_4_.refs_5_.refs_1_), channel_id=1, source_target_pairs={{0,16},{2,18},{4,20},{6,22},{8,24},{10,26},{12,28},{14,30},{16,0},... | collective-permute-start | bytes 368648 | tf_op jit(solution)/shard_map/ppermute | solution.py:563
  233.1 13.0 %collective-permute-start.28 = (bf16[24,2560]{1,0:T(8,128)(2,1)S(1)}, bf16[24,2560]{1,0:T(8,128)(2,1)S(1)}, u32[]{:S(2)}, u32[]{:S(2)}) collective-permute-start(bf16[24,2560]{1,0:T(8,128)(2,1)S(1)} %shard_map.152.refs_3_.refs_4_.refs_5_.refs_1_), channel_id=1, source_target_pairs={{0,8},{2,10},{4,12},{6,14},{8,0},{10,2},{12,4},{14,6},{16,24},{18,... | collective-permute-start | bytes 368648 | tf_op jit(solution)/shard_map/ppermute | solution.py:563
  246.2 3.6 %collective-permute-start.32 = (bf16[1088,768]{1,0:T(8,128)(2,1)S(1)}, bf16[1088,768]{1,0:T(8,128)(2,1)S(1)}, u32[]{:S(2)}, u32[]{:S(2)}) collective-permute-start(bf16[1088,768]{1,0:T(8,128)(2,1)S(1)} %bitcast.38), channel_id=1, source_target_pairs={{0,2},{2,0},{4,6},{6,4},{8,10},{10,8},{12,14},{14,12},{16,18},{18,... | collective-permute-start | bytes 5013512 | tf_op jit(solution)/shard_map/ppermute | solution.py:563
  246.8 13.7 %collective-permute-start.31 = (bf16[96,2560]{1,0:T(8,128)(2,1)S(1)}, bf16[96,2560]{1,0:T(8,128)(2,1)S(1)}, u32[]{:S(2)}, u32[]{:S(2)}) collective-permute-start(bf16[96,2560]{1,0:T(8,128)(2,1)S(1)} %bitcast.54), channel_id=1, source_target_pairs={{0,4},{2,6},{4,0},{6,2},{8,12},{10,14},{12,8},{14,10},{16,20},{18,... | collective-permute-start | bytes 1474568 | tf_op jit(solution)/shard_map/ppermute | solution.py:563
  (38 other events, 281.9 us)

commit v6 on v5

--- a/solution.py
+++ b/solution.py
@@ -982,9 +982,13 @@
     )
     sent = chain_qkv.advance(grad_tokens, gate=chain_mlp, arrived=2)
     sent = chain_mlp.advance(sent)
-    while chain_mlp.result is None:
+    for _ in range(2 * len(bit_groups()) - 5):
         sent = chain_qkv.advance(sent)
         sent = chain_mlp.advance(sent, gate=chain_qkv, arrived=len(chain_qkv.got))
+    sent = chain_qkv.advance(sent)
+    sent = chain_qkv.advance(sent)
+    while chain_mlp.result is None:
+        chain_mlp.advance(sent)
     in_sum, down_sum, out_sum = run(
         finish_three_kernel,
         1,

time: 270 us -> 269 us (level)
  transfers between devices with their start and end apart: 34 -> 34, of which waited for: 15 -> 17; matrix products, arithmetic and copies ran while one was open for 6% -> 6% of each run, Pallas kernels for 36% -> 35%
where the time goes in v6:
time: 269 us; the launch traced here: 267 us
  Pallas kernels  131 us (49%)
  waiting for transfers between devices  56.9 us (21%)
  starting transfers between devices  53.4 us (20%)
  other arithmetic  15.5 us (6%)
  local copies, waits for them, and re-layouts  9.41 us (3%)
    pallas_call x23, Pallas kernels, run(): pl.pallas_call(body, grid=(grid,), in_specs=specs, out_specs=out_specs, o...  131 us
    ppermute x22, waiting for transfers between devices, exchange(): lax.ppermute(block, 'seq', flip_route(lax.axis_size('seq'), distance))  51.2 us
    ppermute x22, starting transfers between devices, exchange(): lax.ppermute(block, 'seq', flip_route(lax.axis_size('seq'), distance))  37.3 us
    unnamed x72, local copies, waits for them, and re-layouts  8.5 us
    ppermute x6, starting transfers between devices, exchange(): return lax.ppermute(block, 'fsdp', flip_route(2, 1))  7.12 us
    ppermute x4, starting transfers between devices, passed_along(): return lax.ppermute(block, axis, route)  6.19 us
  transfers between devices with their start and end apart: 34, of which 17 were waited for; matrix products, arithmetic and copies ran while one was open for 6% of the time, Pallas kernels for 35%

profile of v6, /device:TPU:0, one launch (start us, length us, event | category | flops | bytes accessed | tf_op | source)
XLA Modules:
  0.0 267.2 jit_solution(13230499445324013666)
XLA Ops:
  1.3 2.5 shard_map.135.refs_5_
  3.8 3.0 %collective-permute-start.1 = (bf16[208,2304]{1,0:T(8,128)(2,1)}, bf16[208,2304]{1,0:T(8,128)(2,1)S(1)}, u32[]{:S(2)}, u32[]{:S(2)}) collective-permute-start(bf16[208,2304]{1,0:T(8,128)(2,1)} %shard_map.135.refs_5_), channel_id=1, source_target_pairs={{0,1},{1,0},{2,3},{3,2},{4,5},{5,4},{6,7},{7,6},{8,9},{9,8},{10,11... | collective-permute-start | bytes 2875400 | tf_op jit(solution)/shard_map/ppermute | solution.py:562
  6.8 4.2 %shard_map.136 = (bf16[352,2304]{1,0:T(8,128)(2,1)}, bf16[8,64,768]{2,1,0:T(8,128)(2,1)}, bf16[8,64,768]{2,1,0:T(8,128)(2,1)}) custom-call(s32[5]{0:T(128)} %stack.19.refs_0_, bf16[384,768]{1,0:T(8,128)(2,1)} %refs_6_.1, bf16[384,2304]{1,0:T(8,128)(2,1)} %refs_7_.1, bf16[576,768]{1,0:T(8,128)(2,1)} %refs_8_.3, bf16[8,128,768]{2,1,0:T(8,128)(2,1)} %refs_2_.5, ...), custom_call_target="tpu_custom_call" | custom-call | flops 1 | bytes 1 | tf_op jit(solution)/shard_map/pallas_call | solution.py:536
  17.5 4.3 %fusion = (f32[8,256,32]{2,1,0:T(8,128)S(1)}, f32[8,256,32]{2,1,0:T(8,128)S(1)}, f32[8,256,32]{2,1,0:T(8,128)S(1)}) fusion(f32[32]{0:T(128)} %negate_power_fusion, f32[8,256]{1,0:T(8,128)S(1)} %convert_element_type.3), kind=kLoop, calls=%fused_computation.7 | loop fusion | flops 131072 | bytes 794752 | tf_op jit(solution)/shard_map/neg | solution.py:701
  23.3 3.0 %pad_maximum_fusion = (f32[8,256,128]{2,1,0:T(8,128)}, f32[8,256,128]{2,1,0:T(8,128)}) fusion(f32[8,256,32]{2,1,0:T(8,128)S(1)} %get-tuple-element.173, f32[8,256,32]{2,1,0:T(8,128)S(1)} %get-tuple-element.172, f32[8,256,32]{2,1,0:T(8,128)S(1)} %get-tuple-element.171), kind=kLoop, calls=%fused_computation.2 | loop fusion | flops 1572864 | bytes 2883584 | tf_op jit(solution)/shard_map/concatenate | solution.py:700
  30.3 2.8 %collective-permute-start.4 = (bf16[208,2304]{1,0:T(8,128)(2,1)S(1)}, bf16[208,2304]{1,0:T(8,128)(2,1)S(1)}, u32[]{:S(2)}, u32[]{:S(2)}) collective-permute-start(bf16[208,2304]{1,0:T(8,128)(2,1)S(1)} %collective-permute-done.1.refs_9_.refs_6_), channel_id=1, source_target_pairs={{0,2},{2,0},{4,6},{6,4},{8,10},{10,8},{12,14},{14,12},{16,18},{18,... | collective-permute-start | bytes 2875400 | tf_op jit(solution)/shard_map/ppermute | solution.py:557
  36.1 26.5 %shard_map.137 = (bf16[8,128,768]{2,1,0:T(8,128)(2,1)}, bf16[8,256,768]{2,1,0:T(8,128)(2,1)}, bf16[8,256,768]{2,1,0:T(8,128)(2,1)}, bf16[8,256,768]{2,1,0:T(8,12...) custom-call(s32[5]{0:T(128)} %stack.19.refs_0_, bf16[8,64,768]{2,1,0:T(8,128)(2,1)} %copy-done.24, ...), custom_call_target="tpu_custom_call" | custom-call | flops 1 | bytes 1 | tf_op jit(solution)/shard_map/pallas_call | solution.py:536
  63.1 3.4 %collective-permute-done.5.refs_10_ = bf16[352,2304]{1,0:T(8,128)(2,1)S(1)} collective-permute-done((bf16[352,2304]{1,0:T(8,128)(2,1)S(1)}, bf16[352,2304]{1,0:T(8,128)(2,1)S(1)}, u32[]{:S(2)}, u32[]{:S(2)}) %collective-permute-start.5) | collective-permute-done | bytes 1622048 | tf_op jit(solution)/shard_map/ppermute | solution.py:557
  67.6 27.3 %shard_map.138 = (bf16[1024,768]{1,0:T(8,128)(2,1)}, f32[1024,768]{1,0:T(8,128)}, bf16[1024,768]{1,0:T(8,128)(2,1)}, bf16[8,80,768]{2,1,0:T(8,128)(2,1)}, bf16[8...) custom-call(s32[5]{0:T(128)} %stack.19.refs_0_, ...), custom_call_target="tpu_custom_call" | custom-call | flops 1 | bytes 1 | tf_op jit(solution)/shard_map/pallas_call | solution.py:536
  94.9 2.1 collective-permute-start.6
  98.3 14.7 %shard_map.139 = (bf16[2,1088,768]{2,1,0:T(8,128)(2,1)}, bf16[2,1088,768]{2,1,0:T(8,128)(2,1)}) custom-call(s32[5]{0:T(128)} %stack.19.refs_0_, bf16[1024,768]{1,0:T(8,128)(2,1)} %get-tuple-element.105.refs_1_, bf16[1024,2304]{1,0:T(8,128)(2,1)} %get-tuple-element.106.refs_2_, bf16[1024,1152]{1,0:T(8,128)(2,1)} %get-tuple-element.107.refs_3_, ...), custom_call_target="tpu_custom_call" | custom-call | flops 1 | bytes 1 | tf_op jit(solution)/shard_map/pallas_call | solution.py:536
  113.0 8.2 %collective-permute-start.8 = (bf16[2,1088,768]{2,1,0:T(8,128)(2,1)}, bf16[2,1088,768]{2,1,0:T(8,128)(2,1)S(1)}, u32[]{:S(2)}, u32[]{:S(2)}) collective-permute-start(bf16[2,1088,768]{2,1,0:T(8,128)(2,1)} %get-tuple-element.117), channel_id=1, source_target_pairs={{0,2},{2,0},{4,6},{6,4},{8,10},{10,8},{12,14},{14,12},{16,18},{18,... | collective-permute-start | bytes 10027016 | tf_op jit(solution)/shard_map/ppermute | solution.py:563
  121.2 11.2 %shard_map.140 = (bf16[8,128,2560]{2,1,0:T(8,128)(2,1)}, f32[8,128]{1,0:T(8,128)}) custom-call(bf16[8,256,768]{2,1,0:T(8,128)(2,1)} %get-tuple-element.99.refs_0_, bf16[8,256,768]{2,1,0:T(8,128)(2,1)} %get-tuple-element.100.refs_1_, bf16[8,256,768]{2,1,0:T(8,128)(2,1)} %get-tuple-element.101.refs_2_, bf16[8,128,768]{2,1,0:T(8,128)(2,1)} %bitcast.71, ...), custom_call_target="tpu_custom_call" | custom-call | flops 1 | bytes 1 | tf_op jit(solution)/shard_map/pallas_call | solution.py:536
  133.1 2.1 shard_map.141
  138.0 3.5 %collective-permute-start.10 = (bf16[2,544,384]{2,1,0:T(8,128)(2,1)S(1)}, bf16[2,544,384]{2,1,0:T(8,128)(2,1)}, u32[]{:S(2)}, u32[]{:S(2)}) collective-permute-start(bf16[2,544,384]{2,1,0:T(8,128)(2,1)S(1)} %get-tuple-element.120.refs_15_), channel_id=1, source_target_pairs={{0,4},{2,6},{4,0},{6,2},{8,12},{10,14},{12,8},{14,10},{16,20},{18,... | collective-permute-start | bytes 2506760 | tf_op jit(solution)/shard_map/ppermute | solution.py:563
  141.6 11.2 %shard_map.142 = (bf16[8,128,2560]{2,1,0:T(8,128)(2,1)}, f32[8,128]{1,0:T(8,128)}) custom-call(bf16[8,256,768]{2,1,0:T(8,128)(2,1)} %get-tuple-element.99.refs_0_, bf16[8,256,768]{2,1,0:T(8,128)(2,1)} %get-tuple-element.100.refs_1_, bf16[8,256,768]{2,1,0:T(8,128)(2,1)} %get-tuple-element.101.refs_2_, ...), custom_call_target="tpu_custom_call", output_to_operand_aliasing={{0}: (13, {})} | custom-call | flops 1 | bytes 1 | tf_op jit(solution)/shard_map/pallas_call | solution.py:536
  152.9 8.2 %shard_map.143 = (bf16[2,192,2560]{2,1,0:T(8,128)(2,1)S(1)}, bf16[2,192,2560]{2,1,0:T(8,128)(2,1)S(1)}) custom-call(s32[5]{0:T(128)S(1)} %copy-done.16, bf16[1024,768]{1,0:T(8,128)(2,1)S(1)} %bitcast.56, bf16[1024,2560]{1,0:T(8,128)(2,1)} %bitcast.34, bf16[2,768]{1,0:T(2,128)(2,1)S(1)} %copy-done.17, f32[8,768]{1,0:T(8,128)S(1)} %copy-done.18, ...), custom_call_target="tpu_custom_call" | custom-call | flops 1 | bytes 1 | tf_op jit(solution)/shard_map/pallas_call | solution.py:536
  168.8 6.9 %collective-permute-done.11 = bf16[544,384]{1,0:T(8,128)(2,1)S(1)} collective-permute-done((bf16[544,384]{1,0:T(8,128)(2,1)S(1)}, bf16[544,384]{1,0:T(8,128)(2,1)S(1)}, u32[]{:S(2)}, u32[]{:S(2)}) %collective-permute-start.11) | collective-permute-done | bytes 417824 | tf_op jit(solution)/shard_map/ppermute | solution.py:563
  176.6 2.9 %collective-permute-start.16 = (bf16[136,768]{1,0:T(8,128)(2,1)S(1)}, bf16[136,768]{1,0:T(8,128)(2,1)S(1)}, u32[]{:S(2)}, u32[]{:S(2)}) collective-permute-start(bf16[136,768]{1,0:T(8,128)(2,1)S(1)} %get-tuple-element.137.refs_8_), channel_id=1, source_target_pairs={{0,8},{2,10},{4,12},{6,14},{8,0},{10,2},{12,4},{14,6},{16,24},{18,... | collective-permute-start | bytes 626696 | tf_op jit(solution)/shard_map/ppermute | solution.py:563
  179.5 2.6 collective-permute-start.17
  182.1 6.9 %shard_map.147.refs_5_ = bf16[1024,768]{1,0:T(8,128)(2,1)} custom-call(s32[5]{0:T(128)S(1)} %copy-done.16, bf16[1024,2560]{1,0:T(8,128)(2,1)S(1)} %bitcast.37, bf16[1024,768]{1,0:T(8,128)(2,1)S(1)} %bitcast.39, f32[1024,768]{1,0:T(8,128)S(1)} %copy-done.8, bf16[2,768]{1,0:T(2,128)(2,1)S(1)} %copy-done.17, bf16[384,2304]{1,0:T(8,128)(2,1)S(1)} %copy-done, ...), custom_call_target="tpu_custom_call" | custom-call | flops 1 | bytes 1 | tf_op jit(solution)/shard_map/pallas_call | solution.py:536
  191.4 5.5 %collective-permute-done.17 = bf16[136,768]{1,0:T(8,128)(2,1)S(1)} collective-permute-done((bf16[136,768]{1,0:T(8,128)(2,1)S(1)}, bf16[136,768]{1,0:T(8,128)(2,1)S(1)}, u32[]{:S(2)}, u32[]{:S(2)}) %collective-permute-start.17) | collective-permute-done | bytes 208928 | tf_op jit(solution)/shard_map/ppermute | solution.py:563
  201.5 2.6 collective-permute-start.22
  211.3 14.7 %collective-permute-done.22.refs_3_ = bf16[136,768]{1,0:T(8,128)(2,1)S(1)} collective-permute-done((bf16[136,768]{1,0:T(8,128)(2,1)S(1)}, bf16[136,768]{1,0:T(8,128)(2,1)S(1)}, u32[]{:S(2)}, u32[]{:S(2)}) %collective-permute-start.22) | collective-permute-done | bytes 208928 | tf_op jit(solution)/shard_map/ppermute | solution.py:563
  229.7 2.2 collective-permute-start.29
  234.2 3.7 %collective-permute-done.29.refs_4_ = bf16[24,2560]{1,0:T(8,128)(2,1)S(1)} collective-permute-done((bf16[24,2560]{1,0:T(8,128)(2,1)S(1)}, bf16[24,2560]{1,0:T(8,128)(2,1)S(1)}, u32[]{:S(2)}, u32[]{:S(2)}) %collective-permute-start.29) | collective-permute-done | bytes 122912 | tf_op jit(solution)/shard_map/ppermute | solution.py:563
  237.9 4.1 %collective-permute-done.28.refs_3_ = bf16[24,2560]{1,0:T(8,128)(2,1)S(1)} collective-permute-done((bf16[24,2560]{1,0:T(8,128)(2,1)S(1)}, bf16[24,2560]{1,0:T(8,128)(2,1)S(1)}, u32[]{:S(2)}, u32[]{:S(2)}) %collective-permute-start.28) | collective-permute-done | bytes 122912 | tf_op jit(solution)/shard_map/ppermute | solution.py:563
  242.6 2.6 collective-permute-done.31.refs_2_
  249.8 3.6 %shard_map.155 = (f32[384,2304]{1,0:T(8,128)}, f32[576,768]{1,0:T(8,128)}, f32[384,768]{1,0:T(8,128)}) custom-call(s32[5]{0:T(128)S(1)} %copy-done.16, bf16[1088,768]{1,0:T(8,128)(2,1)S(1)} %bitcast.49, bf16[1088,768]{1,0:T(8,128)(2,1)S(1)} %collective-permute-done.32.refs_2_, bf16[96,2560]{1,0:T(8,128)(2,1)S(1)} %bitcast.43), custom_call_target="tpu_custom_call" | custom-call | flops 1 | bytes 1 | tf_op jit(solution)/shard_map/pallas_call | solution.py:536
  253.4 6.5 %collective-permute-done.30.refs_2_ = bf16[96,2560]{1,0:T(8,128)(2,1)S(1)} collective-permute-done((bf16[96,2560]{1,0:T(8,128)(2,1)S(1)}, bf16[96,2560]{1,0:T(8,128)(2,1)S(1)}, u32[]{:S(2)}, u32[]{:S(2)}) %collective-permute-start.30) | collective-permute-done | bytes 491552 | tf_op jit(solution)/shard_map/ppermute | solution.py:563
  262.0 2.6 collective-permute-done.33.refs_2_
  264.6 2.6 shard_map.157
  (158 shorter events, 58.0 us)
Async XLA Ops:
  3.8 25.6 %collective-permute-start.1 = (bf16[208,2304]{1,0:T(8,128)(2,1)}, bf16[208,2304]{1,0:T(8,128)(2,1)S(1)}, u32[]{:S(2)}, u32[]{:S(2)}) collective-permute-start(bf16[208,2304]{1,0:T(8,128)(2,1)} %shard_map.135.refs_5_), channel_id=1, source_target_pairs={{0,1},{1,0},{2,3},{3,2},{4,5},{5,4},{6,7},{7,6},{8,9},{9,8},{10,11... | collective-permute-start | bytes 2875400 | tf_op jit(solution)/shard_map/ppermute | solution.py:562
  11.0 18.4 %collective-permute-start.2 = (bf16[8,64,768]{2,1,0:T(8,128)(2,1)}, bf16[8,64,768]{2,1,0:T(8,128)(2,1)S(1)}, u32[]{:S(2)}, u32[]{:S(2)}) collective-permute-start(bf16[8,64,768]{2,1,0:T(8,128)(2,1)} %get-tuple-element.86), channel_id=1, source_target_pairs={{0,2},{2,4},{4,6},{6,8},{8,10},{10,12},{12,14},{14,16},{16,18},{18... | collective-permute-start | bytes 2359304 | tf_op jit(solution)/shard_map/ppermute | solution.py:29
  12.5 16.9 %collective-permute-start.3 = (bf16[8,64,768]{2,1,0:T(8,128)(2,1)}, bf16[8,64,768]{2,1,0:T(8,128)(2,1)}, u32[]{:S(2)}, u32[]{:S(2)}) collective-permute-start(bf16[8,64,768]{2,1,0:T(8,128)(2,1)} %get-tuple-element.87), channel_id=1, source_target_pairs={{2,0},{4,2},{6,4},{8,6},{10,8},{12,10},{14,12},{16,14},{18,16},{20... | collective-permute-start | bytes 2359304 | tf_op jit(solution)/shard_map/ppermute | solution.py:29
  13.8 49.2 %collective-permute-start = (bf16[352,2304]{1,0:T(8,128)(2,1)}, bf16[352,2304]{1,0:T(8,128)(2,1)S(1)}, u32[]{:S(2)}, u32[]{:S(2)}) collective-permute-start(bf16[352,2304]{1,0:T(8,128)(2,1)} %get-tuple-element.85), channel_id=1, source_target_pairs={{0,1},{1,0},{2,3},{3,2},{4,5},{5,4},{6,7},{7,6},{8,9},{9,8},{10,11... | collective-permute-start | bytes 4866056 | tf_op jit(solution)/shard_map/ppermute | solution.py:562
  30.3 4.9 %collective-permute-start.4 = (bf16[208,2304]{1,0:T(8,128)(2,1)S(1)}, bf16[208,2304]{1,0:T(8,128)(2,1)S(1)}, u32[]{:S(2)}, u32[]{:S(2)}) collective-permute-start(bf16[208,2304]{1,0:T(8,128)(2,1)S(1)} %collective-permute-done.1.refs_9_.refs_6_), channel_id=1, source_target_pairs={{0,2},{2,0},{4,6},{6,4},{8,10},{10,8},{12,14},{14,12},{16,18},{18,... | collective-permute-start | bytes 2875400 | tf_op jit(solution)/shard_map/ppermute | solution.py:557
  94.9 18.1 %collective-permute-start.6 = (bf16[8,80,768]{2,1,0:T(8,128)(2,1)}, bf16[8,80,768]{2,1,0:T(8,128)(2,1)S(1)}, u32[]{:S(2)}, u32[]{:S(2)}) collective-permute-start(bf16[8,80,768]{2,1,0:T(8,128)(2,1)} %get-tuple-element.103), channel_id=1, source_target_pairs={{0,2},{2,4},{4,6},{6,8},{8,10},{10,12},{12,14},{14,16},{16,18},{18... | collective-permute-start | bytes 2949128 | tf_op jit(solution)/shard_map/ppermute | solution.py:29
  97.0 16.0 %collective-permute-start.7 = (bf16[8,80,768]{2,1,0:T(8,128)(2,1)}, bf16[8,80,768]{2,1,0:T(8,128)(2,1)S(1)}, u32[]{:S(2)}, u32[]{:S(2)}) collective-permute-start(bf16[8,80,768]{2,1,0:T(8,128)(2,1)} %get-tuple-element.104), channel_id=1, source_target_pairs={{2,0},{4,2},{6,4},{8,6},{10,8},{12,10},{14,12},{16,14},{18,16},{20... | collective-permute-start | bytes 2949128 | tf_op jit(solution)/shard_map/ppermute | solution.py:29
  113.0 19.3 %collective-permute-start.8 = (bf16[2,1088,768]{2,1,0:T(8,128)(2,1)}, bf16[2,1088,768]{2,1,0:T(8,128)(2,1)S(1)}, u32[]{:S(2)}, u32[]{:S(2)}) collective-permute-start(bf16[2,1088,768]{2,1,0:T(8,128)(2,1)} %get-tuple-element.117), channel_id=1, source_target_pairs={{0,2},{2,0},{4,6},{6,4},{8,10},{10,8},{12,14},{14,12},{16,18},{18,... | collective-permute-start | bytes 10027016 | tf_op jit(solution)/shard_map/ppermute | solution.py:563
  137.1 24.0 %collective-permute-start.9 = (bf16[2,544,384]{2,1,0:T(8,128)(2,1)}, bf16[2,544,384]{2,1,0:T(8,128)(2,1)}, u32[]{:S(2)}, u32[]{:S(2)}) collective-permute-start(bf16[2,544,384]{2,1,0:T(8,128)(2,1)} %get-tuple-element.119.refs_14_), channel_id=1, source_target_pairs={{0,1},{1,0},{2,3},{3,2},{4,5},{5,4},{6,7},{7,6},{8,9},{9,8},{10,11... | collective-permute-start | bytes 2506760 | tf_op jit(solution)/shard_map/ppermute | solution.py:562
  138.0 23.1 %collective-permute-start.10 = (bf16[2,544,384]{2,1,0:T(8,128)(2,1)S(1)}, bf16[2,544,384]{2,1,0:T(8,128)(2,1)}, u32[]{:S(2)}, u32[]{:S(2)}) collective-permute-start(bf16[2,544,384]{2,1,0:T(8,128)(2,1)S(1)} %get-tuple-element.120.refs_15_), channel_id=1, source_target_pairs={{0,4},{2,6},{4,0},{6,2},{8,12},{10,14},{12,8},{14,10},{16,20},{18,... | collective-permute-start | bytes 2506760 | tf_op jit(solution)/shard_map/ppermute | solution.py:563
  161.1 4.0 %collective-permute-start.13 = (bf16[2,192,2560]{2,1,0:T(8,128)(2,1)S(1)}, bf16[2,192,2560]{2,1,0:T(8,128)(2,1)S(1)}, u32[]{:S(2)}, u32[]{:S(2)}) collective-permute-start(bf16[2,192,2560]{2,1,0:T(8,128)(2,1)S(1)} %get-tuple-element.134), channel_id=1, source_target_pairs={{0,2},{2,0},{4,6},{6,4},{8,10},{10,8},{12,14},{14,12},{16,18},{18,... | collective-permute-start | bytes 5898248 | tf_op jit(solution)/shard_map/ppermute | solution.py:563
  163.2 12.5 %collective-permute-start.11 = (bf16[544,384]{1,0:T(8,128)(2,1)S(1)}, bf16[544,384]{1,0:T(8,128)(2,1)S(1)}, u32[]{:S(2)}, u32[]{:S(2)}) collective-permute-start(bf16[544,384]{1,0:T(8,128)(2,1)S(1)} %get-tuple-element.132.refs_3_), channel_id=1, source_target_pairs={{0,4},{2,6},{4,0},{6,2},{8,12},{10,14},{12,8},{14,10},{16,20},{18,... | collective-permute-start | bytes 1253384 | tf_op jit(solution)/shard_map/ppermute | solution.py:563
  163.3 12.5 %collective-permute-start.12 = (bf16[544,384]{1,0:T(8,128)(2,1)S(1)}, bf16[544,384]{1,0:T(8,128)(2,1)S(1)}, u32[]{:S(2)}, u32[]{:S(2)}) collective-permute-start(bf16[544,384]{1,0:T(8,128)(2,1)S(1)} %get-tuple-element.133.refs_4_), channel_id=1, source_target_pairs={{0,1},{1,0},{2,3},{3,2},{4,5},{5,4},{6,7},{7,6},{8,9},{9,8},{10,11... | collective-permute-start | bytes 1253384 | tf_op jit(solution)/shard_map/ppermute | solution.py:562
  166.6 22.4 %collective-permute-start.14 = (bf16[2,96,1280]{2,1,0:T(8,128)(2,1)S(1)}, bf16[2,96,1280]{2,1,0:T(8,128)(2,1)S(1)}, u32[]{:S(2)}, u32[]{:S(2)}) collective-permute-start(bf16[2,96,1280]{2,1,0:T(8,128)(2,1)S(1)} %get-tuple-element.135.refs_4_), channel_id=1, source_target_pairs={{0,1},{1,0},{2,3},{3,2},{4,5},{5,4},{6,7},{7,6},{8,9},{9,8},{10,11... | collective-permute-start | bytes 1474568 | tf_op jit(solution)/shard_map/ppermute | solution.py:562
  167.7 21.2 %collective-permute-start.15 = (bf16[2,96,1280]{2,1,0:T(8,128)(2,1)S(1)}, bf16[2,96,1280]{2,1,0:T(8,128)(2,1)S(1)}, u32[]{:S(2)}, u32[]{:S(2)}) collective-permute-start(bf16[2,96,1280]{2,1,0:T(8,128)(2,1)S(1)} %get-tuple-element.136.refs_5_), channel_id=1, source_target_pairs={{0,4},{2,6},{4,0},{6,2},{8,12},{10,14},{12,8},{14,10},{16,20},{18,... | collective-permute-start | bytes 1474568 | tf_op jit(solution)/shard_map/ppermute | solution.py:563
  176.6 14.8 %collective-permute-start.16 = (bf16[136,768]{1,0:T(8,128)(2,1)S(1)}, bf16[136,768]{1,0:T(8,128)(2,1)S(1)}, u32[]{:S(2)}, u32[]{:S(2)}) collective-permute-start(bf16[136,768]{1,0:T(8,128)(2,1)S(1)} %get-tuple-element.137.refs_8_), channel_id=1, source_target_pairs={{0,8},{2,10},{4,12},{6,14},{8,0},{10,2},{12,4},{14,6},{16,24},{18,... | collective-permute-start | bytes 626696 | tf_op jit(solution)/shard_map/ppermute | solution.py:563
  179.5 17.4 %collective-permute-start.17 = (bf16[136,768]{1,0:T(8,128)(2,1)S(1)}, bf16[136,768]{1,0:T(8,128)(2,1)S(1)}, u32[]{:S(2)}, u32[]{:S(2)}) collective-permute-start(bf16[136,768]{1,0:T(8,128)(2,1)S(1)} %get-tuple-element.138.refs_9_), channel_id=1, source_target_pairs={{0,16},{2,18},{4,20},{6,22},{8,24},{10,26},{12,28},{14,30},{16,0},... | collective-permute-start | bytes 626696 | tf_op jit(solution)/shard_map/ppermute | solution.py:563
  182.1 16.8 %collective-permute-start.20 = (bf16[136,768]{1,0:T(8,128)(2,1)S(1)}, bf16[136,768]{1,0:T(8,128)(2,1)S(1)}, u32[]{:S(2)}, u32[]{:S(2)}) collective-permute-start(bf16[136,768]{1,0:T(8,128)(2,1)S(1)} %get-tuple-element.139.refs_10_), channel_id=1, source_target_pairs={{0,24},{2,26},{4,28},{6,30},{8,16},{10,18},{12,20},{14,22},{16,8},... | collective-permute-start | bytes 626696 | tf_op jit(solution)/shard_map/ppermute | solution.py:563
  196.9 7.3 %collective-permute-start.18 = (bf16[96,1280]{1,0:T(8,128)(2,1)S(1)}, bf16[96,1280]{1,0:T(8,128)(2,1)S(1)}, u32[]{:S(2)}, u32[]{:S(2)}) collective-permute-start(bf16[96,1280]{1,0:T(8,128)(2,1)S(1)} %get-tuple-element.145.refs_5_), channel_id=1, source_target_pairs={{0,4},{2,6},{4,0},{6,2},{8,12},{10,14},{12,8},{14,10},{16,20},{18,... | collective-permute-start | bytes 737288 | tf_op jit(solution)/shard_map/ppermute | solution.py:563
  198.3 6.2 %collective-permute-start.19 = (bf16[96,1280]{1,0:T(8,128)(2,1)S(1)}, bf16[96,1280]{1,0:T(8,128)(2,1)S(1)}, u32[]{:S(2)}, u32[]{:S(2)}) collective-permute-start(bf16[96,1280]{1,0:T(8,128)(2,1)S(1)} %get-tuple-element.146.refs_6_), channel_id=1, source_target_pairs={{0,1},{1,0},{2,3},{3,2},{4,5},{5,4},{6,7},{7,6},{8,9},{9,8},{10,11... | collective-permute-start | bytes 737288 | tf_op jit(solution)/shard_map/ppermute | solution.py:562
  199.5 9.8 %collective-permute-start.23 = (bf16[136,768]{1,0:T(8,128)(2,1)S(1)}, bf16[136,768]{1,0:T(8,128)(2,1)S(1)}, u32[]{:S(2)}, u32[]{:S(2)}) collective-permute-start(bf16[136,768]{1,0:T(8,128)(2,1)S(1)} %shard_map.149.refs_4_.refs_5_.refs_6_.refs_1_), channel_id=1, source_target_pairs={{0,24},{2,26},{4,28},{6,30},{8,16},{10,18},{12,20},{14,22},{16,8},... | collective-permute-start | bytes 626696 | tf_op jit(solution)/shard_map/ppermute | solution.py:563
  201.5 24.5 %collective-permute-start.22 = (bf16[136,768]{1,0:T(8,128)(2,1)S(1)}, bf16[136,768]{1,0:T(8,128)(2,1)S(1)}, u32[]{:S(2)}, u32[]{:S(2)}) collective-permute-start(bf16[136,768]{1,0:T(8,128)(2,1)S(1)} %shard_map.149.refs_4_.refs_5_.refs_6_.refs_1_), channel_id=1, source_target_pairs={{0,16},{2,18},{4,20},{6,22},{8,24},{10,26},{12,28},{14,30},{16,0},... | collective-permute-start | bytes 626696 | tf_op jit(solution)/shard_map/ppermute | solution.py:563
  204.1 21.9 %collective-permute-start.21 = (bf16[136,768]{1,0:T(8,128)(2,1)S(1)}, bf16[136,768]{1,0:T(8,128)(2,1)S(1)}, u32[]{:S(2)}, u32[]{:S(2)}) collective-permute-start(bf16[136,768]{1,0:T(8,128)(2,1)S(1)} %shard_map.149.refs_4_.refs_5_.refs_6_.refs_1_), channel_id=1, source_target_pairs={{0,8},{2,10},{4,12},{6,14},{8,0},{10,2},{12,4},{14,6},{16,24},{18,... | collective-permute-start | bytes 626696 | tf_op jit(solution)/shard_map/ppermute | solution.py:563
  205.2 21.7 %collective-permute-start.24 = (bf16[24,2560]{1,0:T(8,128)(2,1)S(1)}, bf16[24,2560]{1,0:T(8,128)(2,1)S(1)}, u32[]{:S(2)}, u32[]{:S(2)}) collective-permute-start(bf16[24,2560]{1,0:T(8,128)(2,1)S(1)} %get-tuple-element.151.refs_5_), channel_id=1, source_target_pairs={{0,8},{2,10},{4,12},{6,14},{8,0},{10,2},{12,4},{14,6},{16,24},{18,... | collective-permute-start | bytes 368648 | tf_op jit(solution)/shard_map/ppermute | solution.py:563
  206.9 20.8 %collective-permute-start.25 = (bf16[24,2560]{1,0:T(8,128)(2,1)S(1)}, bf16[24,2560]{1,0:T(8,128)(2,1)S(1)}, u32[]{:S(2)}, u32[]{:S(2)}) collective-permute-start(bf16[24,2560]{1,0:T(8,128)(2,1)S(1)} %get-tuple-element.152.refs_6_), channel_id=1, source_target_pairs={{0,16},{2,18},{4,20},{6,22},{8,24},{10,26},{12,28},{14,30},{16,0},... | collective-permute-start | bytes 368648 | tf_op jit(solution)/shard_map/ppermute | solution.py:563
  209.3 18.4 %collective-permute-start.26 = (bf16[24,2560]{1,0:T(8,128)(2,1)S(1)}, bf16[24,2560]{1,0:T(8,128)(2,1)S(1)}, u32[]{:S(2)}, u32[]{:S(2)}) collective-permute-start(bf16[24,2560]{1,0:T(8,128)(2,1)S(1)} %get-tuple-element.153.refs_7_), channel_id=1, source_target_pairs={{0,24},{2,26},{4,28},{6,30},{8,16},{10,18},{12,20},{14,22},{16,8},... | collective-permute-start | bytes 368648 | tf_op jit(solution)/shard_map/ppermute | solution.py:563
  227.7 17.5 %collective-permute-start.31 = (bf16[544,768]{1,0:T(8,128)(2,1)S(1)}, bf16[544,768]{1,0:T(8,128)(2,1)S(1)}, u32[]{:S(2)}, u32[]{:S(2)}) collective-permute-start(bf16[544,768]{1,0:T(8,128)(2,1)S(1)} %bitcast.45), channel_id=1, source_target_pairs={{0,4},{2,6},{4,0},{6,2},{8,12},{10,14},{12,8},{14,10},{16,20},{18,... | collective-permute-start | bytes 2506760 | tf_op jit(solution)/shard_map/ppermute | solution.py:563
  229.7 8.1 %collective-permute-start.29 = (bf16[24,2560]{1,0:T(8,128)(2,1)S(1)}, bf16[24,2560]{1,0:T(8,128)(2,1)S(1)}, u32[]{:S(2)}, u32[]{:S(2)}) collective-permute-start(bf16[24,2560]{1,0:T(8,128)(2,1)S(1)} %shard_map.152.refs_1_.refs_5_.refs_6_.refs_7_), channel_id=1, source_target_pairs={{0,24},{2,26},{4,28},{6,30},{8,16},{10,18},{12,20},{14,22},{16,8},... | collective-permute-start | bytes 368648 | tf_op jit(solution)/shard_map/ppermute | solution.py:563
  231.9 10.1 %collective-permute-start.28 = (bf16[24,2560]{1,0:T(8,128)(2,1)S(1)}, bf16[24,2560]{1,0:T(8,128)(2,1)S(1)}, u32[]{:S(2)}, u32[]{:S(2)}) collective-permute-start(bf16[24,2560]{1,0:T(8,128)(2,1)S(1)} %shard_map.152.refs_1_.refs_5_.refs_6_.refs_7_), channel_id=1, source_target_pairs={{0,16},{2,18},{4,20},{6,22},{8,24},{10,26},{12,28},{14,30},{16,0},... | collective-permute-start | bytes 368648 | tf_op jit(solution)/shard_map/ppermute | solution.py:563
  233.1 8.9 %collective-permute-start.27 = (bf16[24,2560]{1,0:T(8,128)(2,1)S(1)}, bf16[24,2560]{1,0:T(8,128)(2,1)S(1)}, u32[]{:S(2)}, u32[]{:S(2)}) collective-permute-start(bf16[24,2560]{1,0:T(8,128)(2,1)S(1)} %shard_map.152.refs_1_.refs_5_.refs_6_.refs_7_), channel_id=1, source_target_pairs={{0,8},{2,10},{4,12},{6,14},{8,0},{10,2},{12,4},{14,6},{16,24},{18,... | collective-permute-start | bytes 368648 | tf_op jit(solution)/shard_map/ppermute | solution.py:563
  246.1 3.6 %collective-permute-start.32 = (bf16[1088,768]{1,0:T(8,128)(2,1)S(1)}, bf16[1088,768]{1,0:T(8,128)(2,1)S(1)}, u32[]{:S(2)}, u32[]{:S(2)}) collective-permute-start(bf16[1088,768]{1,0:T(8,128)(2,1)S(1)} %bitcast.48), channel_id=1, source_target_pairs={{0,2},{2,0},{4,6},{6,4},{8,10},{10,8},{12,14},{14,12},{16,18},{18,... | collective-permute-start | bytes 5013512 | tf_op jit(solution)/shard_map/ppermute | solution.py:563
  246.2 13.6 %collective-permute-start.30 = (bf16[96,2560]{1,0:T(8,128)(2,1)S(1)}, bf16[96,2560]{1,0:T(8,128)(2,1)S(1)}, u32[]{:S(2)}, u32[]{:S(2)}) collective-permute-start(bf16[96,2560]{1,0:T(8,128)(2,1)S(1)} %bitcast.42), channel_id=1, source_target_pairs={{0,4},{2,6},{4,0},{6,2},{8,12},{10,14},{12,8},{14,10},{16,20},{18,... | collective-permute-start | bytes 1474568 | tf_op jit(solution)/shard_map/ppermute | solution.py:563
  (38 other events, 281.9 us)
